TPU v7x, 32 devices: a whole 2x2x4 slice. The times are simulated.
32 devices in a mesh: grp: 4 (over z), dat: 4 (over y, x), mdl: 2 (over core).
Axes of the slice: x: 2, y: 2, z: 4, core: 2. Of those that a mesh axis runs over, the one named last changes fastest.
Arguments:
- token_ids: int32 [64, 512], P(('grp', 'dat')), may hold values from 0 to 32127
- item_lengths: int32 [64], P(('grp', 'dat')), may hold values from 128 to 512
- prefix_lengths: int32 [64], P(('grp', 'dat')), may hold values from 1 to 64
- group_live: int32 [4], replicated, may hold values from 2 to 16, as said below
- partner: int32 [64], P(('grp', 'dat')), may hold values from 0 to 15, as said below
- embedding: float32 [768, 32128], P('dat'), may hold values from -6 to 6
- qkv_weight: float32 [768, 3, 768], P('dat', None, 'mdl'), may hold values from -0.21875 to 0.21875
- out_weight: float32 [768, 768], P('mdl', 'dat'), may hold values from -1.25 to 1.25
- up_weight: float32 [768, 3072], P('dat', 'mdl'), may hold values from -0.21875 to 0.21875
- down_weight: float32 [768, 3072], P('dat', 'mdl'), may hold values from -0.109375 to 0.109375
- bias_table: float32 [32, 12], P(None, 'mdl'), may hold values from -6 to 6
- norm_gains: float32 [3, 768], replicated, may hold values from 0.5 to 1.5
- embedding_first: float32 [768, 32128], P('dat')
- embedding_second: float32 [768, 32128], P('dat'), as said below
- qkv_first: float32 [768, 3, 768], P('dat', None, 'mdl')
- qkv_second: float32 [768, 3, 768], P('dat', None, 'mdl'), as said below
- out_first: float32 [768, 768], P('mdl', 'dat')
- out_second: float32 [768, 768], P('mdl', 'dat'), as said below
- up_first: float32 [768, 3072], P('dat', 'mdl')
- up_second: float32 [768, 3072], P('dat', 'mdl'), as said below
- down_first: float32 [768, 3072], P('dat', 'mdl')
- down_second: float32 [768, 3072], P('dat', 'mdl'), as said below
- bias_first: float32 [32, 12], P(None, 'mdl')
- bias_second: float32 [32, 12], P(None, 'mdl'), as said below
- gains_first: float32 [3, 768], replicated
- gains_second: float32 [3, 768], replicated, as said below
Outputs:
- loss_pair: float32 [2], replicated
- matrix_norms: float32 [9, 2], replicated
- embedding_momentum: float32 [768, 32128], P('dat')
- embedding_variance: float32 [768, 32128], P('dat')
- embedding_updated: float32 [768, 32128], P('dat')
- qkv_momentum: float32 [768, 3, 768], P('dat', None, 'mdl')
- qkv_variance: float32 [768, 3, 768], P('dat', None, 'mdl')
- qkv_updated: float32 [768, 3, 768], P('dat', None, 'mdl')
- out_momentum: float32 [768, 768], P('mdl', 'dat')
- out_variance: float32 [768, 768], P('mdl', 'dat')
- out_updated: float32 [768, 768], P('mdl', 'dat')
- up_momentum: float32 [768, 3072], P('dat', 'mdl')
- up_variance: float32 [768, 3072], P('dat', 'mdl')
- up_updated: float32 [768, 3072], P('dat', 'mdl')
- down_momentum: float32 [768, 3072], P('dat', 'mdl')
- down_variance: float32 [768, 3072], P('dat', 'mdl')
- down_updated: float32 [768, 3072], P('dat', 'mdl')
- bias_momentum: float32 [32, 12], P(None, 'mdl')
- bias_variance: float32 [32, 12], P(None, 'mdl')
- bias_updated: float32 [32, 12], P(None, 'mdl')
- gains_momentum: float32 [3, 768], replicated
- gains_variance: float32 [3, 768], replicated
- gains_updated: float32 [3, 768], replicated
Inputs may be any that keep to these rules, and one draw needn't show every extreme that they name: `group_live`: Even; the items of a group at slots below it are live, the rest are dead; the last group is full. `partner`: for a live item, the slot of another live item of the same group whose partner is this item; a dead item names its own slot. `embedding_second`: positive. `qkv_second`: positive. `out_second`: positive. `up_second`: positive. `down_second`: positive. `bias_second`: positive. `gains_second`: positive.
All inputs are finite; a program needn't handle non-finite values.
Results may differ from a plain program's by a relative error of at most 0.012.
The roundings to bfloat16 on the way count: a program that leaves them out, or rounds other values in their place, can miss the bound.
Values may be sent and summed in bfloat16 or wider, within the bound.
A program may use at most 512 MiB of HBM per device.

v0:
```python
import jax
import jax.numpy as jnp
from jax import lax
from jax.sharding import PartitionSpec as P

HEADS = 12
HEAD = 64
BUCKETS = 32
STEP = 10


SOFTMAX_WARMTH = 0.01
NORM_EPS = 1e-06
BUCKET_EDGES = (12, 16, 23, 32, 46, 64, 91)
BETA_ONE = 0.9
BETA_TWO = 0.999
ADAM_EPS = 1e-06
WEIGHT_DECAY = 0.01
LEARN_RATE = 0.5
MASK_FILL = -1000000000.0
MAX_PRECISION = lax.Precision.HIGHEST


def bucket_table(extent):
    positions = jnp.arange(extent, dtype=jnp.int32)
    relative = positions[None, :] - positions[:, None]
    distance = jnp.abs(relative)
    far_bucket = 8 + sum(((distance >= threshold).astype(jnp.int32) for threshold in BUCKET_EDGES))
    return jnp.where(distance < 8, distance, far_bucket) + jnp.where(relative > 0, 16, 0)


def norm_scale(stream, gain_row):
    return (
        stream * lax.rsqrt(jnp.mean(stream * stream, axis=-1, keepdims=True) + NORM_EPS) * gain_row
    )


def gelu_tanh(pre_act):
    return jax.nn.gelu(pre_act, approximate=True)


def tensor_sum(partial_rows):
    return lax.psum(partial_rows, "mdl")


def back_sum(partial_rows):
    return lax.psum(partial_rows, "mdl")


def dense_slice(left_rows, partner_side_rows):
    return lax.psum_scatter(
        lax.dot_general(
            left_rows,
            partner_side_rows,
            (((0,), (0,)), ((), ())),
            preferred_element_type=jnp.float32,
        ),
        "dat",
        scatter_dimension=0,
        tiled=True,
    )


def masked_scores(queries, key_heads, bias_heads, item_length, score_scale):
    raw_scores = (
        jnp.einsum("qhd,khd->hqk", queries, key_heads, preferred_element_type=jnp.float32)
        * score_scale
    )
    key_valid = jnp.arange(key_heads.shape[0]) < item_length
    return jnp.where(key_valid[None, None, :], raw_scores + bias_heads, MASK_FILL)


def attend(queries, key_heads, value_heads, bias_heads, item_length, score_scale):
    scores = masked_scores(queries, key_heads, bias_heads, item_length, score_scale)
    row_top = jnp.max(scores, axis=-1, keepdims=True)
    exp_scores = jnp.exp(scores - row_top)
    row_total = jnp.sum(exp_scores, axis=-1, keepdims=True)
    soft_probs = (exp_scores / row_total).astype(jnp.bfloat16)
    mixed_heads = jnp.einsum(
        "hqk,khd->qhd", soft_probs, value_heads, preferred_element_type=jnp.float32
    )
    return (mixed_heads.astype(jnp.bfloat16), (row_top + jnp.log(row_total))[..., 0])


def attend_back(
    queries, key_heads, value_heads, bias_heads, item_length, log_total, grad_mixed, score_scale
):
    scores = masked_scores(queries, key_heads, bias_heads, item_length, score_scale)
    soft_probs = jnp.exp(scores - log_total[..., None])
    grad_probs = jnp.einsum(
        "qhd,khd->hqk", grad_mixed, value_heads, preferred_element_type=jnp.float32
    )
    grad_value = jnp.einsum(
        "hqk,qhd->khd",
        soft_probs.astype(jnp.bfloat16),
        grad_mixed,
        preferred_element_type=jnp.float32,
    )
    grad_scores = soft_probs * (
        grad_probs - jnp.sum(soft_probs * grad_probs, axis=-1, keepdims=True)
    )
    low_scores = grad_scores.astype(jnp.bfloat16)
    grad_query = (
        jnp.einsum("hqk,khd->qhd", low_scores, key_heads, preferred_element_type=jnp.float32)
        * score_scale
    )
    grad_key = (
        jnp.einsum("hqk,qhd->khd", low_scores, queries, preferred_element_type=jnp.float32)
        * score_scale
    )
    return (jnp.stack([grad_query, grad_key, grad_value], axis=1).astype(jnp.bfloat16), grad_scores)


def lamb_direction(weight, gradient, moment_one, moment_two):
    momentum = BETA_ONE * moment_one + (1.0 - BETA_ONE) * gradient
    variance = BETA_TWO * moment_two + (1.0 - BETA_TWO) * gradient * gradient
    direction = (
        momentum / (1.0 - BETA_ONE**STEP) / (jnp.sqrt(variance / (1.0 - BETA_TWO**STEP)) + ADAM_EPS)
        + WEIGHT_DECAY * weight
    )
    return (momentum, variance, direction)


def shards(
    token_ids,
    item_lengths,
    prefix_lengths,
    group_live,
    partner,
    embedding,
    qkv_weight,
    out_weight,
    up_weight,
    down_weight,
    bias_table,
    norm_gains,
    embedding_first,
    embedding_second,
    qkv_first,
    qkv_second,
    out_first,
    out_second,
    up_first,
    up_second,
    down_first,
    down_second,
    bias_first,
    bias_second,
    gains_first,
    gains_second,
):
    item_count, length = token_ids.shape
    dat_size = lax.axis_size("dat")
    head_local = HEADS // lax.axis_size("mdl")
    group_items = item_count * dat_size
    score_scale = HEAD ** (-0.5)
    group_index = lax.axis_index("grp")
    dat_index = lax.axis_index("dat")
    mdl_index = lax.axis_index("mdl")
    slot_index = dat_index * item_count + jnp.arange(item_count)
    live_count = jnp.sum(jnp.where(jnp.arange(group_live.shape[0]) == group_index, group_live, 0))
    live_rows = slot_index < live_count
    live_total = jnp.sum(group_live).astype(jnp.float32)
    onehot = (bucket_table(length)[:, :, None] == jnp.arange(BUCKETS)).astype(jnp.float32)
    bias_heads = jnp.einsum("qkb,bh->hqk", onehot, bias_table, precision=MAX_PRECISION)
    qkv_full, out_full, up_full, down_full = (
        lax.all_gather(qkv_weight.astype(jnp.bfloat16), "dat", axis=0, tiled=True),
        lax.all_gather(out_weight.astype(jnp.bfloat16), "dat", axis=1, tiled=True),
        lax.all_gather(up_weight.astype(jnp.bfloat16), "dat", axis=0, tiled=True),
        lax.all_gather(down_weight.astype(jnp.bfloat16), "dat", axis=0, tiled=True),
    )
    qkv_flat = qkv_full.reshape(qkv_full.shape[0], -1)
    group_ids = lax.all_gather(token_ids, "dat", axis=0, tiled=True).reshape(-1)
    feature_cols = embedding.astype(jnp.bfloat16)[:, group_ids].T
    embedded = lax.all_to_all(feature_cols, "dat", split_axis=0, concat_axis=1, tiled=True).astype(
        jnp.float32
    )
    normed_one_f, norm_one_back = jax.vjp(norm_scale, embedded, norm_gains[0])
    normed_one = normed_one_f.astype(jnp.bfloat16)
    qkv_rows = jnp.dot(normed_one, qkv_flat, preferred_element_type=jnp.float32).astype(
        jnp.bfloat16
    )
    qkv_items = qkv_rows.reshape(item_count, length, 3, head_local, HEAD)

    def forward_item(packed):
        item_qkv, item_length = packed
        return attend(
            item_qkv[:, 0], item_qkv[:, 1], item_qkv[:, 2], bias_heads, item_length, score_scale
        )

    mixed_heads, log_totals = lax.map(forward_item, (qkv_items, item_lengths))
    mixed_rows = mixed_heads.reshape(item_count * length, head_local * HEAD)
    after_attn = embedded + tensor_sum(
        jnp.dot(mixed_rows, out_full, preferred_element_type=jnp.float32)
    )
    normed_two_f, norm_two_back = jax.vjp(norm_scale, after_attn, norm_gains[1])
    normed_two = normed_two_f.astype(jnp.bfloat16)
    gate_pre = jnp.dot(normed_two, up_full, preferred_element_type=jnp.float32)
    gate_act, gelu_back = jax.vjp(gelu_tanh, gate_pre)
    activated = gate_act.astype(jnp.bfloat16)
    down_part = lax.dot_general(
        activated, down_full, (((1,), (1,)), ((), ())), preferred_element_type=jnp.float32
    )
    after_ffn = after_attn + tensor_sum(down_part)
    positions = jnp.arange(length)
    pool_mask = (
        (positions[None, :] >= prefix_lengths[:, None])
        & (positions[None, :] < item_lengths[:, None])
    ).astype(jnp.float32)

    def pool_tail(stream, gain_row):
        normed_three = norm_scale(stream, gain_row).reshape(item_count, length, -1)
        pooled = jnp.sum(normed_three * pool_mask[:, :, None], axis=1) / jnp.sum(
            pool_mask, axis=1, keepdims=True
        )
        return pooled * lax.rsqrt(jnp.sum(pooled * pooled, axis=1, keepdims=True) + NORM_EPS)

    sentence_embeddings, tail_back = jax.vjp(pool_tail, after_ffn, norm_gains[2])
    grouped_embeddings = lax.all_gather(sentence_embeddings, "dat", axis=0, tiled=True)
    similarity_logits = (
        jnp.dot(sentence_embeddings, grouped_embeddings.T, precision=MAX_PRECISION) / SOFTMAX_WARMTH
    )
    column_index = jnp.arange(group_items)
    allowed = (column_index[None, :] < live_count) & (column_index[None, :] != slot_index[:, None])
    masked = jnp.where(allowed, similarity_logits, MASK_FILL)
    row_top = jnp.max(masked, axis=1, keepdims=True)
    log_total = row_top[:, 0] + jnp.log(jnp.sum(jnp.exp(masked - row_top), axis=1))
    mate_hits = column_index[None, :] == partner[:, None]
    target = jnp.sum(jnp.where(mate_hits, similarity_logits, 0.0), axis=1)
    loss_part = jnp.sum(jnp.where(live_rows, log_total - target, 0.0))
    row_weight = jnp.where(live_rows, 1.0 / live_total, 0.0)
    grad_logits = (
        row_weight[:, None]
        * (jnp.exp(masked - log_total[:, None]) - mate_hits.astype(jnp.float32))
        / SOFTMAX_WARMTH
    )
    grad_vectors = jnp.dot(grad_logits, grouped_embeddings, precision=MAX_PRECISION)
    grad_vectors = grad_vectors + lax.psum_scatter(
        jnp.dot(grad_logits.T, sentence_embeddings, precision=MAX_PRECISION),
        "dat",
        scatter_dimension=0,
        tiled=True,
    )
    grad_after_ffn, grad_gain_three = tail_back(grad_vectors)
    grad_ffn = grad_after_ffn.astype(jnp.bfloat16)
    grad_down = dense_slice(grad_ffn, activated)
    grad_act = jnp.dot(grad_ffn, down_full, preferred_element_type=jnp.float32)
    grad_gate = gelu_back(grad_act)[0].astype(jnp.bfloat16)
    grad_up = dense_slice(normed_two, grad_gate)
    two_partial = jnp.dot(grad_gate, up_full.T, preferred_element_type=jnp.float32)
    grad_after_attn, grad_gain_two = norm_two_back(back_sum(two_partial))
    grad_after_attn = grad_after_attn + grad_after_ffn
    grad_attn = grad_after_attn.astype(jnp.bfloat16)
    grad_out = dense_slice(grad_attn, mixed_rows).T
    grad_mixed = jnp.dot(grad_attn, out_full.T, preferred_element_type=jnp.float32).astype(
        jnp.bfloat16
    )
    grad_mixed = grad_mixed.reshape(item_count, length, head_local, HEAD)

    def backward_item(running, packed):
        item_qkv, item_length, item_log_total, item_grad_mixed = packed
        grad_item_qkv, grad_scores = attend_back(
            item_qkv[:, 0],
            item_qkv[:, 1],
            item_qkv[:, 2],
            bias_heads,
            item_length,
            item_log_total,
            item_grad_mixed,
            score_scale,
        )
        return (running + grad_scores, grad_item_qkv)

    score_total, grad_qkv_items = lax.scan(
        backward_item,
        jnp.zeros((head_local, length, length), jnp.float32),
        (qkv_items, item_lengths, log_totals, grad_mixed),
    )
    grad_qkv_rows = grad_qkv_items.reshape(item_count * length, -1)
    grad_qkv = dense_slice(normed_one, grad_qkv_rows).reshape(qkv_weight.shape)
    grad_bias = jnp.einsum("qkb,hqk->bh", onehot, score_total, precision=MAX_PRECISION)
    one_partial = jnp.dot(grad_qkv_rows, qkv_flat.T, preferred_element_type=jnp.float32)
    grad_embedded, grad_gain_one = norm_one_back(back_sum(one_partial))
    grad_embedded = grad_embedded + grad_after_attn
    back_cols = lax.all_to_all(grad_embedded, "dat", split_axis=1, concat_axis=0, tiled=True)
    grad_embed = jnp.zeros_like(embedding).at[:, group_ids].add(back_cols.T)
    grad_qkv, grad_out, grad_up, grad_down, grad_embed = lax.psum(
        (grad_qkv, grad_out, grad_up, grad_down, grad_embed), "grp"
    )
    grad_gains, grad_bias, loss_total = lax.psum(
        (jnp.stack([grad_gain_one, grad_gain_two, grad_gain_three]), grad_bias, loss_part),
        ("grp", "dat"),
    )
    weights = (embedding, qkv_weight, out_weight, up_weight, down_weight, bias_table, norm_gains)
    gradients = (grad_embed, grad_qkv, grad_out, grad_up, grad_down, grad_bias, grad_gains)
    moments = (
        (embedding_first, embedding_second),
        (qkv_first, qkv_second),
        (out_first, out_second),
        (up_first, up_second),
        (down_first, down_second),
        (bias_first, bias_second),
        (gains_first, gains_second),
    )
    results = [
        lamb_direction(weight, gradient, states[0], states[1])
        for weight, gradient, states in zip(weights, gradients, moments)
    ]
    first_mdl = (mdl_index == 0).astype(jnp.float32)
    first_dat = (dat_index == 0).astype(jnp.float32)
    holder_mask = [first_mdl, 1.0, 1.0, 1.0, 1.0, first_dat]
    square_rows = [
        jnp.stack(
            [
                jnp.sum(weights[position] * weights[position]),
                jnp.sum(results[position][2] * results[position][2]),
            ]
        )
        * holder_mask[position]
        for position in range(6)
    ]
    gain_rows = jnp.stack(
        [jnp.sum(norm_gains * norm_gains, axis=1), jnp.sum(results[6][2] * results[6][2], axis=1)],
        axis=1,
    ) * (first_mdl * first_dat)
    square_table = jnp.concatenate([jnp.stack(square_rows), gain_rows], axis=0)
    matrix_norms = jnp.sqrt(lax.psum(square_table, ("dat", "mdl")))
    trust_ratio = matrix_norms[:, 0] / matrix_norms[:, 1]
    updated = [
        weights[position] - LEARN_RATE * trust_ratio[position] * results[position][2]
        for position in range(6)
    ]
    updated.append(norm_gains - LEARN_RATE * trust_ratio[6:, None] * results[6][2])
    outputs = [jnp.stack([loss_total, live_total]), matrix_norms]
    for position in range(7):
        outputs.extend([results[position][0], results[position][1], updated[position]])
    return tuple(outputs)


def solution(mesh):
    placed = (
        P(("grp", "dat"), None),
        P(("grp", "dat")),
        P(("grp", "dat")),
        P(),
        P(("grp", "dat")),
        P("dat", None),
        P("dat", None, "mdl"),
        P("mdl", "dat"),
        P("dat", "mdl"),
        P("dat", "mdl"),
        P(None, "mdl"),
        P(),
        P("dat", None),
        P("dat", None),
        P("dat", None, "mdl"),
        P("dat", None, "mdl"),
        P("mdl", "dat"),
        P("mdl", "dat"),
        P("dat", "mdl"),
        P("dat", "mdl"),
        P("dat", "mdl"),
        P("dat", "mdl"),
        P(None, "mdl"),
        P(None, "mdl"),
        P(),
        P(),
    )
    return jax.shard_map(
        shards,
        mesh=mesh,
        in_specs=placed,
        out_specs=(
            P(),
            P(),
            P("dat", None),
            P("dat", None),
            P("dat", None),
            P("dat", None, "mdl"),
            P("dat", None, "mdl"),
            P("dat", None, "mdl"),
            P("mdl", "dat"),
            P("mdl", "dat"),
            P("mdl", "dat"),
            P("dat", "mdl"),
            P("dat", "mdl"),
            P("dat", "mdl"),
            P("dat", "mdl"),
            P("dat", "mdl"),
            P("dat", "mdl"),
            P(None, "mdl"),
            P(None, "mdl"),
            P(None, "mdl"),
            P(),
            P(),
            P(),
        ),
        check_vma=False,
    )
```

profile of v0, /device:TPU:17, one launch (start us, length us, event | category | flops | bytes accessed | tf_op | source)
XLA Modules:
  0.0 2464.7 jit_solution(18040672817684092020)
XLA Ops:
  16.5 23.6 multiply_reduce_fusion.2
  40.1 18.5 copy.206
  58.6 38.9 %gather_fusion = bf16[8192,192]{1,0:T(8,128)(2,1)} fusion(bf16[192,32128]{0,1:T(8,128)(2,1)} %copy.206, s32[8192]{0:T(1024)S(1)} %broadcast_clamp_fusion), kind=kCustom, calls=%fused_computation | custom fusion | bytes 6324224 | tf_op jit(solution)/shard_map/gather | solution.py:174
  120.0 45.9 %copy.210 = pred[512,512,32]{1,2,0:T(32,128)(4,1)S(1)} copy(pred[512,512,32]{0,2,1:T(32,128)(4,1)} %iota_compare_fusion.2) | data formatting | bytes 16777216 | tf_op jit(solution)/shard_map/eq | solution.py:164
  234.0 44.4 %while.25 = (s32[]{:T(128)}, bf16[4,512,6,64]{1,3,2,0:T(8,128)(2,1)}, f32[4,6,512]{2,1,0:T(8,128)}, bf16[4,512,3,6,64]{1,4,3,2,0:T(8,128)(2,1)}, s32[4]{0:T(128)}, /*index=5*/f32[6,512,512]{1,2,0:T(8,128)}, s32[]{:T(128)}) while((s32[]{:T(128)}, bf16[4,512,6,64]{1,3,2,0:T(8,128)(2,1)}, f32[4,6,512]{2,1,0:T(8,128)}, ...), condition=%wide.region_5.6_spmd, body=%wide.region_2.5_spmd.sunk | while | flops 417003008 | bytes 29209712 | solution.py:191
  302.2 21.6 all-reduce.9.cloned.1.call-done
  331.7 32.6 %all-gather.8.cloned.1.call-done = bf16[768,1536]{1,0:T(8,128)(2,1)} async-done(((bf16[192,1536]{1,0:T(8,128)(2,1)}), bf16[768,1536]{1,0:T(8,128)(2,1)}) %all-gather.8.cloned.1.call-update) | async-done | bytes 2359312 | tf_op jit(solution)/shard_map/all_gather | solution.py:169
  364.3 13.1 multiply_convert_fusion
  377.4 26.8 %all-gather.10.cloned.1.call-done = bf16[768,1536]{1,0:T(8,128)(2,1)} async-done(((bf16[192,1536]{1,0:T(8,128)(2,1)}), bf16[768,1536]{1,0:T(8,128)(2,1)}) %all-gather.10.cloned.1.call-update) | async-done | bytes 2359312 | tf_op jit(solution)/shard_map/all_gather | solution.py:170
  419.9 26.8 %all-reduce.11.cloned.1.call-done = f32[2048,768]{1,0:T(8,128)} async-done(((f32[2048,768]{1,0:T(8,128)}), f32[2048,768]{1,0:T(8,128)}) %all-reduce.11.cloned.1.call-update) | async-done | bytes 6291472 | tf_op jit(solution)/shard_map/psum | solution.py:43
  464.3 12.0 all-reduce
  483.5 14.2 fusion.34
  507.4 38.2 %all-reduce.13.cloned.1.call-done = f32[2048,768]{1,0:T(8,128)} async-done(((f32[2048,768]{1,0:T(8,128)}), f32[2048,768]{1,0:T(8,128)}) %all-reduce.13.cloned.1.call-update) | async-done | bytes 6291472 | tf_op jit(solution)/shard_map/psum | solution.py:47
  566.6 121.7 %while.26 = (s32[]{:T(128)}, f32[6,512,512]{1,2,0:T(8,128)}, bf16[4,512,3,6,64]{1,4,3,2,0:T(8,128)(2,1)}, s32[4]{0:T(128)}, bf16[4,512,3,6,64]{1,4,3,2,0:T(8,128...) while((s32[]{:T(128)}, f32[6,512,512]{1,2,0:T(8,128)}, ...), condition=%wide.region_27.28_spmd.clone, body=%wide.region_25.27_spmd.clone.sunk | while | flops 1030026752 | bytes 154993920 | solution.py:274
  609.9 11.7 fusion.151
  731.8 12.0 fusion.87
  771.4 57.5 %reduce-scatter.5.cloned.1.call-done = f32[192,1152]{1,0:T(8,128)} async-done(((f32[768,1152]{1,0:T(8,128)}), f32[192,1152]{1,0:T(8,128)}) %reduce-scatter.5.cloned.1.call-update) | async-done | bytes 884752 | tf_op jit(solution)/shard_map/reduce_scatter | solution.py:51
  831.0 26.0 %all-to-all-done.1 = f32[2048,4,192]{0,2,1:T(8,128)} async-done(((f32[2048,4,192]{0,2,1:T(8,128)}), f32[2048,4,192]{0,2,1:T(8,128)}, u32[]{:S(2)}, u32[]{:S(2)}) %all-to-all-start.1) | async-done | bytes 6291488 | tf_op jit(solution)/shard_map/all_to_all | solution.py:285
  865.2 58.7 %scatter_custom_fusion = f32[192,32128]{0,1:T(8,128)} fusion(s32[8192]{0:T(1024)} %bitcast.247, f32[8192,192]{1,0:T(8,128)} %bitcast.235, f32[]{:T(128)} %constant.67.clone.1), kind=kCustom, calls=%fused_computation.55 | custom fusion | flops 1572864 | bytes 24674816 | tf_op jit(solution)/shard_map/scatter-add | solution.py:286
  929.4 60.7 %reduce-scatter.9.cloned.1.call-done = f32[192,1536]{1,0:T(8,128)} async-done(((f32[768,1536]{1,0:T(8,128)}), f32[192,1536]{1,0:T(8,128)}) %reduce-scatter.9.cloned.1.call-update) | async-done | bytes 1179664 | tf_op jit(solution)/shard_map/reduce_scatter | solution.py:51
  990.1 28.5 %copy.227 = f32[192,32128]{0,1:T(8,128)} copy(f32[192,32128]{1,0:T(8,128)} %param.35) | data formatting | bytes 49348608 | tf_op args[5]
  1018.6 28.6 %copy.215 = f32[192,32128]{0,1:T(8,128)} copy(f32[192,32128]{1,0:T(8,128)} %param.42) | data formatting | bytes 49348608 | tf_op args[12]
  1047.2 28.6 %copy.226 = f32[192,32128]{0,1:T(8,128)} copy(f32[192,32128]{1,0:T(8,128)} %param.43) | data formatting | bytes 49348608 | tf_op args[13]
  1075.8 19.8 fusion.51
  1096.3 84.2 %all-reduce.1 = (f32[1]{0:T(128)}, f32[32,6]{0,1:T(8,128)}, f32[3,768]{1,0:T(4,128)}) all-reduce(f32[1]{0:T(128)} %bitcast.20, f32[32,6]{0,1:T(8,128)} %fusion.51, f32[3,768]{1,0:T(4,128)} %pad_maximum_fusion), channel_id=1, replica_groups=mesh['grp'=4,'dat'=4,'mdl'=2] {'grp','dat'}, use_global_device_ids=true, to_apply=%region_17.18 | all-reduce | flops 2497 | bytes 19976 | tf_op jit(solution)/shard_map/psum | solution.py:290
  1184.6 1013.8 %all-reduce.17.cloned.1.call-done = (f32[192,32128]{0,1:T(8,128)}, f32[192,3,384]{2,0,1:T(8,128)}, f32[384,192]{0,1:T(8,128)}, f32[192,1536]{1,0:T(8,128)}, f32[192,1536]{1,0:T(8,128)}) async-done(((f32[192,32128]{0,1:T(8,128)}, f32[192,3,384]{2,0,1:T(8,128)}, f32[384,192]{0,1:T(8,128)}, f32[192,1536]{1,0:T(8,128)}, f32[192,1536]{1,0:T(8,128)}), (f32[192,32128]{0,1:T(8,128)}, f32[192,3,384]{2,0,1:T(8,128)}, ...) | async-done | bytes 28213264 | tf_op jit(solution)/shard_map/psum | solution.py:287
  2225.5 64.7 %multiply_reduce_fusion.1 = (f32[]{:T(128)}, f32[192,32128]{0,1:T(8,128)}, f32[192,32128]{0,1:T(8,128)}) fusion(f32[192,32128]{0,1:T(8,128)} %copy.227, f32[192,32128]{0,1:T(8,128)} %get-tuple-element.369, f32[192,32128]{0,1:T(8,128)} %copy.215, f32[192,32128]{0,1:T(8,128)} %copy.226), kind=kLoop, calls=%fused_computation.49 | loop fusion | flops 92528640 | bytes 148045824 | tf_op jit(solution)/shard_map/reduce_sum | solution.py:316
  2296.0 12.8 psum.103
  2314.6 29.1 %copy.236 = f32[192,32128]{1,0:T(8,128)} copy(f32[192,32128]{0,1:T(8,128)} %get-tuple-element.389) | data formatting | bytes 49348608
  2343.8 29.1 %copy.237 = f32[192,32128]{1,0:T(8,128)} copy(f32[192,32128]{0,1:T(8,128)} %get-tuple-element.390) | data formatting | bytes 49348608
  2372.9 43.1 %multiply_subtract_fusion = f32[192,32128]{0,1:T(8,128)} fusion(f32[192,32128]{0,1:T(8,128)} %copy.227, f32[]{:T(128)} %bitcast.48, f32[192,32128]{0,1:T(8,128)} %get-tuple-element.390, f32[192,32128]{0,1:T(8,128)} %get-tuple-element.389), kind=kLoop, calls=%fused_computation.48 | loop fusion | flops 49348608 | bytes 98697216 | tf_op jit(solution)/shard_map/sub | solution.py:330
  2416.0 29.1 %copy.238 = f32[192,32128]{1,0:T(8,128)} copy(f32[192,32128]{0,1:T(8,128)} %multiply_subtract_fusion) | data formatting | bytes 49348608
  (343 shorter events, 493.5 us)
Async XLA Ops:
  7.2 192.6 %all-gather.6.cloned.1.call-start = ((), (), s32[]{:S(2)}) async-start(), calls=%async_computation.6 | async-start | bytes 2211840 | tf_op jit(solution)/shard_map/all_gather | solution.py:167
  103.6 91.9 %all-to-all-start = ((bf16[4,2048,192]{1,2,0:T(8,128)(2,1)}), bf16[4,2048,192]{1,2,0:T(8,128)(2,1)S(1)}, u32[]{:S(2)}, u32[]{:S(2)}) async-start(bf16[4,2048,192]{1,2,0:T(8,128)(2,1)} %copy.207), calls=%async_computation | async-start | bytes 6291456 | tf_op jit(solution)/shard_map/all_to_all | solution.py:175
  107.3 216.4 %all-reduce.9.cloned.1.call-start = ((), (), s32[]{:S(2)}) async-start(), calls=%async_computation.7 | async-start | bytes 12582912 | tf_op jit(solution)/shard_map/psum | solution.py:43
  119.2 46.7 %copy-start.35 = (f32[768]{0:T(1024)}, f32[768]{0:T(1024)S(1)}, u32[]{:S(2)}) copy-start(f32[768]{0:T(1024)S(1)} %get-tuple-element.331) | copy-start | bytes 9220
  119.2 432.9 %copy-start.37 = (f32[768]{0:T(1024)}, f32[768]{0:T(1024)S(1)}, u32[]{:S(2)}) copy-start(f32[768]{0:T(1024)S(1)} %get-tuple-element.330) | copy-start | bytes 9220
  120.0 45.9 %copy-start.39 = (f32[32,6]{0,1:T(8,128)S(1)}, f32[32,6]{0,1:T(8,128)}, u32[]{:S(2)}) copy-start(f32[32,6]{0,1:T(8,128)} %param.40) | copy-start | bytes 2308
  287.2 77.1 %all-gather.8.cloned.1.call-start = ((), (), s32[]{:S(2)}) async-start(), calls=%async_computation.8 | async-start | bytes 2949120 | tf_op jit(solution)/shard_map/all_gather | solution.py:169
  289.4 114.8 %all-gather.10.cloned.1.call-start = ((), (), s32[]{:S(2)}) async-start(), calls=%async_computation.9 | async-start | bytes 2949120 | tf_op jit(solution)/shard_map/all_gather | solution.py:170
  291.7 155.1 %all-reduce.11.cloned.1.call-start = ((), (), s32[]{:S(2)}) async-start(), calls=%async_computation.10 | async-start | bytes 12582912 | tf_op jit(solution)/shard_map/psum | solution.py:43
  331.7 220.4 %copy-start.33 = (f32[2048]{0:T(1024)}, f32[2048]{0:T(1024)S(1)}, u32[]{:S(2)}) copy-start(f32[2048]{0:T(1024)S(1)} %fusion.74) | copy-start | bytes 24580
  413.8 131.7 %all-reduce.13.cloned.1.call-start = ((), (), s32[]{:S(2)}) async-start(), calls=%async_computation.11 | async-start | bytes 12582912 | tf_op jit(solution)/shard_map/psum | solution.py:47
  419.9 34.8 %copy-start.28 = (f32[768]{0:T(1024)S(1)}, f32[768]{0:T(1024)}, u32[]{:S(2)}) copy-start(f32[768]{0:T(1024)} %get-tuple-element.329) | copy-start | bytes 9220
  483.4 14.3 copy-start.20
  483.5 16.9 copy-start.48
  507.3 236.6 %all-reduce.15.cloned.1.call-start = ((), (), s32[]{:S(2)}) async-start(), calls=%async_computation.12 | async-start | bytes 12582912 | tf_op jit(solution)/shard_map/psum | solution.py:47
  705.3 123.6 %reduce-scatter.5.cloned.1.call-start = ((), (), s32[]{:S(2)}) async-start(), calls=%async_computation.13 | async-start | bytes 4423680 | tf_op jit(solution)/shard_map/reduce_scatter | solution.py:51
  714.8 209.1 %reduce-scatter.7.cloned.1.call-start = ((), (), s32[]{:S(2)}) async-start(), calls=%async_computation.14 | async-start | bytes 1474560 | tf_op jit(solution)/shard_map/reduce_scatter | solution.py:51
  722.0 207.3 %reduce-scatter.11.cloned.1.call-start = ((), (), s32[]{:S(2)}) async-start(), calls=%async_computation.16 | async-start | bytes 5898240 | tf_op jit(solution)/shard_map/reduce_scatter | solution.py:51
  731.7 12.2 copy-start.27
  731.8 258.3 %reduce-scatter.9.cloned.1.call-start = ((), (), s32[]{:S(2)}) async-start(), calls=%async_computation.15 | async-start | bytes 5898240 | tf_op jit(solution)/shard_map/reduce_scatter | solution.py:51
  765.6 91.4 %all-to-all-start.1 = ((f32[2048,4,192]{0,2,1:T(8,128)}), f32[2048,4,192]{0,2,1:T(8,128)}, u32[]{:S(2)}, u32[]{:S(2)}) async-start(f32[2048,4,192]{0,2,1:T(8,128)} %bitcast.229), calls=%async_computation.1 | async-start | bytes 12582912 | tf_op jit(solution)/shard_map/all_to_all | solution.py:285
  770.9 1427.4 %all-reduce.17.cloned.1.call-start = ((), (), s32[]{:S(2)}) async-start(), calls=%async_computation.17 | async-start | bytes 72876032 | tf_op jit(solution)/shard_map/psum | solution.py:287
  1047.1 28.6 %copy-start.43 = (f32[768]{0:T(1024)S(1)}, f32[768]{0:T(1024)}, u32[]{:S(2)}) copy-start(f32[768]{0:T(1024)} %get-tuple-element.319) | copy-start | bytes 9220
  1047.1 28.6 %copy-start.41 = (f32[768]{0:T(1024)S(1)}, f32[768]{0:T(1024)}, u32[]{:S(2)}) copy-start(f32[768]{0:T(1024)} %get-tuple-element.317) | copy-start | bytes 9220
  1047.2 28.7 %copy-start.19 = (s32[512,512]{0,1:T(8,128)S(1)}, s32[512,512]{0,1:T(8,128)}, u32[]{:S(2)}) copy-start(s32[512,512]{0,1:T(8,128)} %fusion.54) | copy-start | bytes 3145732
  1075.7 19.9 copy-start.42
  1075.7 104.8 %copy-start.30 = (f32[3,768]{1,0:T(4,128)S(1)}, f32[3,768]{1,0:T(4,128)}, u32[]{:S(2)}) copy-start(f32[3,768]{1,0:T(4,128)} %param.41) | copy-start | bytes 27652
  1075.7 106.9 %copy-start.40 = (f32[32,6]{0,1:T(8,128)S(1)}, f32[32,6]{0,1:T(8,128)}, u32[]{:S(2)}) copy-start(f32[32,6]{0,1:T(8,128)} %param.40) | copy-start | bytes 2308
  1075.7 1122.6 %copy-start.22 = (f32[384,192]{0,1:T(8,128)S(1)}, f32[384,192]{0,1:T(8,128)}, u32[]{:S(2)}) copy-start(f32[384,192]{0,1:T(8,128)} %param.37) | copy-start | bytes 884740
  1075.8 1128.5 %copy-start.13 = (f32[192,3,384]{2,0,1:T(8,128)S(1)}, f32[192,3,384]{2,0,1:T(8,128)}, u32[]{:S(2)}) copy-start(f32[192,3,384]{2,0,1:T(8,128)} %param.36) | copy-start | bytes 2654212
  1095.6 1116.1 %copy-start.11 = (f32[192,1536]{1,0:T(8,128)S(1)}, f32[192,1536]{1,0:T(8,128)}, u32[]{:S(2)}) copy-start(f32[192,1536]{1,0:T(8,128)} %param.39) | copy-start | bytes 3538948
  1095.6 1116.1 %copy-start.12 = (f32[192,1536]{1,0:T(8,128)S(1)}, f32[192,1536]{1,0:T(8,128)}, u32[]{:S(2)}) copy-start(f32[192,1536]{1,0:T(8,128)} %param.38) | copy-start | bytes 3538948
  (46 other events, 238.9 us)
Sparse Core Ops, SparseCore 0:
  10.4 33.6 all-gather.5
  287.3 36.3 all-reduce.8
  326.3 37.9 all-gather.7
  366.7 37.4 all-gather.9
  413.9 32.7 all-reduce.10
  507.4 38.0 all-reduce.12
  705.4 33.2 all-reduce.14
  741.7 87.1 reduce-scatter.4
  832.4 36.9 reduce-scatter.6
  872.2 57.0 reduce-scatter.10
  932.9 57.0 reduce-scatter.8
  993.6 1204.6 all-reduce.16
where the time goes:
time: 2480 us; the launch traced here: 2460 us
  waiting for transfers between devices  1310 us (53%)
  local copies, waits for them, and re-layouts  415 us (17%)
  other arithmetic  375 us (15%)
  matrix products  203 us (8%)
  blocking collectives  132 us (5%)
    psum x1, waiting for transfers between devices, shards(): lax.psum((grad_qkv, grad_out, grad_up, grad_down, grad_embed), 'grp')  1010 us
    unnamed x108, local copies, waits for them, and re-layouts  192 us
    reduce_scatter x4, waiting for transfers between devices, dense_slice(): lax.psum_scatter(lax.dot_general(left_rows, partner_side_rows, (((0,), (0...  124 us
    psum x1, blocking collectives, shards(): lax.psum((jnp.stack([grad_gain_one, grad_gain_two, grad_gain_three]), gra...  84.2 us
    reduce_sum x1, other arithmetic, shards(): jnp.sum(results[position][2] * results[position][2])  64.7 us
    scatter-add x1, other arithmetic, shards(): grad_embed = jnp.zeros_like(embedding).at[:, group_ids].add(back_cols.T)  58.7 us
    sub x6, other arithmetic, shards(): weights[position]  54.1 us
  transfers between devices with their start and end apart: 14, of which 10 were waited for; matrix products, arithmetic and copies ran while one was open for 18% of the time, Pallas kernels for 0%

commit v1 on v0

v1 whole, which is shorter than its diff:
```python
import functools

import jax
import jax.numpy as jnp
from jax import lax
from jax.experimental import pallas as pl
from jax.experimental.pallas import tpu as pltpu
from jax.sharding import PartitionSpec as P

HEADS = 12
HEAD = 64
BUCKETS = 32
STEP = 10


SOFTMAX_WARMTH = 0.01
NORM_EPS = 1e-06
BUCKET_EDGES = (12, 16, 23, 32, 46, 64, 91)
BETA_ONE = 0.9
BETA_TWO = 0.999
ADAM_EPS = 1e-06
WEIGHT_DECAY = 0.01
LEARN_RATE = 0.5
MASK_FILL = -1000000000.0
MAX_PRECISION = lax.Precision.HIGHEST
LANES = 128
bf = jnp.bfloat16
f32 = jnp.float32


BLOCK=128
NT=(((1,),(1,)),((),()))
TN=(((0,),(0,)),((),()))

def toeplitz(line, rows):
    out = line
    size = 1
    while size < rows:
        out = jnp.concatenate([out, pltpu.roll(out, size, 1)], axis=0)
        size *= 2
    return out

def diagonal_sums(square):
    rows, width = square.shape
    while rows > 8:
        rows //= 2
        square = square[:rows] + pltpu.roll(square[rows:], width - rows, 1)
    for shift in (4, 2, 1):
        square = square + pltpu.roll(pltpu.roll(square, width - shift, 1), 8 - shift, 0)
    return square[:1]

def attend_kernel(pairs, scale, lens_ref, line_ref, qkv_ref, mixed_ref, lse_ref):
    items, length, _ = mixed_ref.shape
    blocks = length // BLOCK
    first = lax.broadcasted_iota(jnp.int32, (1, LANES), 1) < HEAD
    lane = lax.broadcasted_iota(jnp.int32, (BLOCK, LANES), 1)
    column = lax.broadcasted_iota(jnp.int32, (1, length), 1)

    def one_pair(pair, carry):
        at = lambda part: pl.ds(pl.multiple_of((part * pairs + pair) * LANES, LANES), LANES)
        biases = [toeplitz(line_ref[pl.ds(2 * pair + head, 1), :], BLOCK) for head in range(2)]
        for item in range(items):
            keys = qkv_ref[item, :, at(1)]
            values = qkv_ref[item, :, at(2)]
            valid = column < lens_ref[item]
            for block in range(blocks):
                rows = pl.ds(block * BLOCK, BLOCK)
                queries = qkv_ref[item, rows, at(0)] * scale
                low = length - block * BLOCK
                mixed = []
                stats = jnp.zeros((BLOCK, LANES), f32)
                for head in range(2):
                    mine = first if head == 0 else jnp.logical_not(first)
                    scores = lax.dot_general(jnp.where(mine, queries, 0), keys, NT, preferred_element_type=f32)
                    scores = jnp.where(valid, scores + biases[head][:, low : low + length], MASK_FILL)
                    top = jnp.max(scores, axis=1, keepdims=True)
                    powers = jnp.exp(scores - top)
                    whole = jnp.sum(powers, axis=1, keepdims=True)
                    probs = (powers * (1.0 / whole)).astype(bf)
                    mixed.append(jnp.dot(probs, values, preferred_element_type=f32))
                    stats = jnp.where(lane == head, top + jnp.log(whole), stats)
                mixed_ref[item, rows, at(0)] = jnp.where(first, mixed[0], mixed[1]).astype(bf)
                lse_ref[item, rows, at(0)] = stats
        return carry

    lax.fori_loop(0, pairs, one_pair, 0)

def attend(qkv, lines, lengths):
    items, length, width = qkv.shape
    width //= 3
    pairs = width // LANES
    vm = pl.BlockSpec(memory_space=pltpu.VMEM)
    return pl.pallas_call(
        functools.partial(attend_kernel, pairs, HEAD ** -0.5),
        in_specs=[pl.BlockSpec(memory_space=pltpu.SMEM), vm, vm],
        out_specs=[vm, vm],
        out_shape=[jax.ShapeDtypeStruct((items, length, width), bf), jax.ShapeDtypeStruct((items, length, width), f32)],
        compiler_params=pltpu.CompilerParams(vmem_limit_bytes=40 * 2**20),
        cost_estimate=pl.CostEstimate(flops=8 * items * length * length * width, bytes_accessed=items * length * width * 12, transcendentals=items * length * length * width // HEAD),
        name="attend",
    )(lengths, lines, qkv)

def attend_back_kernel(pairs, scale, lens_ref, line_ref, qkv_ref, lse_ref, dmix_ref, dqkv_ref, dline_ref, dkey, dval, diag):
    items, length, _ = dmix_ref.shape
    blocks = length // BLOCK
    first = lax.broadcasted_iota(jnp.int32, (1, LANES), 1) < HEAD
    column = lax.broadcasted_iota(jnp.int32, (1, length), 1)

    def one_pair(pair, carry):
        at = lambda part: pl.ds(pl.multiple_of((part * pairs + pair) * LANES, LANES), LANES)
        biases = [toeplitz(line_ref[pl.ds(2 * pair + head, 1), :], BLOCK) for head in range(2)]
        diag[...] = jnp.zeros_like(diag)
        for item in range(items):
            keys = qkv_ref[item, :, at(1)]
            values = qkv_ref[item, :, at(2)]
            valid = column < lens_ref[item]
            for block in range(blocks):
                rows = pl.ds(block * BLOCK, BLOCK)
                queries = qkv_ref[item, rows, at(0)] * scale
                given = dmix_ref[item, rows, at(0)]
                stats = lse_ref[item, rows, at(0)]
                low = length - block * BLOCK
                dquery, dkeys, dvals = [], [], []
                for head in range(2):
                    mine = first if head == 0 else jnp.logical_not(first)
                    scores = lax.dot_general(jnp.where(mine, queries, 0), keys, NT, preferred_element_type=f32)
                    scores = jnp.where(valid, scores + biases[head][:, low : low + length], MASK_FILL)
                    probs = jnp.exp(scores - stats[:, head : head + 1])
                    dprobs = lax.dot_general(jnp.where(mine, given, 0), values, NT, preferred_element_type=f32)
                    inner = jnp.sum(probs * dprobs, axis=1, keepdims=True)
                    dscores = probs * (dprobs - inner)
                    diag[head, :, low : low + length] += dscores
                    low_scores = dscores.astype(bf)
                    dquery.append(jnp.dot(low_scores, keys, preferred_element_type=f32))
                    dkeys.append(lax.dot_general(low_scores, queries, TN, preferred_element_type=f32))
                    dvals.append(lax.dot_general(probs.astype(bf), given, TN, preferred_element_type=f32))
                dqkv_ref[item, rows, at(0)] = (jnp.where(first, dquery[0], dquery[1]) * scale).astype(bf)
                dk = jnp.where(first, dkeys[0], dkeys[1])
                dv = jnp.where(first, dvals[0], dvals[1])
                if block == 0:
                    dkey[...] = dk
                    dval[...] = dv
                else:
                    dkey[...] += dk
                    dval[...] += dv
            dqkv_ref[item, :, at(1)] = dkey[...].astype(bf)
            dqkv_ref[item, :, at(2)] = dval[...].astype(bf)
        for head in range(2):
            dline_ref[pl.ds(2 * pair + head, 1), :] = diagonal_sums(diag[head])
        return carry

    lax.fori_loop(0, pairs, one_pair, 0)

def attend_back(qkv, lines, lengths, lse, dmixed):
    items, length, width = dmixed.shape
    pairs = width // LANES
    vm = pl.BlockSpec(memory_space=pltpu.VMEM)
    return pl.pallas_call(
        functools.partial(attend_back_kernel, pairs, HEAD ** -0.5),
        in_specs=[pl.BlockSpec(memory_space=pltpu.SMEM), vm, vm, vm, vm],
        out_specs=[vm, vm],
        out_shape=[jax.ShapeDtypeStruct(qkv.shape, bf), jax.ShapeDtypeStruct(lines.shape, f32)],
        scratch_shapes=[pltpu.VMEM((length, LANES), f32), pltpu.VMEM((length, LANES), f32), pltpu.VMEM((2, BLOCK, 2 * length), f32)],
        compiler_params=pltpu.CompilerParams(vmem_limit_bytes=40 * 2**20),
        cost_estimate=pl.CostEstimate(flops=20 * items * length * length * width, bytes_accessed=items * length * width * 20, transcendentals=items * length * length * width // HEAD),
        name="attend_back",
    )(lengths, lines, qkv, lse, dmixed)


def gather_kernel(features, tiles, load_steps, batch, table_ref, ids_ref, out_ref, stash, rows):
    step = pl.program_id(0)
    width = table_ref.shape[1]

    @pl.when(step < load_steps)
    def _():
        base = pl.multiple_of(step * width, width)
        for tile in range(tiles):
            low = tile * LANES
            high = min(features, low + LANES)
            part = table_ref[low:high, :].astype(bf).astype(jnp.float32)
            if high - low < LANES:
                part = jnp.concatenate([part, jnp.zeros((LANES - (high - low), width), jnp.float32)], axis=0)
            stash[tile, pl.ds(base, width), :] = part.T

    @pl.when(step >= load_steps)
    def _():
        count = out_ref.shape[0]
        for half in range(2):
            def take(index, carry):
                start = pl.multiple_of(index * batch, batch)
                for inner in range(batch):
                    token = ids_ref[0, half, start + inner]
                    for tile in range(tiles):
                        rows[half, tile, pl.ds(start + inner, 1), :] = stash[tile, pl.ds(token, 1), :]
                return carry
            lax.fori_loop(0, count // batch, take, 0)
        pieces = []
        for half in range(2):
            for tile in range(tiles):
                low = tile * LANES
                pieces.append(rows[half, tile, :, : min(LANES, features - low)])
        out_ref[...] = jnp.concatenate(pieces, axis=1).astype(bf)

def gather_rows(table, ids, width=2048, chunk=256, batch=32):
    features, vocab = table.shape
    tiles = pl.cdiv(features, LANES)
    load_steps = pl.cdiv(vocab, width)
    steps = ids.shape[0]
    return pl.pallas_call(
        functools.partial(gather_kernel, features, tiles, load_steps, batch),
        grid=(load_steps + steps,),
        in_specs=[
            pl.BlockSpec((features, width), lambda s: (0, jnp.minimum(s, load_steps - 1))),
            pl.BlockSpec((1, 2, chunk), lambda s: (jnp.maximum(s - load_steps, 0), 0, 0), memory_space=pltpu.SMEM),
        ],
        out_specs=pl.BlockSpec((chunk, 2 * features), lambda s: (jnp.maximum(s - load_steps, 0), 0)),
        out_shape=jax.ShapeDtypeStruct((steps * chunk, 2 * features), bf),
        scratch_shapes=[
            pltpu.VMEM((tiles, load_steps * width, LANES), jnp.float32),
            pltpu.VMEM((2, tiles, chunk, LANES), jnp.float32),
        ],
        compiler_params=pltpu.CompilerParams(vmem_limit_bytes=60 * 2**20),
        name="gather_rows",
    )(table, ids)

def scatter_kernel(features, tiles, scatter_steps, batch, ids_ref, ids_row_ref, rows_ref, out_ref, total, summed):
    step = pl.program_id(0)
    width = out_ref.shape[1]
    count = rows_ref.shape[0]

    @pl.when(step == 0)
    def _():
        total[...] = jnp.zeros_like(total)

    @pl.when(step < scatter_steps)
    def _():
        place = lax.broadcasted_iota(jnp.int32, (count, count), 0) // batch
        same_batch = place == lax.broadcasted_iota(jnp.int32, (count, count), 1) // batch
        for half in range(2):
            across = jnp.broadcast_to(ids_row_ref[0, half : half + 1, :], (count, count))
            match = jnp.where((across == across.T) & same_batch, 1.0, 0.0).astype(bf)
            merged = jnp.dot(match, rows_ref[:, half * features : (half + 1) * features], preferred_element_type=jnp.float32)
            for tile in range(tiles):
                low = tile * LANES
                high = min(features, low + LANES)
                part = merged[:, low:high]
                if high - low < LANES:
                    part = jnp.concatenate([part, jnp.zeros((count, LANES - (high - low)), jnp.float32)], axis=1)
                summed[half, tile] = part
        for half in range(2):
            def add(index, carry):
                start = pl.multiple_of(index * batch, batch)
                tokens = [ids_ref[0, half, start + inner] for inner in range(batch)]
                for tile in range(tiles):
                    fresh = [
                        total[tile, pl.ds(tokens[inner], 1), :] + summed[half, tile, pl.ds(start + inner, 1), :]
                        for inner in range(batch)
                    ]
                    for inner in range(batch):
                        total[tile, pl.ds(tokens[inner], 1), :] = fresh[inner]
                return carry
            lax.fori_loop(0, count // batch, add, 0)

    @pl.when(step >= scatter_steps)
    def _():
        base = pl.multiple_of((step - scatter_steps) * width, width)
        for tile in range(tiles):
            low = tile * LANES
            high = min(features, low + LANES)
            out_ref[low:high, :] = total[tile, pl.ds(base, width), :].T[: high - low].astype(bf)

def scatter_rows(rows, ids, vocab, features, width=2048, chunk=256, batch=32):
    tiles = pl.cdiv(features, LANES)
    steps = ids.shape[0]
    flush = pl.cdiv(vocab, width)
    at = lambda s: jnp.minimum(s, steps - 1)
    return pl.pallas_call(
        functools.partial(scatter_kernel, features, tiles, steps, batch),
        grid=(steps + flush,),
        in_specs=[
            pl.BlockSpec((1, 2, chunk), lambda s: (at(s), 0, 0), memory_space=pltpu.SMEM),
            pl.BlockSpec((1, 2, chunk), lambda s: (at(s), 0, 0)),
            pl.BlockSpec((chunk, 2 * features), lambda s: (at(s), 0)),
        ],
        out_specs=pl.BlockSpec((features, width), lambda s: (0, jnp.maximum(s - steps, 0))),
        out_shape=jax.ShapeDtypeStruct((features, vocab), bf),
        scratch_shapes=[
            pltpu.VMEM((tiles, flush * width, LANES), jnp.float32),
            pltpu.VMEM((2, tiles, chunk, LANES), jnp.float32),
        ],
        compiler_params=pltpu.CompilerParams(vmem_limit_bytes=60 * 2**20),
        name="scatter_rows",
    )(ids, ids, rows)


def lamb_direction(weight, gradient, moment_one, moment_two):
    momentum = BETA_ONE * moment_one + (1.0 - BETA_ONE) * gradient
    variance = BETA_TWO * moment_two + (1.0 - BETA_TWO) * gradient * gradient
    direction = (
        momentum / (1.0 - BETA_ONE**STEP) / (jnp.sqrt(variance / (1.0 - BETA_TWO**STEP)) + ADAM_EPS)
        + WEIGHT_DECAY * weight
    )
    return (momentum, variance, direction)


def table_moments_kernel(weight_ref, first_ref, second_ref, mine_ref, other_ref, momentum_ref, variance_ref, direction_ref, squares_ref):
    weight = weight_ref[...]
    gradient = mine_ref[...].astype(f32) + other_ref[...].astype(f32)
    momentum, variance, direction = lamb_direction(weight, gradient, first_ref[...], second_ref[...])
    momentum_ref[...] = momentum
    variance_ref[...] = variance
    direction_ref[...] = direction.astype(bf)

    @pl.when(pl.program_id(0) == 0)
    def _():
        squares_ref[...] = jnp.zeros_like(squares_ref)

    squares_ref[0:1, :] += jnp.full((1, LANES), jnp.sum(weight * weight))
    squares_ref[1:2, :] += jnp.full((1, LANES), jnp.sum(direction * direction))


def table_moments(weight, first, second, mine, other, rows=16):
    features, vocab = weight.shape
    block = pl.BlockSpec((rows, vocab), lambda s: (s, 0))
    full = jax.ShapeDtypeStruct(weight.shape, f32)
    return pl.pallas_call(
        table_moments_kernel,
        grid=(features // rows,),
        in_specs=[block] * 5,
        out_specs=[block, block, block, pl.BlockSpec((8, LANES), lambda s: (0, 0))],
        out_shape=[full, full, jax.ShapeDtypeStruct(weight.shape, bf), jax.ShapeDtypeStruct((8, LANES), f32)],
        compiler_params=pltpu.CompilerParams(vmem_limit_bytes=48 * 2**20),
        name="table_moments",
    )(weight, first, second, mine, other)


def table_update_kernel(rate_ref, weight_ref, direction_ref, updated_ref):
    updated_ref[...] = weight_ref[...] - rate_ref[0] * direction_ref[...].astype(f32)


def table_update(rate, weight, direction, rows=16):
    features, vocab = weight.shape
    block = pl.BlockSpec((rows, vocab), lambda s: (s, 0))
    return pl.pallas_call(
        table_update_kernel,
        grid=(features // rows,),
        in_specs=[pl.BlockSpec(memory_space=pltpu.SMEM), block, block],
        out_specs=block,
        out_shape=jax.ShapeDtypeStruct(weight.shape, f32),
        compiler_params=pltpu.CompilerParams(vmem_limit_bytes=40 * 2**20),
        name="table_update",
    )(rate, weight, direction)


def norm_scale(stream, gain_row):
    return (
        stream * lax.rsqrt(jnp.mean(stream * stream, axis=-1, keepdims=True) + NORM_EPS) * gain_row
    )


def gelu_tanh(pre_act):
    return jax.nn.gelu(pre_act, approximate=True)


def dot(left, right, dims=((1,), (0,))):
    return lax.dot_general(left, right, (dims, ((), ())), preferred_element_type=f32)


def bucket_onehot(length):
    relative = jnp.arange(2 * length, dtype=jnp.int32) - length
    distance = jnp.abs(relative)
    far_bucket = 8 + sum(((distance >= threshold).astype(jnp.int32) for threshold in BUCKET_EDGES))
    bucket = jnp.where(distance < 8, distance, far_bucket) + jnp.where(relative > 0, 16, 0)
    return (bucket[:, None] == jnp.arange(BUCKETS)).astype(f32)


def swap_cores(value):
    size = lax.axis_size("mdl")
    return lax.ppermute(value, "mdl", [(core, (core + 1) % size) for core in range(size)])


def shards(
    token_ids,
    item_lengths,
    prefix_lengths,
    group_live,
    partner,
    embedding,
    qkv_weight,
    out_weight,
    up_weight,
    down_weight,
    bias_table,
    norm_gains,
    embedding_first,
    embedding_second,
    qkv_first,
    qkv_second,
    out_first,
    out_second,
    up_first,
    up_second,
    down_first,
    down_second,
    bias_first,
    bias_second,
    gains_first,
    gains_second,
):
    item_count, length = token_ids.shape
    features, vocab = embedding.shape
    grp_size, dat_size, mdl_size = lax.axis_size("grp"), lax.axis_size("dat"), lax.axis_size("mdl")
    group_index, dat_index, mdl_index = lax.axis_index("grp"), lax.axis_index("dat"), lax.axis_index("mdl")
    mine = item_count // mdl_size
    rows = mine * length
    pair_rows = rows // 2
    chunk = 256
    chunks = pair_rows // chunk
    group_items = item_count * dat_size
    width = features * dat_size
    first_slot = dat_index * item_count + mdl_index * mine

    facts = jnp.concatenate([token_ids, partner[:, None]], axis=1)
    group_facts = lax.all_gather(facts, "dat", axis=0, tiled=True)
    group_partner = group_facts[:, length]
    core_ids = lax.dynamic_index_in_dim(
        group_facts[:, :length].reshape(dat_size, mdl_size, 2, chunks, chunk), mdl_index, 1, keepdims=False
    ).transpose(0, 2, 1, 3)
    my_lengths = lax.dynamic_slice_in_dim(item_lengths, mdl_index * mine, mine)
    my_prefixes = lax.dynamic_slice_in_dim(prefix_lengths, mdl_index * mine, mine)

    def gathered(shard, axis=0):
        own = lax.all_gather(shard.astype(bf), "dat", axis=axis, tiled=True)
        return own, swap_cores(own)

    qkv_halves = gathered(qkv_weight.reshape(features, -1))
    out_halves = gathered(out_weight, 1)
    up_halves = gathered(up_weight)
    down_halves = gathered(down_weight)
    onehot = bucket_onehot(length)
    line_halves = [
        jnp.einsum("rb,bh->hr", onehot, table, precision=MAX_PRECISION)
        for table in (bias_table, swap_cores(bias_table))
    ]

    looked_up = gather_rows(embedding, core_ids.reshape(-1, 2, chunk))
    spread = lax.all_to_all(
        looked_up.reshape(dat_size, pair_rows, 2 * features), "dat", split_axis=0, concat_axis=0, tiled=True
    )
    embedded = (
        spread.reshape(dat_size, pair_rows, 2, features).transpose(2, 1, 0, 3).reshape(rows, width).astype(f32)
    )
    all_ids = lax.all_gather(core_ids, "grp", axis=0)

    normed_one_f, norm_one_back = jax.vjp(norm_scale, embedded, norm_gains[0])
    normed_one = normed_one_f.astype(bf)
    qkv_rows = [dot(normed_one, weight).astype(bf).reshape(mine, length, -1) for weight in qkv_halves]
    mixed, log_totals = zip(*[attend(item_qkv, lines, my_lengths) for item_qkv, lines in zip(qkv_rows, line_halves)])
    mixed_rows = [heads.reshape(rows, -1) for heads in mixed]
    after_attn = embedded + (dot(mixed_rows[0], out_halves[0]) + dot(mixed_rows[1], out_halves[1]))
    normed_two_f, norm_two_back = jax.vjp(norm_scale, after_attn, norm_gains[1])
    normed_two = normed_two_f.astype(bf)
    gate_acts, gelu_backs = zip(*[jax.vjp(gelu_tanh, dot(normed_two, weight)) for weight in up_halves])
    activated = [act.astype(bf) for act in gate_acts]
    after_ffn = after_attn + (
        dot(activated[0], down_halves[0], ((1,), (1,))) + dot(activated[1], down_halves[1], ((1,), (1,)))
    )
    positions = jnp.arange(length)
    pool_mask = (
        (positions[None, :] >= my_prefixes[:, None]) & (positions[None, :] < my_lengths[:, None])
    ).astype(f32)

    def pool_tail(stream, gain_row):
        normed_three = norm_scale(stream, gain_row).reshape(mine, length, -1)
        pooled = jnp.sum(normed_three * pool_mask[:, :, None], axis=1) / jnp.sum(pool_mask, axis=1, keepdims=True)
        return pooled * lax.rsqrt(jnp.sum(pooled * pooled, axis=1, keepdims=True) + NORM_EPS)

    vectors, tail_back = jax.vjp(pool_tail, after_ffn, norm_gains[2])

    group_vectors = lax.all_gather(vectors, ("dat", "mdl"), axis=0, tiled=True)
    live_count = jnp.sum(jnp.where(jnp.arange(grp_size) == group_index, group_live, 0))
    live_total = jnp.sum(group_live).astype(f32)
    slots = jnp.arange(group_items)
    live_rows = slots < live_count
    logits = jnp.dot(group_vectors, group_vectors.T, precision=MAX_PRECISION) / SOFTMAX_WARMTH
    allowed = live_rows[None, :] & (slots[None, :] != slots[:, None])
    masked = jnp.where(allowed, logits, MASK_FILL)
    row_top = jnp.max(masked, axis=1, keepdims=True)
    log_total = row_top[:, 0] + jnp.log(jnp.sum(jnp.exp(masked - row_top), axis=1))
    mate_hits = slots[None, :] == group_partner[:, None]
    target = jnp.sum(jnp.where(mate_hits, logits, 0.0), axis=1)
    loss_part = jnp.sum(jnp.where(live_rows, log_total - target, 0.0))
    row_weight = jnp.where(live_rows, 1.0 / live_total, 0.0)
    grad_logits = (
        row_weight[:, None] * (jnp.exp(masked - log_total[:, None]) - mate_hits.astype(f32)) / SOFTMAX_WARMTH
    )
    my_pulls = lax.dynamic_slice_in_dim(grad_logits + grad_logits.T, first_slot, mine)
    grad_vectors = jnp.dot(my_pulls, group_vectors, precision=MAX_PRECISION)

    def reduced(own, other):
        total = (own + swap_cores(other.astype(bf)).astype(f32)).astype(bf)
        part = lax.psum_scatter(total, "dat", scatter_dimension=0, tiled=True)
        return lax.psum(part, "grp").astype(f32)

    tn = ((0,), (0,))
    nt = ((1,), (1,))
    grad_after_ffn, grad_gain_three = tail_back(grad_vectors)
    grad_ffn = grad_after_ffn.astype(bf)
    grad_down = reduced(*[dot(grad_ffn, act, tn) for act in activated])
    grad_gates = [
        back(dot(grad_ffn, weight))[0].astype(bf) for back, weight in zip(gelu_backs, down_halves)
    ]
    grad_up = reduced(*[dot(normed_two, grad_gate, tn) for grad_gate in grad_gates])
    two_back = dot(grad_gates[0], up_halves[0], nt) + dot(grad_gates[1], up_halves[1], nt)
    grad_after_attn, grad_gain_two = norm_two_back(two_back)
    grad_after_attn = grad_after_attn + grad_after_ffn
    grad_attn = grad_after_attn.astype(bf)
    grad_out = reduced(*[dot(grad_attn, heads, tn) for heads in mixed_rows]).T
    grad_mixed = [dot(grad_attn, weight, nt).astype(bf).reshape(mine, length, -1) for weight in out_halves]
    grad_qkv_items, grad_lines = zip(
        *[
            attend_back(item_qkv, lines, my_lengths, stats, grad)
            for item_qkv, lines, stats, grad in zip(qkv_rows, line_halves, log_totals, grad_mixed)
        ]
    )
    grad_qkv_rows = [grad.reshape(rows, -1) for grad in grad_qkv_items]
    one_back = dot(grad_qkv_rows[0], qkv_halves[0], nt) + dot(grad_qkv_rows[1], qkv_halves[1], nt)
    grad_embedded, grad_gain_one = norm_one_back(one_back)
    grad_embedded = grad_embedded + grad_after_attn
    grad_qkv = reduced(*[dot(normed_one, grad, tn) for grad in grad_qkv_rows]).reshape(qkv_weight.shape)

    outgoing = grad_embedded.astype(bf).reshape(2, pair_rows, dat_size, features).transpose(2, 1, 0, 3)
    own_rows = lax.all_to_all(
        outgoing.reshape(dat_size, pair_rows, 2 * features), "dat", split_axis=0, concat_axis=0, tiled=True
    ).reshape(dat_size * pair_rows, 2 * features)
    upward = [(group, group + 1) for group in range(grp_size - 1)]
    downward = [(group + 1, group) for group in range(grp_size - 1)]
    from_below, from_above = [own_rows], [own_rows]
    for _ in range(grp_size - 1):
        from_below.append(lax.ppermute(from_below[-1], "grp", upward))
        from_above.append(lax.ppermute(from_above[-1], "grp", downward))
    pieces, piece_ids = [own_rows], [core_ids]
    for hop in range(1, grp_size):
        pieces.append(jnp.where(group_index >= hop, from_below[hop], from_above[grp_size - hop]))
        piece_ids.append(lax.dynamic_index_in_dim(all_ids, (group_index - hop) % grp_size, 0, keepdims=False))
    own_table = scatter_rows(
        jnp.concatenate(pieces, axis=0), jnp.stack(piece_ids).reshape(-1, 2, chunk), vocab, features
    )
    other_table = swap_cores(own_table)

    grad_bias_own, grad_bias_other = [
        jnp.einsum("rb,hr->bh", onehot, grad, precision=MAX_PRECISION) for grad in grad_lines
    ]
    grad_bias_all = jnp.where(
        mdl_index == 0,
        jnp.concatenate([grad_bias_own, grad_bias_other], axis=1),
        jnp.concatenate([grad_bias_other, grad_bias_own], axis=1),
    )
    leader = ((dat_index == 0) & (mdl_index == 0)).astype(f32)
    small = jnp.concatenate(
        [
            jnp.stack([grad_gain_one, grad_gain_two, grad_gain_three]).reshape(-1),
            grad_bias_all.reshape(-1),
            (loss_part * leader).reshape(1),
        ]
    )
    small = lax.psum(small, ("grp", "dat", "mdl"))
    grad_gains = small[: 3 * width].reshape(3, width)
    grad_bias = lax.dynamic_slice_in_dim(
        small[3 * width : -1].reshape(BUCKETS, -1), mdl_index * bias_table.shape[1], bias_table.shape[1], axis=1
    )
    loss_total = small[-1]

    weights = (qkv_weight, out_weight, up_weight, down_weight, bias_table, norm_gains)
    gradients = (grad_qkv, grad_out, grad_up, grad_down, grad_bias, grad_gains)
    moments = (
        (qkv_first, qkv_second),
        (out_first, out_second),
        (up_first, up_second),
        (down_first, down_second),
        (bias_first, bias_second),
        (gains_first, gains_second),
    )
    results = [
        lamb_direction(weight, gradient, states[0], states[1])
        for weight, gradient, states in zip(weights, gradients, moments)
    ]
    table_momentum, table_variance, table_direction, table_squares = table_moments(
        embedding, embedding_first, embedding_second, own_table, other_table
    )
    first_mdl = (mdl_index == 0).astype(f32)
    first_dat = (dat_index == 0).astype(f32)
    holder_mask = [1.0, 1.0, 1.0, 1.0, first_dat]
    square_rows = [table_squares[:2, 0] * first_mdl] + [
        jnp.stack(
            [
                jnp.sum(weights[position] * weights[position]),
                jnp.sum(results[position][2] * results[position][2]),
            ]
        )
        * holder_mask[position]
        for position in range(5)
    ]
    gain_rows = jnp.stack(
        [jnp.sum(norm_gains * norm_gains, axis=1), jnp.sum(results[5][2] * results[5][2], axis=1)],
        axis=1,
    ) * (first_mdl * first_dat)
    square_table = jnp.concatenate([jnp.stack(square_rows), gain_rows], axis=0)
    matrix_norms = jnp.sqrt(lax.psum(square_table, ("dat", "mdl")))
    rates = LEARN_RATE * matrix_norms[:, 0] / matrix_norms[:, 1]
    updated = [weights[position] - rates[position + 1] * results[position][2] for position in range(5)]
    updated.append(norm_gains - rates[6:, None] * results[5][2])
    outputs = [
        jnp.stack([loss_total, live_total]),
        matrix_norms,
        table_momentum,
        table_variance,
        table_update(rates[:1], embedding, table_direction),
    ]
    for position in range(6):
        outputs.extend([results[position][0], results[position][1], updated[position]])
    return tuple(outputs)


def solution(mesh):
    state = [
        P("dat", None),
        P("dat", None, "mdl"),
        P("mdl", "dat"),
        P("dat", "mdl"),
        P("dat", "mdl"),
        P(None, "mdl"),
        P(),
    ]
    placed = [P(("grp", "dat"), None), P(("grp", "dat")), P(("grp", "dat")), P(), P(("grp", "dat"))]
    placed += state + [spec for spec in state for _ in range(2)]
    return jax.shard_map(
        shards,
        mesh=mesh,
        in_specs=tuple(placed),
        out_specs=(P(), P(), *[spec for spec in state for _ in range(3)]),
        check_vma=False,
    )
```

time: 2480 us -> 888 us (0.36)
  waiting for transfers between devices: 1310 us -> 180 us
  local copies, waits for them, and re-layouts: 415 us -> 50.7 us
  other arithmetic: 375 us -> 67.1 us
  Pallas kernels: 0 us -> 287 us
  matrix products: 203 us -> 106 us
  starting transfers between devices: 10.1 us -> 51.1 us
    psum x5 -> x1, waiting for transfers between devices: 1100 us -> 31.2 us  [reduced(): return lax.psum(part, 'grp').astype(f32)]
    pallas_call x0 -> x8, Pallas kernels: none -> 287 us  [the longest x1 95.3 us: scatter_rows(): pl.pallas_call(functools.partial(scatter_kernel, features, tiles, steps,...]
    unnamed x108 -> x151, local copies, waits for them, and re-layouts: 192 us -> 13.7 us
    dot_general x45 -> x30, matrix products: 203 us -> 106 us  [the longest x24 103 us: dot(): lax.dot_general(left, right, (dims, ((), ())), preferred_element_type=f32)]
    reduce_scatter x4, waiting for transfers between devices: 124 us -> 37.1 us  [reduced(): part = lax.psum_scatter(total, 'dat', scatter_dimension=0, tiled=True)]
    ppermute x0 -> x16, waiting for transfers between devices: none -> 74.3 us  [the longest x3 38.4 us: shards(): from_above.append(lax.ppermute(from_above[-1], 'grp', downward))]
    reduce_sum x8 -> x3, other arithmetic: 70.4 us -> 1.44 us  [the longest x1 0.77 us: shards(): jnp.sum(results[5][2] * results[5][2], axis=1)]
    all_gather x3, waiting for transfers between devices: 59.4 us -> 0.02 us  [gathered(): own = lax.all_gather(shard.astype(bf), 'dat', axis=axis, tiled=True)]
  transfers between devices with their start and end apart: 14 -> 26, of which waited for: 10 -> 9; matrix products, arithmetic and copies ran while one was open for 18% -> 17% of each run, Pallas kernels for 0% -> 21%
where the time goes in v1:
time: 888 us; the launch traced here: 877 us
  Pallas kernels  287 us (32%)
  waiting for transfers between devices  180 us (20%)
  blocking collectives  118 us (13%)
  matrix products  106 us (12%)
  other arithmetic  67.1 us (8%)
  starting transfers between devices  51.1 us (6%)
  local copies, waits for them, and re-layouts  50.7 us (6%)
  between operations  17.3 us (2%)
    dot_general x24, matrix products, dot(): lax.dot_general(left, right, (dims, ((), ())), preferred_element_type=f32)  103 us
    pallas_call x1, Pallas kernels, scatter_rows(): pl.pallas_call(functools.partial(scatter_kernel, features, tiles, steps,...  95.3 us
    pallas_call x1, Pallas kernels, table_moments(): pl.pallas_call(table_moments_kernel, grid=(features // rows,), in_specs=[...  57.3 us
    pallas_call x2, Pallas kernels, attend_back(): pl.pallas_call(functools.partial(attend_back_kernel, pairs, HEAD ** (-0.5...  47.3 us
    psum x1, blocking collectives, shards(): small = lax.psum(small, ('grp', 'dat', 'mdl'))  41.9 us
    pallas_call x2, Pallas kernels, attend(): pl.pallas_call(functools.partial(attend_kernel, pairs, HEAD ** (-0.5)), i...  39.3 us
    ppermute x3, waiting for transfers between devices, shards(): from_above.append(lax.ppermute(from_above[-1], 'grp', downward))  38.4 us
    reduce_scatter x4, waiting for transfers between devices, reduced(): part = lax.psum_scatter(total, 'dat', scatter_dimension=0, tiled=True)  37.1 us
  transfers between devices with their start and end apart: 26, of which 9 were waited for; matrix products, arithmetic and copies ran while one was open for 17% of the time, Pallas kernels for 21%

profile of v1, /device:TPU:17, one launch (start us, length us, event | category | flops | bytes accessed | tf_op | source)
XLA Modules:
  0.0 877.0 jit_solution(17207121926671133119)
XLA Ops:
  11.2 11.5 %all_gather.24 = bf16[384,768]{0,1:T(8,128)(2,1)} all-gather(bf16[384,192]{0,1:T(8,128)(2,1)S(1)} %convert_element_type.261), channel_id=1, replica_groups=mesh['grp'=4,'dat'=4,'mdl'=2] {'dat'}, dimensions={1}, use_global_device_ids=true | all-gather | bytes 737280 | tf_op jit(solution)/shard_map/all_gather | solution.py:433
  25.5 6.4 all-gather.1
  32.5 26.4 %gather_rows.1 = bf16[2048,384]{1,0:T(8,128)(2,1)} custom-call(f32[192,32128]{1,0:T(8,128)} %weight_ref.3, s32[8,2,256]{2,1,0:T(2,128)} %bitcast.200), custom_call_target="tpu_custom_call" | custom-call | tf_op jit(solution)/shard_map/gather_rows/pallas_call | solution.py:209
  71.9 21.2 %all-to-all-done = bf16[4,512,384]{1,2,0:T(8,128)(2,1)S(1)} async-done(((bf16[4,512,384]{1,2,0:T(8,128)(2,1)}), bf16[4,512,384]{1,2,0:T(8,128)(2,1)S(1)}, u32[]{:S(2)}, u32[]{:S(2)}) %all-to-all-start) | async-done | bytes 1572896 | tf_op jit(solution)/shard_map/all_to_all | solution.py:447
  109.6 5.7 reshape.431
  119.5 19.4 %attend.2 = (bf16[2,512,384]{2,1,0:T(8,128)(2,1)S(1)}, f32[2,512,384]{2,1,0:T(8,128)S(1)}) custom-call(s32[2]{0:T(128)S(1)} %dynamic_slice.27.lens_ref, f32[6,1024]{1,0:T(8,128)S(1)} %convolution_bitcast_fusion.1.line_ref, bf16[2,512,1152]{2,1,0:T(8,128)(2,1)S(1)} %bitcast.174), custom_call_target="tpu_custom_call" | custom-call | flops 1610612736 | bytes 4718592 | tf_op jit(solution)/shard_map/attend/pallas_call | solution.py:93
  149.4 19.8 %attend.3 = (bf16[2,512,384]{2,1,0:T(8,128)(2,1)S(1)}, f32[2,512,384]{2,1,0:T(8,128)S(1)}) custom-call(s32[2]{0:T(128)S(1)} %dynamic_slice.27.lens_ref, f32[6,1024]{1,0:T(8,128)S(1)} %convolution_bitcast_fusion.line_ref, bf16[2,512,1152]{2,1,0:T(8,128)(2,1)S(1)} %bitcast.176), custom_call_target="tpu_custom_call" | custom-call | flops 1610612736 | bytes 4718592 | tf_op jit(solution)/shard_map/attend/pallas_call | solution.py:93
  183.9 7.4 multiply_reduce_fusion.5
  193.8 9.2 %all-gather.2 = f32[8,2,768]{2,1,0:T(2,128)S(1)} all-gather(f32[1,2,768]{2,1,0:T(2,128)S(1)} %multiply_bitcast_fusion), channel_id=1, replica_groups=mesh['grp'=4,'dat'=4,'mdl'=2] {'dat','mdl'}, dimensions={0}, use_global_device_ids=true | all-gather | bytes 55296 | tf_op jit(solution)/shard_map/all_gather | solution.py:480
  209.2 9.2 %fusion.13 = bf16[1024,1536]{1,0:T(8,128)(2,1)S(1)} fusion(f32[1024,1536]{1,0:T(8,128)} %copy-done.68, bf16[1024,768]{1,0:T(8,128)(2,1)S(1)} %fusion.23, bf16[768,1536]{1,0:T(8,128)(2,1)} %collective-permute-done.4), kind=kOutput, calls=%fused_computation.17 | convolution fusion | flops 2447376384 | bytes 13369344 | tf_op jit(solution)/shard_map/dot_general | solution.py:366
  218.5 6.3 fusion.6
  238.6 23.6 %attend_back.3 = (bf16[2,512,1152]{2,1,0:T(8,128)(2,1)S(1)}, f32[6,1024]{1,0:T(8,128)S(1)}) custom-call(s32[2]{0:T(128)S(1)} %dynamic_slice.27.lens_ref, f32[6,1024]{1,0:T(8,128)S(1)} %convolution_bitcast_fusion.line_ref, bf16[2,512,1152]{2,1,0:T(8,128)(2,1)S(1)} %bitcast.177, f32[2,512,384]{2,1,0:T(8,128)S(1)} %copy-done.7, bf16[2,512,384]{2,1,0:T(8,128)(2,1)S(1)} %bitcast.183), custom_call_target="tpu_custom_call" | custom-call | flops 4026531840 | bytes 7864320 | tf_op jit(solution)/shard_map/attend_back/pallas_call | solution.py:158
  265.8 23.8 %attend_back.2 = (bf16[2,512,1152]{2,1,0:T(8,128)(2,1)S(1)}, f32[6,1024]{1,0:T(8,128)S(1)}) custom-call(s32[2]{0:T(128)S(1)} %dynamic_slice.27.lens_ref, f32[6,1024]{1,0:T(8,128)S(1)} %convolution_bitcast_fusion.1.line_ref, bf16[2,512,1152]{2,1,0:T(8,128)(2,1)S(1)} %bitcast.175, f32[2,512,384]{2,1,0:T(8,128)S(1)} %get-tuple-element.35.lse_ref, ...), custom_call_target="tpu_custom_call" | custom-call | flops 4026531840 | bytes 7864320 | tf_op jit(solution)/shard_map/attend_back/pallas_call | solution.py:158
  316.3 16.0 %all-to-all-done.1 = bf16[4,512,384]{1,2,0:T(8,128)(2,1)} async-done(((bf16[4,512,384]{1,2,0:T(8,128)(2,1)}), bf16[4,512,384]{1,2,0:T(8,128)(2,1)}, u32[]{:S(2)}, u32[]{:S(2)}) %all-to-all-start.1) | async-done | bytes 1572896 | tf_op jit(solution)/shard_map/all_to_all | solution.py:533
  340.9 6.4 convolution_convert_fusion.3
  350.5 19.1 %collective-permute-done.6 = bf16[2048,384]{1,0:T(8,128)(2,1)} collective-permute-done((bf16[2048,384]{1,0:T(8,128)(2,1)S(1)}, bf16[2048,384]{1,0:T(8,128)(2,1)}, u32[]{:S(2)}, u32[]{:S(2)}) %collective-permute-start.6) | collective-permute-done | bytes 1572896 | tf_op jit(solution)/shard_map/ppermute | solution.py:541
  384.8 19.3 %collective-permute-done.7 = bf16[2048,384]{1,0:T(8,128)(2,1)} collective-permute-done((bf16[2048,384]{1,0:T(8,128)(2,1)}, bf16[2048,384]{1,0:T(8,128)(2,1)}, u32[]{:S(2)}, u32[]{:S(2)}) %collective-permute-start.7) | collective-permute-done | bytes 1572896 | tf_op jit(solution)/shard_map/ppermute | solution.py:541
  406.7 36.6 %all-gather = s32[16,2,2,256]{3,2,1,0:T(2,128)S(1)} all-gather(s32[4,2,2,256]{3,2,1,0:T(2,128)S(1)} %bitcast.201), channel_id=2, replica_groups=mesh['grp'=4,'dat'=4,'mdl'=2] {'grp'}, dimensions={0}, use_global_device_ids=true | all-gather | bytes 81920 | tf_op jit(solution)/shard_map/all_gather | solution.py:453
  445.9 7.2 add_convert_fusion.1
  456.6 18.2 %collective-permute-done.10 = bf16[2048,384]{1,0:T(8,128)(2,1)} collective-permute-done((bf16[2048,384]{1,0:T(8,128)(2,1)}, bf16[2048,384]{1,0:T(8,128)(2,1)}, u32[]{:S(2)}, u32[]{:S(2)}) %collective-permute-start.10) | collective-permute-done | bytes 1572896 | tf_op jit(solution)/shard_map/ppermute | solution.py:540
  479.4 95.3 %scatter_rows.1.mine_ref = bf16[192,32128]{1,0:T(8,128)(2,1)} custom-call(s32[32,2,256]{2,1,0:T(2,128)} %bitcast.197, s32[32,2,256]{2,1,0:T(2,128)} %bitcast.198, bf16[8192,384]{1,0:T(8,128)(2,1)} %pad_maximum_fusion.rows_ref), custom_call_target="tpu_custom_call" | custom-call | tf_op jit(solution)/shard_map/scatter_rows/pallas_call | solution.py:277
  574.7 8.3 collective-permute-start.11
  583.0 5.6 convolution_convert_fusion.2
  588.7 16.1 %collective-permute-done.15 = bf16[768,1536]{1,0:T(8,128)(2,1)S(1)} collective-permute-done((bf16[768,1536]{1,0:T(8,128)(2,1)S(1)}, bf16[768,1536]{1,0:T(8,128)(2,1)S(1)}, u32[]{:S(2)}, u32[]{:S(2)}) %collective-permute-start.15) | collective-permute-done | bytes 2359328 | tf_op jit(solution)/shard_map/ppermute | solution.py:379
  604.8 7.3 add_convert_fusion
  614.3 37.1 %reduce-scatter.11.cloned.1.call-done = bf16[192,1536]{1,0:T(8,128)(2,1)} async-done(((bf16[768,1536]{1,0:T(8,128)(2,1)}), bf16[192,1536]{1,0:T(8,128)(2,1)}) %reduce-scatter.11.cloned.1.call-update) | async-done | bytes 589840 | tf_op jit(solution)/shard_map/reduce_scatter | solution.py:502
  653.2 41.9 %psum.42 = f32[2689]{0:T(1024)S(1)} all-reduce(f32[2689]{0:T(1024)S(1)} %pad_maximum_fusion.2), channel_id=1, replica_groups=mesh['grp'=4,'dat'=4,'mdl'=2] {'grp','dat','mdl'}, use_global_device_ids=true, to_apply=%region_18.19 | all-reduce | flops 2689 | bytes 21512 | tf_op jit(solution)/shard_map/psum | solution.py:567
  700.3 31.2 %all-reduce.3.cloned.1.call-done = (bf16[192,3,384]{2,0,1:T(8,128)(2,1)}, bf16[384,192]{0,1:T(8,128)(2,1)}, bf16[192,1536]{1,0:T(8,128)(2,1)}, bf16[192,1536]{1,0:T(8,128)(2,1)}) async-done(((bf16[192,3,384]{2,0,1:T(8,128)(2,1)}, bf16[384,192]{0,1:T(8,128)(2,1)}, bf16[192,1536]{1,0:T(8,128)(2,1)}, bf16[192,1536]{1,0:T(8,128)(2,1)}), (bf16[192,3,384]{2,0,1:T(8,128)(2,1)}, bf16[384,192]{0,1:T(8,128)(2,1)}, ...) | async-done | bytes 1769488 | tf_op jit(solution)/shard_map/psum | solution.py:503
  744.9 7.1 multiply_reduce_fusion.9
  758.3 57.3 %table_moments.1 = (f32[192,32128]{1,0:T(8,128)}, f32[192,32128]{1,0:T(8,128)}, bf16[192,32128]{1,0:T(8,128)(2,1)}, f32[8,128]{1,0:T(8,128)S(1)}) custom-call(f32[192,32128]{1,0:T(8,128)} %weight_ref.3, f32[192,32128]{1,0:T(8,128)} %first_ref.1, f32[192,32128]{1,0:T(8,128)} %second_ref.1, bf16[192,32128]{1,0:T(8,128)(2,1)} %scatter_rows.1.mine_ref, ...), custom_call_target="tpu_custom_call" | custom-call | tf_op jit(solution)/shard_map/table_moments/pallas_call | solution.py:326
  818.8 12.5 %psum.47 = f32[9,2]{0,1:T(2,128)} all-reduce(f32[9,2]{0,1:T(2,128)} %concatenate.30), channel_id=1, replica_groups=mesh['grp'=4,'dat'=4,'mdl'=2] {'dat','mdl'}, use_global_device_ids=true, to_apply=%region_40.41 | all-reduce | flops 18 | bytes 144 | tf_op jit(solution)/shard_map/psum | solution.py:609
  838.6 21.4 %table_update.1 = f32[192,32128]{1,0:T(8,128)} custom-call(f32[1]{0:T(128)} %bitcast.51.rate_ref, f32[192,32128]{1,0:T(8,128)} %weight_ref.3, bf16[192,32128]{1,0:T(8,128)(2,1)S(1)} %copy-done), custom_call_target="tpu_custom_call" | custom-call | tf_op jit(solution)/shard_map/table_update/pallas_call | solution.py:344
  (331 shorter events, 206.1 us)
Async XLA Ops:
  7.2 86.2 %all-gather.7.cloned.1.call-start = ((), (), s32[]{:S(2)}) async-start(), calls=%async_computation.6 | async-start | bytes 2211840 | tf_op jit(solution)/shard_map/all_gather | solution.py:433
  9.4 134.6 %all-gather.11.cloned.1.call-start = ((), (), s32[]{:S(2)}) async-start(), calls=%async_computation.8 | async-start | bytes 2949120 | tf_op jit(solution)/shard_map/all_gather | solution.py:433
  10.4 61.0 %collective-permute-start = (f32[32,6]{0,1:T(8,128)S(1)}, f32[32,6]{0,1:T(8,128)S(1)}, u32[]{:S(2)}, u32[]{:S(2)}) collective-permute-start(f32[32,6]{0,1:T(8,128)S(1)} %copy-done.39), channel_id=1, source_target_pairs={{0,1},{1,0},{2,3},{3,2},{4,5},{5,4},{6,7},{7,6},{8,9},{9,8},{10,11... | collective-permute-start | bytes 2312 | tf_op jit(solution)/shard_map/ppermute | solution.py:379
  22.7 146.6 %collective-permute-start.2 = (bf16[384,768]{0,1:T(8,128)(2,1)}, bf16[384,768]{0,1:T(8,128)(2,1)}, u32[]{:S(2)}, u32[]{:S(2)}) collective-permute-start(bf16[384,768]{0,1:T(8,128)(2,1)} %all_gather.24), channel_id=1, source_target_pairs={{0,1},{1,0},{2,3},{3,2},{4,5},{5,4},{6,7},{7,6},{8,9},{9,8},{10,11... | collective-permute-start | bytes 1769480 | tf_op jit(solution)/shard_map/ppermute | solution.py:379
  61.6 31.5 %all-to-all-start = ((bf16[4,512,384]{1,2,0:T(8,128)(2,1)}), bf16[4,512,384]{1,2,0:T(8,128)(2,1)S(1)}, u32[]{:S(2)}, u32[]{:S(2)}) async-start(bf16[4,512,384]{1,2,0:T(8,128)(2,1)} %copy.133), calls=%async_computation | async-start | bytes 3145728 | tf_op jit(solution)/shard_map/all_to_all | solution.py:447
  65.3 78.8 %all-gather.9.cloned.1.call-start = ((), (), s32[]{:S(2)}) async-start(), calls=%async_computation.7 | async-start | bytes 2949120 | tf_op jit(solution)/shard_map/all_gather | solution.py:433
  93.5 51.1 %collective-permute-start.1 = (bf16[768,1152]{1,0:T(8,128)(2,1)}, bf16[768,1152]{1,0:T(8,128)(2,1)}, u32[]{:S(2)}, u32[]{:S(2)}) collective-permute-start(bf16[768,1152]{1,0:T(8,128)(2,1)} %all-gather.7.cloned.1.call-done), channel_id=1, source_target_pairs={{0,1},{1,0},{2,3},{3,2},{4,5},{5,4},{6,7},{7,6},{8,9},{9,8},{10,11... | collective-permute-start | bytes 5308424 | tf_op jit(solution)/shard_map/ppermute | solution.py:379
  144.0 39.9 %collective-permute-start.4 = (bf16[768,1536]{1,0:T(8,128)(2,1)}, bf16[768,1536]{1,0:T(8,128)(2,1)}, u32[]{:S(2)}, u32[]{:S(2)}) collective-permute-start(bf16[768,1536]{1,0:T(8,128)(2,1)} %all-gather.11.cloned.1.call-done), channel_id=1, source_target_pairs={{0,1},{1,0},{2,3},{3,2},{4,5},{5,4},{6,7},{7,6},{8,9},{9,8},{10,11... | collective-permute-start | bytes 7077896 | tf_op jit(solution)/shard_map/ppermute | solution.py:379
  144.0 37.2 %collective-permute-start.3 = (bf16[768,1536]{1,0:T(8,128)(2,1)}, bf16[768,1536]{1,0:T(8,128)(2,1)S(1)}, u32[]{:S(2)}, u32[]{:S(2)}) collective-permute-start(bf16[768,1536]{1,0:T(8,128)(2,1)} %all-gather.9.cloned.1.call-done), channel_id=1, source_target_pairs={{0,1},{1,0},{2,3},{3,2},{4,5},{5,4},{6,7},{7,6},{8,9},{9,8},{10,11... | collective-permute-start | bytes 7077896 | tf_op jit(solution)/shard_map/ppermute | solution.py:379
  265.6 45.0 %collective-permute-start.12 = (bf16[768,1152]{1,0:T(8,128)(2,1)}, bf16[768,1152]{1,0:T(8,128)(2,1)}, u32[]{:S(2)}, u32[]{:S(2)}) collective-permute-start(bf16[768,1152]{1,0:T(8,128)(2,1)} %convolution_convert_fusion.4), channel_id=1, source_target_pairs={{0,1},{1,0},{2,3},{3,2},{4,5},{5,4},{6,7},{7,6},{8,9},{9,8},{10,11... | collective-permute-start | bytes 5308424 | tf_op jit(solution)/shard_map/ppermute | solution.py:379
  306.1 26.3 %all-to-all-start.1 = ((bf16[4,512,384]{1,2,0:T(8,128)(2,1)}), bf16[4,512,384]{1,2,0:T(8,128)(2,1)}, u32[]{:S(2)}, u32[]{:S(2)}) async-start(bf16[4,512,384]{1,2,0:T(8,128)(2,1)} %bitcast.31), calls=%async_computation.1 | async-start | bytes 3145728 | tf_op jit(solution)/shard_map/all_to_all | solution.py:533
  310.4 301.9 %reduce-scatter.5.cloned.1.call-start = ((), (), s32[]{:S(2)}) async-start(), calls=%async_computation.9 | async-start | bytes 2211840 | tf_op jit(solution)/shard_map/reduce_scatter | solution.py:502
  316.3 298.0 %reduce-scatter.7.cloned.1.call-start = ((), (), s32[]{:S(2)}) async-start(), calls=%async_computation.10 | async-start | bytes 737280 | tf_op jit(solution)/shard_map/reduce_scatter | solution.py:502
  334.2 35.4 %collective-permute-start.6 = (bf16[2048,384]{1,0:T(8,128)(2,1)S(1)}, bf16[2048,384]{1,0:T(8,128)(2,1)}, u32[]{:S(2)}, u32[]{:S(2)}) collective-permute-start(bf16[2048,384]{1,0:T(8,128)(2,1)S(1)} %bitcast.187), channel_id=1, source_target_pairs={{8,0},{16,8},{24,16},{9,1},{17,9},{25,17},{10,2},{18,10},{26,18},{... | collective-permute-start | bytes 4718600 | tf_op jit(solution)/shard_map/ppermute | solution.py:541
  336.3 35.5 %collective-permute-start.5 = (bf16[2048,384]{1,0:T(8,128)(2,1)S(1)}, bf16[2048,384]{1,0:T(8,128)(2,1)}, u32[]{:S(2)}, u32[]{:S(2)}) collective-permute-start(bf16[2048,384]{1,0:T(8,128)(2,1)S(1)} %bitcast.188), channel_id=1, source_target_pairs={{0,8},{8,16},{16,24},{1,9},{9,17},{17,25},{2,10},{10,18},{18,26},{... | collective-permute-start | bytes 4718600 | tf_op jit(solution)/shard_map/ppermute | solution.py:540
  347.3 98.6 %collective-permute-start.14 = (bf16[768,1536]{1,0:T(8,128)(2,1)}, bf16[768,1536]{1,0:T(8,128)(2,1)}, u32[]{:S(2)}, u32[]{:S(2)}) collective-permute-start(bf16[768,1536]{1,0:T(8,128)(2,1)} %convolution_convert_fusion.3), channel_id=1, source_target_pairs={{0,1},{1,0},{2,3},{3,2},{4,5},{5,4},{6,7},{7,6},{8,9},{9,8},{10,11... | collective-permute-start | bytes 7077896 | tf_op jit(solution)/shard_map/ppermute | solution.py:379
  369.6 34.5 %collective-permute-start.7 = (bf16[2048,384]{1,0:T(8,128)(2,1)}, bf16[2048,384]{1,0:T(8,128)(2,1)}, u32[]{:S(2)}, u32[]{:S(2)}) collective-permute-start(bf16[2048,384]{1,0:T(8,128)(2,1)} %collective-permute-done.6), channel_id=1, source_target_pairs={{8,0},{16,8},{24,16},{9,1},{17,9},{25,17},{10,2},{18,10},{26,18},{... | collective-permute-start | bytes 4718600 | tf_op jit(solution)/shard_map/ppermute | solution.py:541
  371.8 72.1 %collective-permute-start.9 = (bf16[2048,384]{1,0:T(8,128)(2,1)}, bf16[2048,384]{1,0:T(8,128)(2,1)}, u32[]{:S(2)}, u32[]{:S(2)}) collective-permute-start(bf16[2048,384]{1,0:T(8,128)(2,1)} %collective-permute-done.5), channel_id=1, source_target_pairs={{0,8},{8,16},{16,24},{1,9},{9,17},{17,25},{2,10},{10,18},{18,26},{... | collective-permute-start | bytes 4718600 | tf_op jit(solution)/shard_map/ppermute | solution.py:540
  377.1 5.8 collective-permute-start.13
  384.8 229.5 %reduce-scatter.9.cloned.1.call-start = ((), (), s32[]{:S(2)}) async-start(), calls=%async_computation.11 | async-start | bytes 2949120 | tf_op jit(solution)/shard_map/reduce_scatter | solution.py:502
  404.1 50.8 %collective-permute-start.8 = (bf16[2048,384]{1,0:T(8,128)(2,1)}, bf16[2048,384]{1,0:T(8,128)(2,1)S(1)}, u32[]{:S(2)}, u32[]{:S(2)}) collective-permute-start(bf16[2048,384]{1,0:T(8,128)(2,1)} %collective-permute-done.7), channel_id=1, source_target_pairs={{8,0},{16,8},{24,16},{9,1},{17,9},{25,17},{10,2},{18,10},{26,18},{... | collective-permute-start | bytes 4718600 | tf_op jit(solution)/shard_map/ppermute | solution.py:541
  443.9 30.8 %collective-permute-start.10 = (bf16[2048,384]{1,0:T(8,128)(2,1)}, bf16[2048,384]{1,0:T(8,128)(2,1)}, u32[]{:S(2)}, u32[]{:S(2)}) collective-permute-start(bf16[2048,384]{1,0:T(8,128)(2,1)} %collective-permute-done.9), channel_id=1, source_target_pairs={{0,8},{8,16},{16,24},{1,9},{9,17},{17,25},{2,10},{10,18},{18,26},{... | collective-permute-start | bytes 4718600 | tf_op jit(solution)/shard_map/ppermute | solution.py:540
  453.1 198.3 %reduce-scatter.11.cloned.1.call-start = ((), (), s32[]{:S(2)}) async-start(), calls=%async_computation.12 | async-start | bytes 2949120 | tf_op jit(solution)/shard_map/reduce_scatter | solution.py:502
  479.4 103.6 %copy-start.28 = (bf16[1024,768]{1,0:T(8,128)(2,1)S(1)}, bf16[1024,768]{1,0:T(8,128)(2,1)}, u32[]{:S(2)}) copy-start(bf16[1024,768]{1,0:T(8,128)(2,1)} %copy-done.27) | copy-start | bytes 4718596
  574.7 183.6 %collective-permute-start.11 = (bf16[192,32128]{1,0:T(8,128)(2,1)}, bf16[192,32128]{1,0:T(8,128)(2,1)}, u32[]{:S(2)}, u32[]{:S(2)}) collective-permute-start(bf16[192,32128]{1,0:T(8,128)(2,1)} %scatter_rows.1.mine_ref), channel_id=1, source_target_pairs={{0,1},{1,0},{2,3},{3,2},{4,5},{5,4},{6,7},{7,6},{8,9},{9,8},{10,11... | collective-permute-start | bytes 37011464 | tf_op jit(solution)/shard_map/ppermute | solution.py:379
  588.6 16.2 %collective-permute-start.15 = (bf16[768,1536]{1,0:T(8,128)(2,1)S(1)}, bf16[768,1536]{1,0:T(8,128)(2,1)S(1)}, u32[]{:S(2)}, u32[]{:S(2)}) collective-permute-start(bf16[768,1536]{1,0:T(8,128)(2,1)S(1)} %convolution_convert_fusion.2), channel_id=1, source_target_pairs={{0,1},{1,0},{2,3},{3,2},{4,5},{5,4},{6,7},{7,6},{8,9},{9,8},{10,11... | collective-permute-start | bytes 7077896 | tf_op jit(solution)/shard_map/ppermute | solution.py:379
  612.1 86.8 %copy-start.38 = (f32[3,768]{1,0:T(4,128)S(1)}, f32[3,768]{1,0:T(4,128)}, u32[]{:S(2)}) copy-start(f32[3,768]{1,0:T(4,128)} %param.37) | copy-start | bytes 27652
  612.2 86.8 %copy-start.44 = (f32[3,768]{1,0:T(4,128)S(1)}, f32[3,768]{1,0:T(4,128)}, u32[]{:S(2)}) copy-start(f32[3,768]{1,0:T(4,128)} %param.50) | copy-start | bytes 27652
  612.2 119.3 %copy-start.26 = (f32[384,192]{0,1:T(8,128)S(1)}, f32[384,192]{0,1:T(8,128)}, u32[]{:S(2)}) copy-start(f32[384,192]{0,1:T(8,128)} %param.33) | copy-start | bytes 884740
  612.2 125.4 %copy-start.18 = (f32[192,3,384]{2,0,1:T(8,128)S(1)}, f32[192,3,384]{2,0,1:T(8,128)}, u32[]{:S(2)}) copy-start(f32[192,3,384]{2,0,1:T(8,128)} %param.32) | copy-start | bytes 2654212
  612.2 119.2 %all-reduce.3.cloned.1.call-start = ((), (), s32[]{:S(2)}) async-start(), calls=%async_computation.13 | async-start | bytes 3538944 | tf_op jit(solution)/shard_map/psum | solution.py:503
  697.1 162.9 %copy-start.42 = (f32[32,6]{0,1:T(8,128)}, f32[32,6]{0,1:T(8,128)S(1)}, u32[]{:S(2)}) copy-start(f32[32,6]{0,1:T(8,128)S(1)} %get-tuple-element.122) | copy-start | bytes 2308
  (66 other events, 1105.0 us)
Sparse Core Ops, SparseCore 0:
  10.5 34.6 all-gather.6
  47.6 50.3 all-gather.10
  100.3 37.4 all-gather.8
  316.4 37.5 reduce-scatter.4
  384.9 23.9 reduce-scatter.6
  453.2 45.6 reduce-scatter.8
  612.4 38.9 reduce-scatter.10
  654.8 76.6 all-reduce.2

commit v2 on v1

--- a/solution.py
+++ b/solution.py
@@ -167,20 +167,56 @@
     )(lengths, lines, qkv, lse, dmixed)
 
 
-def gather_kernel(features, tiles, load_steps, batch, table_ref, ids_ref, out_ref, stash, rows):
+def split_features(features):
+    whole = features // LANES * LANES
+    return whole, features - whole
+
+
+def tile_count(features):
+    whole, rest = split_features(features)
+    return whole // LANES + (rest > 0)
+
+
+def first_of_pair(packed, features):
+    return packed[..., :features]
+
+
+def second_of_pair(packed, features):
+    whole, rest = split_features(features)
+    tail = packed[..., features : features + rest]
+    return jnp.concatenate([packed[..., features + rest :], tail], axis=-1) if whole else tail
+
+
+def pack_pair(first, second):
+    whole, _ = split_features(first.shape[-1])
+    parts = [first, second[..., whole:], second[..., :whole]] if whole else [first, second]
+    return jnp.concatenate(parts, axis=-1)
+
+
+def packed_starts(features, half):
+    whole, rest = split_features(features)
+    base = 0 if half == 0 else features + rest
+    return [base + low for low in range(0, whole, LANES)] + ([whole] if rest else [])
+
+
+def gather_kernel(features, load_steps, batch, table_ref, ids_ref, out_ref, *scratch):
     step = pl.program_id(0)
     width = table_ref.shape[1]
+    tiles = tile_count(features)
+    whole, rest = split_features(features)
+    stash = scratch[:tiles]
+    rows = [scratch[tiles : 2 * tiles], scratch[2 * tiles :]]
 
     @pl.when(step < load_steps)
     def _():
         base = pl.multiple_of(step * width, width)
         for tile in range(tiles):
             low = tile * LANES
-            high = min(features, low + LANES)
-            part = table_ref[low:high, :].astype(bf).astype(jnp.float32)
-            if high - low < LANES:
-                part = jnp.concatenate([part, jnp.zeros((LANES - (high - low), width), jnp.float32)], axis=0)
-            stash[tile, pl.ds(base, width), :] = part.T
+            part = table_ref[low : min(features, low + LANES), :].astype(bf).astype(f32)
+            if low == whole:
+                blank = [jnp.zeros((LANES - 2 * rest, width), f32)] if 2 * rest < LANES else []
+                part = jnp.concatenate([part, part, *blank], axis=0)
+            stash[tile][pl.ds(base, width), :] = part.T
 
     @pl.when(step >= load_steps)
     def _():
@@ -188,26 +224,29 @@
         for half in range(2):
             def take(index, carry):
                 start = pl.multiple_of(index * batch, batch)
-                for inner in range(batch):
-                    token = ids_ref[0, half, start + inner]
-                    for tile in range(tiles):
-                        rows[half, tile, pl.ds(start + inner, 1), :] = stash[tile, pl.ds(token, 1), :]
+                tokens = [ids_ref[0, half, start + inner] for inner in range(batch)]
+                for tile in range(tiles):
+                    for inner in range(batch):
+                        rows[half][tile][pl.ds(start + inner, 1), :] = stash[tile][pl.ds(tokens[inner], 1), :]
                 return carry
             lax.fori_loop(0, count // batch, take, 0)
-        pieces = []
         for half in range(2):
-            for tile in range(tiles):
-                low = tile * LANES
-                pieces.append(rows[half, tile, :, : min(LANES, features - low)])
-        out_ref[...] = jnp.concatenate(pieces, axis=1).astype(bf)
-
-def gather_rows(table, ids, width=2048, chunk=256, batch=32):
+            for tile in range(whole // LANES):
+                low = packed_starts(features, half)[tile]
+                out_ref[:, low : low + LANES] = rows[half][tile][...].astype(bf)
+        if rest:
+            lane = lax.broadcasted_iota(jnp.int32, (1, LANES), 1)
+            shared = jnp.where(lane < rest, rows[0][-1][...], rows[1][-1][...]).astype(bf)
+            out_ref[:, whole : whole + 2 * rest] = shared[:, : 2 * rest]
+
+
+def gather_rows(table, ids, width=4096, batch=16):
     features, vocab = table.shape
-    tiles = pl.cdiv(features, LANES)
+    steps, _, chunk = ids.shape
+    tiles = tile_count(features)
     load_steps = pl.cdiv(vocab, width)
-    steps = ids.shape[0]
     return pl.pallas_call(
-        functools.partial(gather_kernel, features, tiles, load_steps, batch),
+        functools.partial(gather_kernel, features, load_steps, batch),
         grid=(load_steps + steps,),
         in_specs=[
             pl.BlockSpec((features, width), lambda s: (0, jnp.minimum(s, load_steps - 1))),
@@ -215,67 +254,97 @@
         ],
         out_specs=pl.BlockSpec((chunk, 2 * features), lambda s: (jnp.maximum(s - load_steps, 0), 0)),
         out_shape=jax.ShapeDtypeStruct((steps * chunk, 2 * features), bf),
-        scratch_shapes=[
-            pltpu.VMEM((tiles, load_steps * width, LANES), jnp.float32),
-            pltpu.VMEM((2, tiles, chunk, LANES), jnp.float32),
-        ],
+        scratch_shapes=[pltpu.VMEM((load_steps * width, LANES), f32)] * tiles + [pltpu.VMEM((chunk, LANES), f32)] * (2 * tiles),
         compiler_params=pltpu.CompilerParams(vmem_limit_bytes=60 * 2**20),
+        cost_estimate=pl.CostEstimate(flops=0, bytes_accessed=80 * 2**20, transcendentals=0),
         name="gather_rows",
     )(table, ids)
 
-def scatter_kernel(features, tiles, scatter_steps, batch, ids_ref, ids_row_ref, rows_ref, out_ref, total, summed):
+
+def merge_rows(features, batch, ids_row_ref, rows_ref, summed):
+    count = rows_ref.shape[0]
+    whole, rest = split_features(features)
+    place = lax.broadcasted_iota(jnp.int32, (LANES, LANES), 0) // batch
+    same_batch = place == lax.broadcasted_iota(jnp.int32, (LANES, LANES), 1) // batch
+    lane = lax.broadcasted_iota(jnp.int32, (1, LANES), 1)
+    for low in range(0, count, LANES):
+        block = slice(low, low + LANES)
+        for half in range(2):
+            across = jnp.broadcast_to(ids_row_ref[0, half : half + 1, block], (LANES, LANES))
+            match = jnp.where((across == across.T) & same_batch, 1.0, 0.0).astype(bf)
+            for tile, start in enumerate(packed_starts(features, half)):
+                if start == whole:
+                    part = jnp.dot(match, rows_ref[block, start : start + 2 * rest], preferred_element_type=f32)
+                    if 2 * rest < LANES:
+                        part = jnp.concatenate([part, jnp.zeros((LANES, LANES - 2 * rest), f32)], axis=1)
+                    mine = lane < rest if half == 0 else (lane >= rest) & (lane < 2 * rest)
+                    part = jnp.where(mine, part, 0.0)
+                else:
+                    part = jnp.dot(match, rows_ref[block, start : start + LANES], preferred_element_type=f32)
+                summed[half][tile][block, :] = part
+
+
+def add_rows(batch, ids_ref, totals, summed):
+    count = summed[0][0].shape[0]
+    for half in range(2):
+        def add(index, carry):
+            start = pl.multiple_of(index * batch, batch)
+            tokens = [ids_ref[0, half, start + inner] for inner in range(batch)]
+            for total, rows in zip(totals, summed[half]):
+                fresh = [
+                    total[pl.ds(tokens[inner], 1), :] + rows[pl.ds(start + inner, 1), :] for inner in range(batch)
+                ]
+                for inner in range(batch):
+                    total[pl.ds(tokens[inner], 1), :] = fresh[inner]
+            return carry
+        lax.fori_loop(0, count // batch, add, 0)
+
+
+def table_columns(features, totals, base, width):
+    whole, rest = split_features(features)
+    pieces = [total[pl.ds(base, width), :].T for total in totals]
+    if rest:
+        pieces[-1] = pieces[-1][:rest] + pieces[-1][rest : 2 * rest]
+    return pieces
+
+
+def scatter_kernel(features, scatter_steps, batch, ids_ref, ids_row_ref, rows_ref, out_ref, *scratch):
     step = pl.program_id(0)
     width = out_ref.shape[1]
-    count = rows_ref.shape[0]
+    tiles = tile_count(features)
+    totals = scratch[:tiles]
+    summed = [scratch[tiles : 2 * tiles], scratch[2 * tiles :]]
 
     @pl.when(step == 0)
     def _():
-        total[...] = jnp.zeros_like(total)
+        for total in totals:
+            total[...] = jnp.zeros_like(total)
 
     @pl.when(step < scatter_steps)
     def _():
-        place = lax.broadcasted_iota(jnp.int32, (count, count), 0) // batch
-        same_batch = place == lax.broadcasted_iota(jnp.int32, (count, count), 1) // batch
-        for half in range(2):
-            across = jnp.broadcast_to(ids_row_ref[0, half : half + 1, :], (count, count))
-            match = jnp.where((across == across.T) & same_batch, 1.0, 0.0).astype(bf)
-            merged = jnp.dot(match, rows_ref[:, half * features : (half + 1) * features], preferred_element_type=jnp.float32)
-            for tile in range(tiles):
-                low = tile * LANES
-                high = min(features, low + LANES)
-                part = merged[:, low:high]
-                if high - low < LANES:
-                    part = jnp.concatenate([part, jnp.zeros((count, LANES - (high - low)), jnp.float32)], axis=1)
-                summed[half, tile] = part
-        for half in range(2):
-            def add(index, carry):
-                start = pl.multiple_of(index * batch, batch)
-                tokens = [ids_ref[0, half, start + inner] for inner in range(batch)]
-                for tile in range(tiles):
-                    fresh = [
-                        total[tile, pl.ds(tokens[inner], 1), :] + summed[half, tile, pl.ds(start + inner, 1), :]
-                        for inner in range(batch)
-                    ]
-                    for inner in range(batch):
-                        total[tile, pl.ds(tokens[inner], 1), :] = fresh[inner]
-                return carry
-            lax.fori_loop(0, count // batch, add, 0)
+        merge_rows(features, batch, ids_row_ref, rows_ref, summed)
+        add_rows(batch, ids_ref, totals, summed)
 
     @pl.when(step >= scatter_steps)
     def _():
         base = pl.multiple_of((step - scatter_steps) * width, width)
-        for tile in range(tiles):
-            low = tile * LANES
-            high = min(features, low + LANES)
-            out_ref[low:high, :] = total[tile, pl.ds(base, width), :].T[: high - low].astype(bf)
-
-def scatter_rows(rows, ids, vocab, features, width=2048, chunk=256, batch=32):
-    tiles = pl.cdiv(features, LANES)
-    steps = ids.shape[0]
+        low = 0
+        for piece in table_columns(features, totals, base, width):
+            out_ref[low : low + piece.shape[0], :] = piece.astype(bf)
+            low += piece.shape[0]
+
+
+def scatter_scratch(features, vocab, chunk):
+    tiles = tile_count(features)
+    return [pltpu.VMEM((vocab, LANES), f32)] * tiles + [pltpu.VMEM((chunk, LANES), f32)] * (2 * tiles)
+
+
+def scatter_rows(rows, ids, vocab, features, width=2048, batch=16):
+    steps, _, chunk = ids.shape
     flush = pl.cdiv(vocab, width)
     at = lambda s: jnp.minimum(s, steps - 1)
     return pl.pallas_call(
-        functools.partial(scatter_kernel, features, tiles, steps, batch),
+        functools.partial(scatter_kernel, features, steps, batch),
         grid=(steps + flush,),
         in_specs=[
             pl.BlockSpec((1, 2, chunk), lambda s: (at(s), 0, 0), memory_space=pltpu.SMEM),
@@ -284,13 +353,309 @@
         ],
         out_specs=pl.BlockSpec((features, width), lambda s: (0, jnp.maximum(s - steps, 0))),
         out_shape=jax.ShapeDtypeStruct((features, vocab), bf),
-        scratch_shapes=[
-            pltpu.VMEM((tiles, flush * width, LANES), jnp.float32),
-            pltpu.VMEM((2, tiles, chunk, LANES), jnp.float32),
-        ],
+        scratch_shapes=scatter_scratch(features, flush * width, chunk),
         compiler_params=pltpu.CompilerParams(vmem_limit_bytes=60 * 2**20),
+        cost_estimate=pl.CostEstimate(flops=0, bytes_accessed=100 * 2**20, transcendentals=0),
         name="scatter_rows",
     )(ids, ids, rows)
+
+
+def assemble_kernel(features, spread_ref, gain_ref, embedded_ref, normed_ref):
+    for half, take in enumerate((first_of_pair, second_of_pair)):
+        row = jnp.concatenate([take(spread_ref[part], features) for part in range(spread_ref.shape[0])], axis=1)
+        embedded_ref[half] = row
+        stream = row.astype(f32)
+        scale = lax.rsqrt(jnp.mean(stream * stream, axis=1, keepdims=True) + NORM_EPS)
+        normed_ref[half] = (stream * scale * gain_ref[...]).astype(bf)
+
+
+def assemble(spread, gain, block=128):
+    parts, count, features = spread.shape
+    features //= 2
+    width = parts * features
+    block = min(block, count)
+    out = jax.ShapeDtypeStruct((2, count, width), bf)
+    whole_block = pl.BlockSpec((2, block, width), lambda s: (0, s, 0))
+    embedded, normed = pl.pallas_call(
+        functools.partial(assemble_kernel, features),
+        grid=(count // block,),
+        in_specs=[
+            pl.BlockSpec((parts, block, 2 * features), lambda s: (0, s, 0)),
+            pl.BlockSpec((1, width), lambda s: (0, 0)),
+        ],
+        out_specs=[whole_block, whole_block],
+        out_shape=[out, out],
+        compiler_params=pltpu.CompilerParams(vmem_limit_bytes=30 * 2**20),
+        name="assemble",
+    )(spread, gain.reshape(1, width))
+    return embedded.reshape(2 * count, width), normed.reshape(2 * count, width)
+
+
+def pack_back_kernel(features, back_ref, embedded_ref, passed_ref, gain_ref, packed_ref, grad_gain_ref):
+    gain = gain_ref[...]
+    halves = []
+    grad_gain = jnp.zeros_like(gain)
+    for half in range(2):
+        stream = embedded_ref[half].astype(f32)
+        back = back_ref[half]
+        scale = lax.rsqrt(jnp.mean(stream * stream, axis=1, keepdims=True) + NORM_EPS)
+        unit = stream * scale
+        grad_gain += jnp.sum(back * unit, axis=0, keepdims=True)
+        pulled = back * gain
+        along = jnp.mean(pulled * unit, axis=1, keepdims=True)
+        halves.append((passed_ref[half] + scale * (pulled - unit * along)).astype(bf))
+    for part in range(packed_ref.shape[0]):
+        cut = slice(part * features, (part + 1) * features)
+        packed_ref[part] = pack_pair(halves[0][:, cut], halves[1][:, cut])
+
+    @pl.when(pl.program_id(0) == 0)
+    def _():
+        grad_gain_ref[...] = jnp.zeros_like(grad_gain_ref)
+
+    grad_gain_ref[...] += grad_gain
+
+
+def pack_back(back, embedded, passed, gain, features, block=128):
+    rows, width = back.shape
+    count, parts = rows // 2, width // features
+    block = min(block, count)
+    pair = pl.BlockSpec((2, block, width), lambda s: (0, s, 0))
+    line = pl.BlockSpec((1, width), lambda s: (0, 0))
+    packed, grad_gain = pl.pallas_call(
+        functools.partial(pack_back_kernel, features),
+        grid=(count // block,),
+        in_specs=[pair, pair, pair, line],
+        out_specs=[pl.BlockSpec((parts, block, 2 * features), lambda s: (0, s, 0)), line],
+        out_shape=[jax.ShapeDtypeStruct((parts, count, 2 * features), bf), jax.ShapeDtypeStruct((1, width), f32)],
+        compiler_params=pltpu.CompilerParams(vmem_limit_bytes=30 * 2**20),
+        name="pack_back",
+    )(back.reshape(2, count, width), embedded.reshape(2, count, width), passed.reshape(2, count, width), gain.reshape(1, width))
+    return packed, grad_gain[0]
+
+
+def finish_kernel(features, vocab, scatter_steps, batch, ids_ref, ids_row_ref, rows_ref, weight_ref, first_ref, second_ref, *rest):
+    dense_refs, rest = rest[:3], rest[3:]
+    momentum_ref, variance_ref, direction_ref, squares_ref = rest[:4]
+    scratch = rest[4:]
+    step = pl.program_id(0)
+    tiles = tile_count(features)
+    totals = scratch[:tiles]
+    summed = [scratch[tiles : 2 * tiles], scratch[2 * tiles :]]
+
+    @pl.when(step == 0)
+    def _():
+        for total in totals:
+            total[...] = jnp.zeros_like(total)
+        squares_ref[...] = jnp.zeros_like(squares_ref)
+
+    @pl.when(step < scatter_steps)
+    def _():
+        merge_rows(features, batch, ids_row_ref, rows_ref, summed)
+        add_rows(batch, ids_ref, totals, summed)
+
+    @pl.when(step >= scatter_steps)
+    def _():
+        width = weight_ref.shape[1]
+        base = pl.multiple_of((step - scatter_steps) * width, width)
+        inside = base + lax.broadcasted_iota(jnp.int32, (1, width), 1) < vocab
+        low = 0
+        for piece in table_columns(features, totals, base, width):
+            cut = slice(low, low + piece.shape[0])
+            low += piece.shape[0]
+            weight = weight_ref[cut, :]
+            gradient = piece
+            for dense_ref in dense_refs:
+                gradient = gradient + dense_ref[cut, :].astype(f32)
+            momentum, variance, direction = lamb_direction(weight, gradient, first_ref[cut, :], second_ref[cut, :])
+            momentum_ref[cut, :] = momentum
+            variance_ref[cut, :] = variance
+            direction_ref[cut, :] = direction.astype(bf)
+            for line, value in enumerate((weight, direction)):
+                value = jnp.where(inside, value, 0.0)
+                squares_ref[line : line + 1, :] += jnp.sum(value * value, axis=0, keepdims=True)
+
+
+def finish(rows, ids, weight, first, second, dense, width=1024, batch=16):
+    features, vocab = weight.shape
+    steps, _, chunk = ids.shape
+    columns = pl.cdiv(vocab, width)
+    at = lambda s: jnp.minimum(s, steps - 1)
+    block = pl.BlockSpec((features, width), lambda s: (0, jnp.maximum(s - steps, 0)))
+    full = jax.ShapeDtypeStruct(weight.shape, f32)
+    return pl.pallas_call(
+        functools.partial(finish_kernel, features, vocab, steps, batch),
+        grid=(steps + columns,),
+        in_specs=[
+            pl.BlockSpec((1, 2, chunk), lambda s: (at(s), 0, 0), memory_space=pltpu.SMEM),
+            pl.BlockSpec((1, 2, chunk), lambda s: (at(s), 0, 0)),
+            pl.BlockSpec((chunk, 2 * features), lambda s: (at(s), 0)),
+        ]
+        + [block] * 6,
+        out_specs=[block, block, block, pl.BlockSpec((8, width), lambda s: (0, 0))],
+        out_shape=[full, full, jax.ShapeDtypeStruct(weight.shape, bf), jax.ShapeDtypeStruct((8, width), f32)],
+        scratch_shapes=scatter_scratch(features, columns * width, chunk),
+        compiler_params=pltpu.CompilerParams(vmem_limit_bytes=62 * 2**20),
+        cost_estimate=pl.CostEstimate(flops=0, bytes_accessed=300 * 2**20, transcendentals=0),
+        name="finish",
+    )(ids, ids, rows, weight, first, second, *dense)
+
+
+MESH = pl.DeviceIdType.MESH
+
+
+def share_kernel(axes, facts_ref, out_ref, send, received):
+    places = [lax.axis_index(axis) for axis in axes]
+    sizes = [lax.axis_size(axis) for axis in axes]
+    barrier = pltpu.get_barrier_semaphore()
+    for axis, place, size in zip(axes, places, sizes):
+        for step in range(1, size):
+            pl.semaphore_signal(barrier, inc=1, device_id={axis: lax.rem(place + step, size)}, device_id_type=MESH)
+    pl.semaphore_wait(barrier, sum(sizes) - len(sizes))
+    out_ref[places[0], places[1]] = facts_ref[...]
+    slot = 0
+    for axis, place, size in reversed(list(zip(axes, places, sizes))):
+        block = out_ref.at[places[0]] if axis == axes[0] else out_ref.at[places[0], places[1]]
+        copies = []
+        for step in range(1, size):
+            copy = pltpu.make_async_remote_copy(
+                src_ref=block,
+                dst_ref=block,
+                send_sem=send.at[slot],
+                recv_sem=received.at[slot],
+                device_id={axis: lax.rem(place + step, size)},
+                device_id_type=MESH,
+            )
+            copy.start()
+            copies.append(copy)
+            slot += 1
+        for copy in copies:
+            copy.wait()
+
+
+def share_facts(facts, axes, sizes):
+    slots = sum(sizes) - 2
+    return pl.pallas_call(
+        functools.partial(share_kernel, axes),
+        in_specs=[pl.BlockSpec(memory_space=pltpu.VMEM)],
+        out_specs=pl.BlockSpec(memory_space=pltpu.VMEM),
+        out_shape=jax.ShapeDtypeStruct((*sizes, *facts.shape), facts.dtype),
+        scratch_shapes=[pltpu.SemaphoreType.DMA((slots,)), pltpu.SemaphoreType.DMA((slots,))],
+        compiler_params=pltpu.CompilerParams(collective_id=0, has_side_effects=True),
+        name="share_facts",
+    )(facts)
+
+
+def sum_squares_kernel(axes, rows_ref, table_ref, out_ref, slots, send, received):
+    places = [lax.axis_index(axis) for axis in axes]
+    sizes = [lax.axis_size(axis) for axis in axes]
+    count = sizes[0] * sizes[1]
+    mine = places[0] * sizes[1] + places[1]
+    barrier = pltpu.get_barrier_semaphore()
+    peers = []
+    for step in range(1, count):
+        peer = lax.rem(mine + step, count)
+        peers.append({axes[0]: peer // sizes[1], axes[1]: lax.rem(peer, sizes[1])})
+    for peer in peers:
+        pl.semaphore_signal(barrier, inc=1, device_id=peer, device_id_type=MESH)
+    pl.semaphore_wait(barrier, count - 1)
+    lane = lax.broadcasted_iota(jnp.int32, (1, LANES), 1)
+    sums = jnp.sum(rows_ref[...], axis=1, keepdims=True)
+    slots[mine] = table_ref[...]
+    slots[mine, 0:1, :] = jnp.where(lane == 0, sums[0:1], jnp.where(lane == 1, sums[1:2], 0.0)) * table_ref[0:1, :]
+    copies = []
+    for step, peer in enumerate(peers):
+        copy = pltpu.make_async_remote_copy(
+            src_ref=slots.at[mine],
+            dst_ref=slots.at[mine],
+            send_sem=send.at[step],
+            recv_sem=received.at[step],
+            device_id=peer,
+            device_id_type=MESH,
+        )
+        copy.start()
+        copies.append(copy)
+    for copy in copies:
+        copy.wait()
+    total = slots[0]
+    for other in range(1, count):
+        total = total + slots[other]
+    out_ref[...] = total
+
+
+def sum_over(rows, table, axes, sizes):
+    count = sizes[0] * sizes[1]
+    return pl.pallas_call(
+        functools.partial(sum_squares_kernel, axes),
+        in_specs=[pl.BlockSpec(memory_space=pltpu.VMEM)] * 2,
+        out_specs=pl.BlockSpec(memory_space=pltpu.VMEM),
+        out_shape=jax.ShapeDtypeStruct(table.shape, f32),
+        scratch_shapes=[
+            pltpu.VMEM((count, *table.shape), f32),
+            pltpu.SemaphoreType.DMA((count - 1,)),
+            pltpu.SemaphoreType.DMA((count - 1,)),
+        ],
+        compiler_params=pltpu.CompilerParams(collective_id=1, has_side_effects=True),
+        name="sum_over",
+    )(rows, table)
+
+
+def sum_all_kernel(near, far, value_ref, out_ref, near_slots, far_slots, send, received):
+    places = [lax.axis_index(axis) for axis in (*near, far)]
+    sizes = [lax.axis_size(axis) for axis in (*near, far)]
+    count = sizes[0] * sizes[1]
+    mine = places[0] * sizes[1] + places[1]
+    barrier = pltpu.get_barrier_semaphore()
+    plane, line = [], []
+    for step in range(1, count):
+        peer = lax.rem(mine + step, count)
+        plane.append({near[0]: peer // sizes[1], near[1]: lax.rem(peer, sizes[1])})
+    for step in range(1, sizes[2]):
+        line.append({far: lax.rem(places[2] + step, sizes[2])})
+    for peer in plane + line:
+        pl.semaphore_signal(barrier, inc=1, device_id=peer, device_id_type=MESH)
+    pl.semaphore_wait(barrier, len(plane) + len(line))
+    slot = 0
+    value = value_ref[...]
+    for peers, slots, at in ((plane, near_slots, mine), (line, far_slots, places[2])):
+        slots[at] = value
+        copies = []
+        for peer in peers:
+            copy = pltpu.make_async_remote_copy(
+                src_ref=slots.at[at],
+                dst_ref=slots.at[at],
+                send_sem=send.at[slot],
+                recv_sem=received.at[slot],
+                device_id=peer,
+                device_id_type=MESH,
+            )
+            copy.start()
+            copies.append(copy)
+            slot += 1
+        for copy in copies:
+            copy.wait()
+        value = slots[0]
+        for other in range(1, slots.shape[0]):
+            value = value + slots[other]
+    out_ref[...] = value
+
+
+def sum_all(value, near, far, sizes):
+    count = sizes[0] * sizes[1]
+    slots = count - 1 + sizes[2] - 1
+    return pl.pallas_call(
+        functools.partial(sum_all_kernel, near, far),
+        in_specs=[pl.BlockSpec(memory_space=pltpu.VMEM)],
+        out_specs=pl.BlockSpec(memory_space=pltpu.VMEM),
+        out_shape=jax.ShapeDtypeStruct(value.shape, f32),
+        scratch_shapes=[
+            pltpu.VMEM((count, *value.shape), f32),
+            pltpu.VMEM((sizes[2], *value.shape), f32),
+            pltpu.SemaphoreType.DMA((slots,)),
+            pltpu.SemaphoreType.DMA((slots,)),
+        ],
+        compiler_params=pltpu.CompilerParams(collective_id=2, has_side_effects=True),
+        name="sum_all",
+    )(value)
 
 
 def lamb_direction(weight, gradient, moment_one, moment_two):
@@ -303,53 +668,24 @@
     return (momentum, variance, direction)
 
 
-def table_moments_kernel(weight_ref, first_ref, second_ref, mine_ref, other_ref, momentum_ref, variance_ref, direction_ref, squares_ref):
-    weight = weight_ref[...]
-    gradient = mine_ref[...].astype(f32) + other_ref[...].astype(f32)
-    momentum, variance, direction = lamb_direction(weight, gradient, first_ref[...], second_ref[...])
-    momentum_ref[...] = momentum
-    variance_ref[...] = variance
-    direction_ref[...] = direction.astype(bf)
-
-    @pl.when(pl.program_id(0) == 0)
-    def _():
-        squares_ref[...] = jnp.zeros_like(squares_ref)
-
-    squares_ref[0:1, :] += jnp.full((1, LANES), jnp.sum(weight * weight))
-    squares_ref[1:2, :] += jnp.full((1, LANES), jnp.sum(direction * direction))
-
-
-def table_moments(weight, first, second, mine, other, rows=16):
-    features, vocab = weight.shape
-    block = pl.BlockSpec((rows, vocab), lambda s: (s, 0))
-    full = jax.ShapeDtypeStruct(weight.shape, f32)
-    return pl.pallas_call(
-        table_moments_kernel,
-        grid=(features // rows,),
-        in_specs=[block] * 5,
-        out_specs=[block, block, block, pl.BlockSpec((8, LANES), lambda s: (0, 0))],
-        out_shape=[full, full, jax.ShapeDtypeStruct(weight.shape, bf), jax.ShapeDtypeStruct((8, LANES), f32)],
-        compiler_params=pltpu.CompilerParams(vmem_limit_bytes=48 * 2**20),
-        name="table_moments",
-    )(weight, first, second, mine, other)
-
-
-def table_update_kernel(rate_ref, weight_ref, direction_ref, updated_ref):
-    updated_ref[...] = weight_ref[...] - rate_ref[0] * direction_ref[...].astype(f32)
-
-
-def table_update(rate, weight, direction, rows=16):
+def table_update_kernel(squares_ref, weight_ref, direction_ref, updated_ref):
+    norms = jnp.sqrt(squares_ref[0:1, :])
+    rate = LEARN_RATE * norms[:, 0:1] / norms[:, 1:2]
+    updated_ref[...] = weight_ref[...] - rate * direction_ref[...].astype(f32)
+
+
+def table_update(squares, weight, direction, rows=16):
     features, vocab = weight.shape
     block = pl.BlockSpec((rows, vocab), lambda s: (s, 0))
     return pl.pallas_call(
         table_update_kernel,
         grid=(features // rows,),
-        in_specs=[pl.BlockSpec(memory_space=pltpu.SMEM), block, block],
+        in_specs=[pl.BlockSpec(squares.shape, lambda s: (0, 0)), block, block],
         out_specs=block,
         out_shape=jax.ShapeDtypeStruct(weight.shape, f32),
         compiler_params=pltpu.CompilerParams(vmem_limit_bytes=40 * 2**20),
         name="table_update",
-    )(rate, weight, direction)
+    )(squares, weight, direction)
 
 
 def norm_scale(stream, gain_row):
@@ -372,6 +708,21 @@
     far_bucket = 8 + sum(((distance >= threshold).astype(jnp.int32) for threshold in BUCKET_EDGES))
     bucket = jnp.where(distance < 8, distance, far_bucket) + jnp.where(relative > 0, 16, 0)
     return (bucket[:, None] == jnp.arange(BUCKETS)).astype(f32)
+
+
+def after(value, *others):
+    return lax.optimization_barrier((value, *others))[0]
+
+
+def arrivals(groups):
+    found = []
+    for group in range(groups):
+        found.append([])
+        for hop in range(1, groups):
+            for source, way in ((group - hop, 0), (group + hop, 1)):
+                if 0 <= source < groups:
+                    found[-1].append((source, way, hop))
+    return found
 
 
 def swap_cores(value):
@@ -414,56 +765,65 @@
     mine = item_count // mdl_size
     rows = mine * length
     pair_rows = rows // 2
-    chunk = 256
+    chunk = min(512, pair_rows)
     chunks = pair_rows // chunk
     group_items = item_count * dat_size
     width = features * dat_size
     first_slot = dat_index * item_count + mdl_index * mine
 
+    tn = ((0,), (0,))
+    nt = ((1,), (1,))
+
     facts = jnp.concatenate([token_ids, partner[:, None]], axis=1)
-    group_facts = lax.all_gather(facts, "dat", axis=0, tiled=True)
-    group_partner = group_facts[:, length]
-    core_ids = lax.dynamic_index_in_dim(
-        group_facts[:, :length].reshape(dat_size, mdl_size, 2, chunks, chunk), mdl_index, 1, keepdims=False
-    ).transpose(0, 2, 1, 3)
+    facts = jnp.pad(facts, ((0, 0), (0, -facts.shape[1] % LANES)))
+    shared = share_facts(facts, ("grp", "dat"), (grp_size, dat_size))
+    all_ids = shared[..., :length].reshape(grp_size, dat_size, mdl_size, 2, chunks, chunk).transpose(2, 0, 1, 4, 3, 5)
+    all_ids = all_ids.reshape(mdl_size, grp_size, dat_size * chunks, 2, chunk)
+    core_ids = lax.dynamic_index_in_dim(all_ids, mdl_index, 0, keepdims=False)
+    other_ids = lax.dynamic_index_in_dim(all_ids, (mdl_index + 1) % mdl_size, 0, keepdims=False)
+    group_partner = lax.dynamic_index_in_dim(shared[..., length], group_index, 0, keepdims=False).reshape(-1)
     my_lengths = lax.dynamic_slice_in_dim(item_lengths, mdl_index * mine, mine)
     my_prefixes = lax.dynamic_slice_in_dim(prefix_lengths, mdl_index * mine, mine)
 
-    def gathered(shard, axis=0):
-        own = lax.all_gather(shard.astype(bf), "dat", axis=axis, tiled=True)
-        return own, swap_cores(own)
-
-    qkv_halves = gathered(qkv_weight.reshape(features, -1))
-    out_halves = gathered(out_weight, 1)
-    up_halves = gathered(up_weight)
-    down_halves = gathered(down_weight)
+    def gathered(*shards):
+        return lax.all_gather(
+            jnp.concatenate([shard.astype(bf) for shard in shards], axis=1), "dat", axis=0, tiled=True
+        )
+
+    def halves(own):
+        return (own, swap_cores(own))
+
+    first_own = gathered(qkv_weight.reshape(features, -1), out_weight.T)
+    split = qkv_weight.shape[1] * qkv_weight.shape[2]
+    first_halves = halves(first_own)
+    qkv_halves = [part[:, :split] for part in first_halves]
+    out_halves = [part[:, split:] for part in first_halves]
+    up_own = gathered(after(up_weight, first_own))
     onehot = bucket_onehot(length)
     line_halves = [
         jnp.einsum("rb,bh->hr", onehot, table, precision=MAX_PRECISION)
         for table in (bias_table, swap_cores(bias_table))
     ]
 
-    looked_up = gather_rows(embedding, core_ids.reshape(-1, 2, chunk))
+    looked_up = gather_rows(embedding, lax.dynamic_index_in_dim(core_ids, group_index, 0, keepdims=False))
     spread = lax.all_to_all(
         looked_up.reshape(dat_size, pair_rows, 2 * features), "dat", split_axis=0, concat_axis=0, tiled=True
     )
-    embedded = (
-        spread.reshape(dat_size, pair_rows, 2, features).transpose(2, 1, 0, 3).reshape(rows, width).astype(f32)
-    )
-    all_ids = lax.all_gather(core_ids, "grp", axis=0)
-
-    normed_one_f, norm_one_back = jax.vjp(norm_scale, embedded, norm_gains[0])
-    normed_one = normed_one_f.astype(bf)
+    embedded_low, normed_one = assemble(spread, norm_gains[0])
+    down_own = gathered(after(down_weight, embedded_low))
+    embedded = embedded_low.astype(f32)
     qkv_rows = [dot(normed_one, weight).astype(bf).reshape(mine, length, -1) for weight in qkv_halves]
     mixed, log_totals = zip(*[attend(item_qkv, lines, my_lengths) for item_qkv, lines in zip(qkv_rows, line_halves)])
     mixed_rows = [heads.reshape(rows, -1) for heads in mixed]
-    after_attn = embedded + (dot(mixed_rows[0], out_halves[0]) + dot(mixed_rows[1], out_halves[1]))
+    up_halves = halves(after(up_own, mixed[0]))
+    down_halves = halves(after(down_own, mixed[1]))
+    after_attn = embedded + (dot(mixed_rows[0], out_halves[0], nt) + dot(mixed_rows[1], out_halves[1], nt))
     normed_two_f, norm_two_back = jax.vjp(norm_scale, after_attn, norm_gains[1])
     normed_two = normed_two_f.astype(bf)
     gate_acts, gelu_backs = zip(*[jax.vjp(gelu_tanh, dot(normed_two, weight)) for weight in up_halves])
     activated = [act.astype(bf) for act in gate_acts]
     after_ffn = after_attn + (
-        dot(activated[0], down_halves[0], ((1,), (1,))) + dot(activated[1], down_halves[1], ((1,), (1,)))
+        dot(activated[0], down_halves[0], nt) + dot(activated[1], down_halves[1], nt)
     )
     positions = jnp.arange(length)
     pool_mask = (
@@ -497,26 +857,26 @@
     my_pulls = lax.dynamic_slice_in_dim(grad_logits + grad_logits.T, first_slot, mine)
     grad_vectors = jnp.dot(my_pulls, group_vectors, precision=MAX_PRECISION)
 
-    def reduced(own, other):
-        total = (own + swap_cores(other.astype(bf)).astype(f32)).astype(bf)
-        part = lax.psum_scatter(total, "dat", scatter_dimension=0, tiled=True)
-        return lax.psum(part, "grp").astype(f32)
-
-    tn = ((0,), (0,))
-    nt = ((1,), (1,))
+    def both_cores(own, other):
+        return (own + swap_cores(other.astype(bf)).astype(f32)).astype(bf)
+
+    def scattered(total):
+        return lax.psum_scatter(total, "dat", scatter_dimension=0, tiled=True)
+
     grad_after_ffn, grad_gain_three = tail_back(grad_vectors)
     grad_ffn = grad_after_ffn.astype(bf)
-    grad_down = reduced(*[dot(grad_ffn, act, tn) for act in activated])
+    total_down = both_cores(*[dot(grad_ffn, act, tn) for act in activated])
     grad_gates = [
         back(dot(grad_ffn, weight))[0].astype(bf) for back, weight in zip(gelu_backs, down_halves)
     ]
-    grad_up = reduced(*[dot(normed_two, grad_gate, tn) for grad_gate in grad_gates])
+    total_up = both_cores(*[dot(normed_two, grad_gate, tn) for grad_gate in grad_gates])
+    part_ffn = scattered(jnp.concatenate([total_down, total_up], axis=1))
     two_back = dot(grad_gates[0], up_halves[0], nt) + dot(grad_gates[1], up_halves[1], nt)
     grad_after_attn, grad_gain_two = norm_two_back(two_back)
     grad_after_attn = grad_after_attn + grad_after_ffn
     grad_attn = grad_after_attn.astype(bf)
-    grad_out = reduced(*[dot(grad_attn, heads, tn) for heads in mixed_rows]).T
-    grad_mixed = [dot(grad_attn, weight, nt).astype(bf).reshape(mine, length, -1) for weight in out_halves]
+    total_out = both_cores(*[dot(grad_attn, heads, tn) for heads in mixed_rows])
+    grad_mixed = [dot(grad_attn, weight).astype(bf).reshape(mine, length, -1) for weight in out_halves]
     grad_qkv_items, grad_lines = zip(
         *[
             attend_back(item_qkv, lines, my_lengths, stats, grad)
@@ -525,28 +885,10 @@
     )
     grad_qkv_rows = [grad.reshape(rows, -1) for grad in grad_qkv_items]
     one_back = dot(grad_qkv_rows[0], qkv_halves[0], nt) + dot(grad_qkv_rows[1], qkv_halves[1], nt)
-    grad_embedded, grad_gain_one = norm_one_back(one_back)
-    grad_embedded = grad_embedded + grad_after_attn
-    grad_qkv = reduced(*[dot(normed_one, grad, tn) for grad in grad_qkv_rows]).reshape(qkv_weight.shape)
-
-    outgoing = grad_embedded.astype(bf).reshape(2, pair_rows, dat_size, features).transpose(2, 1, 0, 3)
-    own_rows = lax.all_to_all(
-        outgoing.reshape(dat_size, pair_rows, 2 * features), "dat", split_axis=0, concat_axis=0, tiled=True
-    ).reshape(dat_size * pair_rows, 2 * features)
-    upward = [(group, group + 1) for group in range(grp_size - 1)]
-    downward = [(group + 1, group) for group in range(grp_size - 1)]
-    from_below, from_above = [own_rows], [own_rows]
-    for _ in range(grp_size - 1):
-        from_below.append(lax.ppermute(from_below[-1], "grp", upward))
-        from_above.append(lax.ppermute(from_above[-1], "grp", downward))
-    pieces, piece_ids = [own_rows], [core_ids]
-    for hop in range(1, grp_size):
-        pieces.append(jnp.where(group_index >= hop, from_below[hop], from_above[grp_size - hop]))
-        piece_ids.append(lax.dynamic_index_in_dim(all_ids, (group_index - hop) % grp_size, 0, keepdims=False))
-    own_table = scatter_rows(
-        jnp.concatenate(pieces, axis=0), jnp.stack(piece_ids).reshape(-1, 2, chunk), vocab, features
-    )
-    other_table = swap_cores(own_table)
+    outgoing, grad_gain_one = pack_back(one_back, embedded_low, grad_after_attn, norm_gains[0], features)
+    total_qkv = both_cores(*[dot(normed_one, grad, tn) for grad in grad_qkv_rows])
+    total_rest = jnp.concatenate([total_qkv, total_out], axis=1)
+    part_rest = scattered(total_rest)
 
     grad_bias_own, grad_bias_other = [
         jnp.einsum("rb,hr->bh", onehot, grad, precision=MAX_PRECISION) for grad in grad_lines
@@ -564,12 +906,84 @@
             (loss_part * leader).reshape(1),
         ]
     )
-    small = lax.psum(small, ("grp", "dat", "mdl"))
+    used = small.shape[0]
+    small = after(jnp.pad(small, (0, -used % (8 * LANES))).reshape(-1, LANES), total_rest)
+    small = sum_all(small, ("dat", "mdl"), "grp", (dat_size, mdl_size, grp_size)).reshape(-1)
     grad_gains = small[: 3 * width].reshape(3, width)
     grad_bias = lax.dynamic_slice_in_dim(
-        small[3 * width : -1].reshape(BUCKETS, -1), mdl_index * bias_table.shape[1], bias_table.shape[1], axis=1
-    )
-    loss_total = small[-1]
+        small[3 * width : used - 1].reshape(BUCKETS, -1), mdl_index * bias_table.shape[1], bias_table.shape[1], axis=1
+    )
+    loss_total = small[used - 1]
+
+    outgoing = after(outgoing, part_ffn)
+    own_rows = lax.all_to_all(outgoing, "dat", split_axis=0, concat_axis=0, tiled=True)
+    own_rows = own_rows.reshape(dat_size * pair_rows, 2 * features)
+    by_group = arrivals(grp_size)
+    moving = [[own_rows], [own_rows]]
+
+    def move(hop, *waits):
+        senders = range(hop - 1, grp_size - 1)
+        upward = [(group, group + 1) for group in senders]
+        downward = [(grp_size - 1 - group, grp_size - 2 - group) for group in senders]
+        if {group for group, _ in upward} & {group for group, _ in downward}:
+            for way, pairs in enumerate((upward, downward)):
+                moving[way].append(lax.ppermute(after(moving[way][-1], *waits), "grp", pairs))
+        else:
+            rising = group_index >= hop - 1
+            moved = lax.ppermute(after(jnp.where(rising, moving[0][-1], moving[1][-1]), *waits), "grp", upward + downward)
+            moving[0].append(moved)
+            moving[1].append(moved)
+
+    def arrived(place):
+        chosen = None
+        for way, hop in sorted({found[place][1:] for found in by_group}):
+            hit = jnp.any(jnp.array([found[place][1:] == (way, hop) for found in by_group])[group_index])
+            chosen = moving[way][hop] if chosen is None else jnp.where(hit, moving[way][hop], chosen)
+        return chosen, jnp.array([found[place][0] for found in by_group], jnp.int32)[group_index]
+
+    def ids_of(table, group):
+        return lax.dynamic_index_in_dim(table, group, 0, keepdims=False)
+
+    def both_rows(part, group):
+        return (
+            jnp.concatenate([part, swap_cores(part)], axis=0),
+            jnp.concatenate([ids_of(core_ids, group), ids_of(other_ids, group)], axis=0),
+        )
+
+    early = [(own_rows, group_index)]
+    move(1)
+    for hop in range(2, grp_size - 1):
+        early.append(arrived(hop - 2))
+        move(hop, small, early[-1][0])
+    own_table = scatter_rows(
+        after(jnp.concatenate([part for part, _ in early], axis=0), part_rest, small),
+        jnp.concatenate([ids_of(core_ids, group) for _, group in early], axis=0),
+        vocab,
+        features,
+    )
+    other_table = swap_cores(after(own_table, *[ways[-1] for ways in moving]))
+    late_part, late_group = arrived(grp_size - 3)
+    move(grp_size - 1, own_table, late_part)
+    late_rows, late_ids = both_rows(late_part, late_group)
+    late_table = scatter_rows(late_rows, late_ids, vocab, features)
+    last_part, last_group = arrived(grp_size - 2)
+    last_rows, last_ids = both_rows(after(last_part, late_table), last_group)
+    full_ffn, full_rest = lax.psum((after(part_ffn, moving[0][-1], moving[1][-1]), part_rest), "grp")
+
+    table_momentum, table_variance, table_direction, table_squares = finish(
+        last_rows,
+        last_ids,
+        embedding,
+        embedding_first,
+        embedding_second,
+        (own_table, other_table, late_table),
+    )
+    full_ffn, full_rest = after(full_ffn, table_squares), after(full_rest, table_squares)
+    half = total_down.shape[1]
+    grad_down, grad_up = full_ffn[:, :half].astype(f32), full_ffn[:, half:].astype(f32)
+    half = total_qkv.shape[1]
+    grad_qkv = full_rest[:, :half].astype(f32).reshape(qkv_weight.shape)
+    grad_out = full_rest[:, half:].astype(f32).T
 
     weights = (qkv_weight, out_weight, up_weight, down_weight, bias_table, norm_gains)
     gradients = (grad_qkv, grad_out, grad_up, grad_down, grad_bias, grad_gains)
@@ -585,13 +999,10 @@
         lamb_direction(weight, gradient, states[0], states[1])
         for weight, gradient, states in zip(weights, gradients, moments)
     ]
-    table_momentum, table_variance, table_direction, table_squares = table_moments(
-        embedding, embedding_first, embedding_second, own_table, other_table
-    )
     first_mdl = (mdl_index == 0).astype(f32)
     first_dat = (dat_index == 0).astype(f32)
     holder_mask = [1.0, 1.0, 1.0, 1.0, first_dat]
-    square_rows = [table_squares[:2, 0] * first_mdl] + [
+    square_rows = [jnp.stack([first_mdl, first_mdl])] + [
         jnp.stack(
             [
                 jnp.sum(weights[position] * weights[position]),
@@ -606,7 +1017,9 @@
         axis=1,
     ) * (first_mdl * first_dat)
     square_table = jnp.concatenate([jnp.stack(square_rows), gain_rows], axis=0)
-    matrix_norms = jnp.sqrt(lax.psum(square_table, ("dat", "mdl")))
+    square_table = jnp.pad(square_table, ((0, 16 - square_table.shape[0]), (0, LANES - 2)))
+    squares = sum_over(table_squares, square_table, ("dat", "mdl"), (dat_size, mdl_size))
+    matrix_norms = jnp.sqrt(squares[:9, :2])
     rates = LEARN_RATE * matrix_norms[:, 0] / matrix_norms[:, 1]
     updated = [weights[position] - rates[position + 1] * results[position][2] for position in range(5)]
     updated.append(norm_gains - rates[6:, None] * results[5][2])
@@ -615,7 +1028,7 @@
         matrix_norms,
         table_momentum,
         table_variance,
-        table_update(rates[:1], embedding, table_direction),
+        table_update(squares, embedding, table_direction),
     ]
     for position in range(6):
         outputs.extend([results[position][0], results[position][1], updated[position]])

time: 888 us -> 713 us (0.80)
  waiting for transfers between devices: 180 us -> 69.7 us
  blocking collectives: 118 us -> 8.91 us
  Pallas kernels: 287 us -> 384 us
  local copies, waits for them, and re-layouts: 50.7 us -> 24.9 us
  starting transfers between devices: 51.1 us -> 30.8 us
  matrix products: 106 us -> 87.3 us
  other arithmetic: 67.1 us -> 79.7 us
    pallas_call x3 -> x9, Pallas kernels: 179 us -> 276 us  [the longest x1 98.6 us: finish(): pl.pallas_call(functools.partial(finish_kernel, features, vocab, steps, b...]
    ppermute x6 -> x5, waiting for transfers between devices: 56.6 us -> 0.01 us  [the longest x4 0.01 us: move(): lax.ppermute(after(moving[way][-1], *waits), 'grp', pairs)]
    all_gather x3 -> x0, blocking collectives: 54.5 us -> none  [the longest x1 36.6 us: shards(): all_ids = lax.all_gather(core_ids, 'grp', axis=0)]
    psum x2 -> x0, blocking collectives: 54.3 us -> none  [the longest x1 41.9 us: shards(): small = lax.psum(small, ('grp', 'dat', 'mdl'))]
    reduce_scatter x4 -> x2, waiting for transfers between devices: 37.1 us -> 0.02 us  [scattered(): return lax.psum_scatter(total, 'dat', scatter_dimension=0, tiled=True)]
    psum x1, waiting for transfers between devices: 31.2 us -> 0.02 us  [shards(): lax.psum((after(part_ffn, moving[0][-1], moving[1][-1]), part_rest), 'grp')]
    dot_general x24, matrix products: 103 us -> 85 us  [dot(): lax.dot_general(left, right, (dims, ((), ())), preferred_element_type=f32)]
    ppermute x10 -> x11, starting transfers between devices: 24.9 us -> 8.75 us  [swap_cores(): lax.ppermute(value, 'mdl', [(core, (core + 1) % size) for core in range(s...]
  transfers between devices with their start and end apart: 26 -> 24, of which waited for: 9 -> 4; matrix products, arithmetic and copies ran while one was open for 17% -> 16% of each run, Pallas kernels for 21% -> 49%
where the time goes in v2:
time: 713 us; the launch traced here: 708 us
  Pallas kernels  384 us (54%)
  matrix products  87.3 us (12%)
  other arithmetic  79.7 us (11%)
  waiting for transfers between devices  69.7 us (10%)
  starting transfers between devices  30.8 us (4%)
  local copies, waits for them, and re-layouts  24.9 us (3%)
  between operations  22.8 us (3%)
  blocking collectives  8.91 us (1%)
    pallas_call x1, Pallas kernels, finish(): pl.pallas_call(functools.partial(finish_kernel, features, vocab, steps, b...  98.6 us
    pallas_call x2, Pallas kernels, scatter_rows(): pl.pallas_call(functools.partial(scatter_kernel, features, steps, batch),...  94.2 us
    dot_general x24, matrix products, dot(): lax.dot_general(left, right, (dims, ((), ())), preferred_element_type=f32)  85 us
    pallas_call x2, Pallas kernels, attend_back(): pl.pallas_call(functools.partial(attend_back_kernel, pairs, HEAD ** (-0.5...  47.1 us
    pallas_call x2, Pallas kernels, attend(): pl.pallas_call(functools.partial(attend_kernel, pairs, HEAD ** (-0.5)), i...  39.1 us
    pallas_call x1, Pallas kernels, sum_all(): pl.pallas_call(functools.partial(sum_all_kernel, near, far), in_specs=[pl...  31.7 us
    pallas_call x1, Pallas kernels, gather_rows(): pl.pallas_call(functools.partial(gather_kernel, features, load_steps, bat...  23.9 us
    all_to_all x1, waiting for transfers between devices, shards(): lax.all_to_all(outgoing, 'dat', split_axis=0, concat_axis=0, tiled=True)  22.3 us
  transfers between devices with their start and end apart: 24, of which 4 were waited for; matrix products, arithmetic and copies ran while one was open for 16% of the time, Pallas kernels for 49%

profile of v2, /device:TPU:17, one launch (start us, length us, event | category | flops | bytes accessed | tf_op | source)
XLA Modules:
  0.0 708.1 jit_solution(16670895674111183232)
XLA Ops:
  18.8 10.2 %share_facts.1 = s32[4,4,4,640]{3,2,1,0:T(4,128)} custom-call(s32[4,640]{1,0:T(4,128)} %pad.12.facts_ref), custom_call_target="tpu_custom_call" | custom-call | tf_op jit(solution)/shard_map/share_facts/pallas_call | solution.py:537
  30.7 23.9 %gather_rows.1 = bf16[2048,384]{1,0:T(8,128)(2,1)} custom-call(f32[192,32128]{1,0:T(8,128)} %weight_ref.3, s32[4,2,512]{2,1,0:T(2,128)} %get-tuple-element.252.ids_ref), custom_call_target="tpu_custom_call" | custom-call | bytes 83886080 | tf_op jit(solution)/shard_map/gather_rows/pallas_call | solution.py:248
  58.5 18.6 %all-to-all-done.spread_ref = bf16[4,512,384]{2,1,0:T(8,128)(2,1)S(1)} async-done(((bf16[4,512,384]{2,1,0:T(8,128)(2,1)}), bf16[4,512,384]{2,1,0:T(8,128)(2,1)S(1)}, u32[]{:S(2)}, u32[]{:S(2)}) %all-to-all-start) | async-done | bytes 1572896 | tf_op jit(solution)/shard_map/all_to_all | solution.py:809
  91.2 3.8 convolution_convert_fusion.1
  95.0 19.4 %attend.2 = (bf16[2,512,384]{2,1,0:T(8,128)(2,1)S(1)}, f32[2,512,384]{2,1,0:T(8,128)S(1)}) custom-call(s32[2]{0:T(128)S(1)} %dynamic_slice.66.lens_ref, f32[6,1024]{1,0:T(8,128)S(1)} %convolution_bitcast_fusion.3.line_ref, bf16[2,512,1152]{2,1,0:T(8,128)(2,1)S(1)} %bitcast.192), custom_call_target="tpu_custom_call" | custom-call | flops 1610612736 | bytes 4718592 | tf_op jit(solution)/shard_map/attend/pallas_call | solution.py:93
  114.5 4.3 fusion.39
  122.6 19.6 %attend.3 = (bf16[2,512,384]{2,1,0:T(8,128)(2,1)S(1)}, f32[2,512,384]{2,1,0:T(8,128)S(1)}) custom-call(s32[2]{0:T(128)S(1)} %dynamic_slice.66.lens_ref, f32[6,1024]{1,0:T(8,128)S(1)} %convolution_bitcast_fusion.2.line_ref, bf16[2,512,1152]{2,1,0:T(8,128)(2,1)S(1)} %bitcast.194), custom_call_target="tpu_custom_call" | custom-call | flops 1610612736 | bytes 4718592 | tf_op jit(solution)/shard_map/attend/pallas_call | solution.py:93
  145.2 16.1 %all-gather.7.cloned.1.call-done = bf16[768,1536]{1,0:T(8,128)(2,1)} async-done(((bf16[192,1536]{1,0:T(8,128)(2,1)}), bf16[768,1536]{1,0:T(8,128)(2,1)}) %all-gather.7.cloned.1.call-update) | async-done | bytes 2359312 | tf_op jit(solution)/shard_map/all_gather | solution.py:789
  170.6 3.8 fusion.93
  177.1 8.8 %multiply_reduce_fusion.3 = (f32[1024]{0:T(1024)S(1)}, f32[1024,768]{1,0:T(8,128)}) fusion(f32[1024,768]{1,0:T(8,128)S(1)} %get-tuple-element.266, f32[1024,768]{1,0:T(8,128)S(1)} %fusion.93, bf16[768,1536]{1,0:T(8,128)(2,1)} %collective-permute-done.3, f32[1024,1536]{1,0:T(8,128)S(1)} %fusion.110), kind=kOutput, calls=%fused_computation.47 | convolution fusion | flops 2433219584 | bytes 18092032 | tf_op jit(solution)/shard_map/dot_general | solution.py:702
  188.5 8.9 %all-gather = f32[8,2,768]{2,1,0:T(2,128)S(1)} all-gather(f32[1,2,768]{2,1,0:T(2,128)S(1)} %multiply_bitcast_fusion), channel_id=1, replica_groups=mesh['grp'=4,'dat'=4,'mdl'=2] {'dat','mdl'}, dimensions={0}, use_global_device_ids=true | all-gather | bytes 55296 | tf_op jit(solution)/shard_map/all_gather | solution.py:840
  208.9 7.6 %fusion.13 = bf16[1024,1536]{1,0:T(8,128)(2,1)S(1)} fusion(f32[1024,1536]{1,0:T(8,128)S(1)} %copy-done.74, bf16[1024,768]{1,0:T(8,128)(2,1)S(1)} %fusion.22, bf16[768,1536]{1,0:T(8,128)(2,1)} %collective-permute-done.3), kind=kOutput, calls=%fused_computation.17 | convolution fusion | flops 2447376384 | bytes 13369344 | tf_op jit(solution)/shard_map/dot_general | solution.py:702
  219.9 6.3 fusion.6
  235.8 5.4 fusion.111
  249.8 23.5 %attend_back.3 = (bf16[2,512,1152]{2,1,0:T(8,128)(2,1)S(1)}, f32[6,1024]{1,0:T(8,128)S(1)}) custom-call(s32[2]{0:T(128)S(1)} %dynamic_slice.66.lens_ref, f32[6,1024]{1,0:T(8,128)S(1)} %convolution_bitcast_fusion.2.line_ref, bf16[2,512,1152]{2,1,0:T(8,128)(2,1)S(1)} %bitcast.195, f32[2,512,384]{2,1,0:T(8,128)S(1)} %copy-done.13, ...), custom_call_target="tpu_custom_call" | custom-call | flops 4026531840 | bytes 7864320 | tf_op jit(solution)/shard_map/attend_back/pallas_call | solution.py:158
  280.2 23.6 %attend_back.2 = (bf16[2,512,1152]{2,1,0:T(8,128)(2,1)S(1)}, f32[6,1024]{1,0:T(8,128)S(1)}) custom-call(s32[2]{0:T(128)S(1)} %dynamic_slice.66.lens_ref, f32[6,1024]{1,0:T(8,128)S(1)} %convolution_bitcast_fusion.3.line_ref, bf16[2,512,1152]{2,1,0:T(8,128)(2,1)S(1)} %bitcast.193, f32[2,512,384]{2,1,0:T(8,128)S(1)} %copy-done.11, ...), custom_call_target="tpu_custom_call" | custom-call | flops 4026531840 | bytes 7864320 | tf_op jit(solution)/shard_map/attend_back/pallas_call | solution.py:158
  306.0 3.7 convolution_add_fusion.1
  316.5 4.4 all-to-all-start.1
  322.6 22.3 %all-to-all-done.1 = bf16[4,512,384]{2,1,0:T(8,128)(2,1)} async-done(((bf16[4,512,384]{2,1,0:T(8,128)(2,1)}), bf16[4,512,384]{2,1,0:T(8,128)(2,1)}, u32[]{:S(2)}, u32[]{:S(2)}) %all-to-all-start.1) | async-done | bytes 1572896 | tf_op jit(solution)/shard_map/all_to_all | solution.py:919
  353.1 31.7 %sum_all.1 = f32[24,128]{1,0:T(8,128)} custom-call(f32[24,128]{1,0:T(8,128)} %fusion.48.value_ref), custom_call_target="tpu_custom_call" | custom-call | tf_op jit(solution)/shard_map/sum_all/pallas_call | solution.py:645
  389.0 4.6 collective-permute-start.11
  397.7 46.7 %scatter_rows.2.rest_0_ = bf16[192,32128]{1,0:T(8,128)(2,1)} custom-call(s32[8,2,512]{2,1,0:T(2,128)} %pad_add_fusion.1.ids_ref.ids_row_ref, s32[8,2,512]{2,1,0:T(2,128)} %pad_add_fusion.1.ids_ref.ids_row_ref, bf16[4096,384]{1,0:T(8,128)(2,1)} %pad_maximum_fusion.1.rows_ref), custom_call_target="tpu_custom_call" | custom-call | bytes 104857600 | tf_op jit(solution)/shard_map/scatter_rows/pallas_call | solution.py:346
  444.4 4.3 collective-permute-start.15
  449.3 4.2 select_select_fusion.1
  456.7 12.6 %collective-permute-done.13 = bf16[2048,384]{1,0:T(8,128)(2,1)S(1)} collective-permute-done((bf16[2048,384]{1,0:T(8,128)(2,1)S(1)}, bf16[2048,384]{1,0:T(8,128)(2,1)S(1)}, u32[]{:S(2)}, u32[]{:S(2)}) %collective-permute-start.13) | collective-permute-done | bytes 1572896 | tf_op jit(solution)/shard_map/ppermute | solution.py:730
  471.3 47.5 %scatter_rows.3.rest_2_ = bf16[192,32128]{1,0:T(8,128)(2,1)} custom-call(s32[8,2,512]{2,1,0:T(2,128)} %pad_add_fusion.2.ids_ref.ids_row_ref, s32[8,2,512]{2,1,0:T(2,128)} %pad_add_fusion.2.ids_ref.ids_row_ref, bf16[4096,384]{1,0:T(8,128)(2,1)} %pad_maximum_fusion.2.rows_ref), custom_call_target="tpu_custom_call" | custom-call | bytes 104857600 | tf_op jit(solution)/shard_map/scatter_rows/pallas_call | solution.py:346
  532.0 98.6 %finish.1 = (f32[192,32128]{1,0:T(8,128)}, f32[192,32128]{1,0:T(8,128)}, bf16[192,32128]{1,0:T(8,128)(2,1)}, f32[8,1024]{1,0:T(8,128)}) custom-call(s32[8,2,512]{2,1,0:T(2,128)} %pad_add_fusion.ids_ref.ids_row_ref, s32[8,2,512]{2,1,0:T(2,128)} %pad_add_fusion.ids_ref.ids_row_ref, bf16[4096,384]{1,0:T(8,128)(2,1)} %pad_maximum_fusion.3.rows_ref, ...), custom_call_target="tpu_custom_call" | custom-call | bytes 314572800 | tf_op jit(solution)/shard_map/finish/pallas_call | solution.py:485
  631.7 7.6 %multiply_reduce_fusion.6 = (f32[]{:T(128)}, f32[]{:T(128)}, f32[192,1536]{1,0:T(8,128)}, f32[192,1536]{1,0:T(8,128)}, f32[]{:T(128)}, /*index=5*/f32[192,1536]{1,0:T(8,128)}, f32[192,1536]{1,0:T(8,128)}, f32[]{:T(128)}) fusion(f32[192,1536]{1,0:T(8,128)S(1)} %copy-done.16, bf16[192,3072]{1,0:T(8,128)(2,1)} %get-tuple-element.81, f32[192,1536]{1,0:T(8,128)} %param.55, ...), kind=kLoop, calls=%fused_computation.82 | loop fusion | flops 10616828 | bytes 12976144 | tf_op jit(solution)/shard_map/reduce_sum | solution.py:1008
  650.0 11.8 %sum_over.1.squares_ref = f32[16,128]{1,0:T(8,128)} custom-call(f32[8,1024]{1,0:T(8,128)} %get-tuple-element.78.rows_ref, f32[16,128]{1,0:T(8,128)} %pad.14.table_ref), custom_call_target="tpu_custom_call" | custom-call | tf_op jit(solution)/shard_map/sum_over/pallas_call | solution.py:587
  663.9 4.5 copy-done
  669.1 22.2 %table_update.1 = f32[192,32128]{1,0:T(8,128)} custom-call(f32[16,128]{1,0:T(8,128)S(1)} %copy-done.1, f32[192,32128]{1,0:T(8,128)} %weight_ref.3, bf16[192,32128]{1,0:T(8,128)(2,1)S(1)} %copy-done), custom_call_target="tpu_custom_call" | custom-call | tf_op jit(solution)/shard_map/table_update/pallas_call | solution.py:680
  697.3 3.8 multiply_subtract_fusion
  (332 shorter events, 150.9 us)
Async XLA Ops:
  7.2 75.2 %all-gather.5.cloned.1.call-start = ((), (), s32[]{:S(2)}) async-start(), calls=%async_computation.4 | async-start | bytes 2949120 | tf_op jit(solution)/shard_map/all_gather | solution.py:789
  54.7 22.4 %all-to-all-start = ((bf16[4,512,384]{2,1,0:T(8,128)(2,1)}), bf16[4,512,384]{2,1,0:T(8,128)(2,1)S(1)}, u32[]{:S(2)}, u32[]{:S(2)}) async-start(bf16[4,512,384]{2,1,0:T(8,128)(2,1)} %bitcast.200), calls=%async_computation | async-start | bytes 3145728 | tf_op jit(solution)/shard_map/all_to_all | solution.py:809
  58.4 86.4 %all-gather.9.cloned.1.call-start = ((), (), s32[]{:S(2)}) async-start(), calls=%async_computation.6 | async-start | bytes 2949120 | tf_op jit(solution)/shard_map/all_gather | solution.py:789
  82.4 78.9 %all-gather.7.cloned.1.call-start = ((), (), s32[]{:S(2)}) async-start(), calls=%async_computation.5 | async-start | bytes 2949120 | tf_op jit(solution)/shard_map/all_gather | solution.py:789
  84.6 231.8 %reduce-scatter.3.cloned.1.call-start = ((), (), s32[]{:S(2)}) async-start(), calls=%async_computation.7 | async-start | bytes 5898240 | tf_op jit(solution)/shard_map/reduce_scatter | solution.py:864
  85.2 5.5 collective-permute-start
  86.8 32.1 %collective-permute-start.1 = (bf16[768,1536]{1,0:T(8,128)(2,1)}, bf16[768,1536]{1,0:T(8,128)(2,1)}, u32[]{:S(2)}, u32[]{:S(2)}) collective-permute-start(bf16[768,1536]{1,0:T(8,128)(2,1)} %all-gather.5.cloned.1.call-done), channel_id=1, source_target_pairs={{0,1},{1,0},{2,3},{3,2},{4,5},{5,4},{6,7},{7,6},{8,9},{9,8},{10,11... | collective-permute-start | bytes 7077896 | tf_op jit(solution)/shard_map/ppermute | solution.py:730
  144.8 32.3 %collective-permute-start.3 = (bf16[768,1536]{1,0:T(8,128)(2,1)}, bf16[768,1536]{1,0:T(8,128)(2,1)}, u32[]{:S(2)}, u32[]{:S(2)}) collective-permute-start(bf16[768,1536]{1,0:T(8,128)(2,1)} %all-gather.9.cloned.1.call-done), channel_id=1, source_target_pairs={{0,1},{1,0},{2,3},{3,2},{4,5},{5,4},{6,7},{7,6},{8,9},{9,8},{10,11... | collective-permute-start | bytes 7077896 | tf_op jit(solution)/shard_map/ppermute | solution.py:730
  161.2 13.2 %collective-permute-start.2 = (bf16[768,1536]{1,0:T(8,128)(2,1)}, bf16[768,1536]{1,0:T(8,128)(2,1)S(1)}, u32[]{:S(2)}, u32[]{:S(2)}) collective-permute-start(bf16[768,1536]{1,0:T(8,128)(2,1)} %all-gather.7.cloned.1.call-done), channel_id=1, source_target_pairs={{0,1},{1,0},{2,3},{3,2},{4,5},{5,4},{6,7},{7,6},{8,9},{9,8},{10,11... | collective-permute-start | bytes 7077896 | tf_op jit(solution)/shard_map/ppermute | solution.py:730
  208.7 17.6 %collective-permute-start.6 = (bf16[768,1536]{1,0:T(8,128)(2,1)S(1)}, bf16[768,1536]{1,0:T(8,128)(2,1)S(1)}, u32[]{:S(2)}, u32[]{:S(2)}) collective-permute-start(bf16[768,1536]{1,0:T(8,128)(2,1)S(1)} %convolution_convert_fusion.3), channel_id=1, source_target_pairs={{0,1},{1,0},{2,3},{3,2},{4,5},{5,4},{6,7},{7,6},{8,9},{9,8},{10,11... | collective-permute-start | bytes 7077896 | tf_op jit(solution)/shard_map/ppermute | solution.py:730
  219.5 10.0 %collective-permute-start.7 = (bf16[768,1536]{1,0:T(8,128)(2,1)S(1)}, bf16[768,1536]{1,0:T(8,128)(2,1)S(1)}, u32[]{:S(2)}, u32[]{:S(2)}) collective-permute-start(bf16[768,1536]{1,0:T(8,128)(2,1)S(1)} %convolution_convert_fusion.2), channel_id=1, source_target_pairs={{0,1},{1,0},{2,3},{3,2},{4,5},{5,4},{6,7},{7,6},{8,9},{9,8},{10,11... | collective-permute-start | bytes 7077896 | tf_op jit(solution)/shard_map/ppermute | solution.py:730
  276.8 37.4 %collective-permute-start.4 = (bf16[768,1152]{1,0:T(8,128)(2,1)}, bf16[768,1152]{1,0:T(8,128)(2,1)S(1)}, u32[]{:S(2)}, u32[]{:S(2)}) collective-permute-start(bf16[768,1152]{1,0:T(8,128)(2,1)} %fusion.14), channel_id=1, source_target_pairs={{0,1},{1,0},{2,3},{3,2},{4,5},{5,4},{6,7},{7,6},{8,9},{9,8},{10,11... | collective-permute-start | bytes 5308424 | tf_op jit(solution)/shard_map/ppermute | solution.py:730
  278.0 35.2 %collective-permute-start.5 = (bf16[768,384]{1,0:T(8,128)(2,1)S(1)}, bf16[768,384]{1,0:T(8,128)(2,1)S(1)}, u32[]{:S(2)}, u32[]{:S(2)}) collective-permute-start(bf16[768,384]{1,0:T(8,128)(2,1)S(1)} %convolution_convert_fusion.6), channel_id=1, source_target_pairs={{0,1},{1,0},{2,3},{3,2},{4,5},{5,4},{6,7},{7,6},{8,9},{9,8},{10,11... | collective-permute-start | bytes 1769480 | tf_op jit(solution)/shard_map/ppermute | solution.py:730
  316.5 28.4 %all-to-all-start.1 = ((bf16[4,512,384]{2,1,0:T(8,128)(2,1)}), bf16[4,512,384]{2,1,0:T(8,128)(2,1)}, u32[]{:S(2)}, u32[]{:S(2)}) async-start(bf16[4,512,384]{2,1,0:T(8,128)(2,1)} %get-tuple-element.71), calls=%async_computation.2 | async-start | bytes 3145728 | tf_op jit(solution)/shard_map/all_to_all | solution.py:919
  320.8 76.8 %reduce-scatter.5.cloned.1.call-start = ((), (), s32[]{:S(2)}) async-start(), calls=%async_computation.8 | async-start | bytes 2949120 | tf_op jit(solution)/shard_map/reduce_scatter | solution.py:864
  322.5 71.1 %copy-start.36 = (s32[4,2,512]{2,1,0:T(2,128)S(1)}, s32[4,2,512]{2,1,0:T(2,128)}, u32[]{:S(2)}) copy-start(s32[4,2,512]{2,1,0:T(2,128)} %get-tuple-element.252.ids_ref) | copy-start | bytes 49156
  322.5 71.1 %copy-start.43 = (s32[4,2,512]{2,1,0:T(2,128)S(1)}, s32[4,2,512]{2,1,0:T(2,128)}, u32[]{:S(2)}) copy-start(s32[4,2,512]{2,1,0:T(2,128)} %get-tuple-element.249) | copy-start | bytes 49156
  322.5 308.0 %all-reduce.6.cloned.1.call-start = ((), (), s32[]{:S(2)}) async-start(), calls=%async_computation.9 | async-start | bytes 3538944 | tf_op jit(solution)/shard_map/psum | solution.py:971
  344.9 39.9 %collective-permute-start.8 = (bf16[2048,384]{1,0:T(8,128)(2,1)}, bf16[2048,384]{1,0:T(8,128)(2,1)}, u32[]{:S(2)}, u32[]{:S(2)}) collective-permute-start(bf16[2048,384]{1,0:T(8,128)(2,1)} %bitcast.32), channel_id=1, source_target_pairs={{0,8},{8,16},{16,24},{1,9},{9,17},{17,25},{2,10},{10,18},{18,26},{... | collective-permute-start | bytes 4718600 | tf_op jit(solution)/shard_map/ppermute | solution.py:930
  348.0 36.8 %collective-permute-start.9 = (bf16[2048,384]{1,0:T(8,128)(2,1)}, bf16[2048,384]{1,0:T(8,128)(2,1)S(1)}, u32[]{:S(2)}, u32[]{:S(2)}) collective-permute-start(bf16[2048,384]{1,0:T(8,128)(2,1)} %bitcast.32), channel_id=1, source_target_pairs={{24,16},{16,8},{8,0},{25,17},{17,9},{9,1},{26,18},{18,10},{10,2},{... | collective-permute-start | bytes 4718600 | tf_op jit(solution)/shard_map/ppermute | solution.py:930
  387.1 57.3 %collective-permute-start.10 = (bf16[2048,384]{1,0:T(8,128)(2,1)}, bf16[2048,384]{1,0:T(8,128)(2,1)S(1)}, u32[]{:S(2)}, u32[]{:S(2)}) collective-permute-start(bf16[2048,384]{1,0:T(8,128)(2,1)} %collective-permute-done.8), channel_id=1, source_target_pairs={{8,16},{16,24},{9,17},{17,25},{10,18},{18,26},{11,19},{19,27},{12,... | collective-permute-start | bytes 4718600 | tf_op jit(solution)/shard_map/ppermute | solution.py:930
  389.0 55.3 %collective-permute-start.11 = (bf16[2048,384]{1,0:T(8,128)(2,1)S(1)}, bf16[2048,384]{1,0:T(8,128)(2,1)}, u32[]{:S(2)}, u32[]{:S(2)}) collective-permute-start(bf16[2048,384]{1,0:T(8,128)(2,1)S(1)} %collective-permute-done.9), channel_id=1, source_target_pairs={{16,8},{8,0},{17,9},{9,1},{18,10},{10,2},{19,11},{11,3},{20,12},{1... | collective-permute-start | bytes 4718600 | tf_op jit(solution)/shard_map/ppermute | solution.py:930
  397.7 51.0 %copy-start.65 = (pred[4]{0:T(512)(128)(4,1)S(1)}, pred[4]{0:T(512)(128)(4,1)}, u32[]{:S(2)}) copy-start(pred[4]{0:T(512)(128)(4,1)} %constant.371.clone) | copy-start | bytes 16
  444.4 87.6 %collective-permute-start.15 = (bf16[192,32128]{1,0:T(8,128)(2,1)}, bf16[192,32128]{1,0:T(8,128)(2,1)}, u32[]{:S(2)}, u32[]{:S(2)}) collective-permute-start(bf16[192,32128]{1,0:T(8,128)(2,1)} %scatter_rows.2.rest_0_), channel_id=1, source_target_pairs={{0,1},{1,0},{2,3},{3,2},{4,5},{5,4},{6,7},{7,6},{8,9},{9,8},{10,11... | collective-permute-start | bytes 37011464 | tf_op jit(solution)/shard_map/ppermute | solution.py:730
  453.5 15.8 %collective-permute-start.13 = (bf16[2048,384]{1,0:T(8,128)(2,1)S(1)}, bf16[2048,384]{1,0:T(8,128)(2,1)S(1)}, u32[]{:S(2)}, u32[]{:S(2)}) collective-permute-start(bf16[2048,384]{1,0:T(8,128)(2,1)S(1)} %get-tuple-element.242), channel_id=1, source_target_pairs={{0,1},{1,0},{2,3},{3,2},{4,5},{5,4},{6,7},{7,6},{8,9},{9,8},{10,11... | collective-permute-start | bytes 4718600 | tf_op jit(solution)/shard_map/ppermute | solution.py:730
  453.5 65.3 %collective-permute-start.12 = (bf16[2048,384]{1,0:T(8,128)(2,1)}, bf16[2048,384]{1,0:T(8,128)(2,1)S(1)}, u32[]{:S(2)}, u32[]{:S(2)}) collective-permute-start(bf16[2048,384]{1,0:T(8,128)(2,1)} %get-tuple-element.75), channel_id=1, source_target_pairs={{16,24},{8,0},{17,25},{9,1},{18,26},{10,2},{19,27},{11,3},{20,28},... | collective-permute-start | bytes 4718600 | tf_op jit(solution)/shard_map/ppermute | solution.py:933
  523.7 6.3 collective-permute-start.14
  528.5 163.5 %copy-start.47 = (f32[32,6]{0,1:T(8,128)}, f32[32,6]{0,1:T(8,128)S(1)}, u32[]{:S(2)}) copy-start(f32[32,6]{0,1:T(8,128)S(1)} %get-tuple-element.224) | copy-start | bytes 2308
  528.5 163.5 %copy-start.48 = (f32[32,6]{0,1:T(8,128)}, f32[32,6]{0,1:T(8,128)S(1)}, u32[]{:S(2)}) copy-start(f32[32,6]{0,1:T(8,128)S(1)} %get-tuple-element.225) | copy-start | bytes 2308
  532.0 99.7 %copy-start.16 = (f32[192,1536]{1,0:T(8,128)S(1)}, f32[192,1536]{1,0:T(8,128)}, u32[]{:S(2)}) copy-start(f32[192,1536]{1,0:T(8,128)} %param.44) | copy-start | bytes 3538948
  643.9 49.8 %copy-start.29 = (f32[384,192]{0,1:T(8,128)}, f32[384,192]{0,1:T(8,128)S(1)}, u32[]{:S(2)}) copy-start(f32[384,192]{0,1:T(8,128)S(1)} %get-tuple-element.230) | copy-start | bytes 884740
  643.9 49.8 %copy-start.30 = (f32[384,192]{0,1:T(8,128)}, f32[384,192]{0,1:T(8,128)S(1)}, u32[]{:S(2)}) copy-start(f32[384,192]{0,1:T(8,128)S(1)} %get-tuple-element.231) | copy-start | bytes 884740
  (71 other events, 575.5 us)
Sparse Core Ops, SparseCore 0:
  10.6 38.9 all-gather.4
  82.5 38.7 all-gather.8
  123.7 37.4 all-gather.6
  235.9 56.6 reduce-scatter.2
  325.0 44.0 reduce-scatter.4
  524.3 73.6 all-reduce.5

commit v3 on v2

--- a/solution.py
+++ b/solution.py
@@ -28,9 +28,10 @@
 f32 = jnp.float32
 
 
-BLOCK=128
-NT=(((1,),(1,)),((),()))
-TN=(((0,),(0,)),((),()))
+BLOCK = 128
+NT = (((1,), (1,)), ((), ()))
+TN = (((0,), (0,)), ((), ()))
+
 
 def toeplitz(line, rows):
     out = line
@@ -39,6 +40,7 @@
         out = jnp.concatenate([out, pltpu.roll(out, size, 1)], axis=0)
         size *= 2
     return out
+
 
 def diagonal_sums(square):
     rows, width = square.shape
@@ -49,12 +51,17 @@
         square = square + pltpu.roll(pltpu.roll(square, width - shift, 1), 8 - shift, 0)
     return square[:1]
 
-def attend_kernel(pairs, scale, lens_ref, line_ref, qkv_ref, mixed_ref, lse_ref):
+
+def head_halves(pair):
+    first = lax.broadcasted_iota(jnp.int32, (1, LANES), 1) < HEAD
+    return jnp.where(first, pair, 0), jnp.where(first, 0, pair)
+
+
+def attend_kernel(pairs, scale, lens_ref, line_ref, qkv_ref, mixed_ref, lse_ref, scores, probs):
     items, length, _ = mixed_ref.shape
     blocks = length // BLOCK
     first = lax.broadcasted_iota(jnp.int32, (1, LANES), 1) < HEAD
-    lane = lax.broadcasted_iota(jnp.int32, (BLOCK, LANES), 1)
-    column = lax.broadcasted_iota(jnp.int32, (1, length), 1)
+    key = lax.broadcasted_iota(jnp.int32, (BLOCK, 1), 0)
 
     def one_pair(pair, carry):
         at = lambda part: pl.ds(pl.multiple_of((part * pairs + pair) * LANES, LANES), LANES)
@@ -62,28 +69,34 @@
         for item in range(items):
             keys = qkv_ref[item, :, at(1)]
             values = qkv_ref[item, :, at(2)]
-            valid = column < lens_ref[item]
-            for block in range(blocks):
-                rows = pl.ds(block * BLOCK, BLOCK)
-                queries = qkv_ref[item, rows, at(0)] * scale
-                low = length - block * BLOCK
-                mixed = []
-                stats = jnp.zeros((BLOCK, LANES), f32)
-                for head in range(2):
-                    mine = first if head == 0 else jnp.logical_not(first)
-                    scores = lax.dot_general(jnp.where(mine, queries, 0), keys, NT, preferred_element_type=f32)
-                    scores = jnp.where(valid, scores + biases[head][:, low : low + length], MASK_FILL)
-                    top = jnp.max(scores, axis=1, keepdims=True)
-                    powers = jnp.exp(scores - top)
-                    whole = jnp.sum(powers, axis=1, keepdims=True)
-                    probs = (powers * (1.0 / whole)).astype(bf)
-                    mixed.append(jnp.dot(probs, values, preferred_element_type=f32))
-                    stats = jnp.where(lane == head, top + jnp.log(whole), stats)
-                mixed_ref[item, rows, at(0)] = jnp.where(first, mixed[0], mixed[1]).astype(bf)
-                lse_ref[item, rows, at(0)] = stats
+            mixed = []
+            for head, queries in enumerate(head_halves(qkv_ref[item, :, at(0)] * scale)):
+                top = jnp.full((1, length), MASK_FILL, f32)
+                for block in range(blocks):
+                    rows = slice(block * BLOCK, (block + 1) * BLOCK)
+                    low = length - block * BLOCK
+                    part = lax.dot_general(keys[rows], queries, NT, preferred_element_type=f32)
+                    part = part + biases[head][:, low : low + length]
+                    part = jnp.where(key < lens_ref[item] - block * BLOCK, part, MASK_FILL)
+                    scores[head, rows, :] = part
+                    top = jnp.maximum(top, jnp.max(part, axis=0, keepdims=True))
+                whole = jnp.zeros((1, length), f32)
+                for block in range(blocks):
+                    rows = slice(block * BLOCK, (block + 1) * BLOCK)
+                    part = jnp.exp(scores[head, rows, :] - top)
+                    scores[head, rows, :] = part
+                    whole += jnp.sum(part, axis=0, keepdims=True)
+                share = 1.0 / whole
+                for block in range(blocks):
+                    rows = slice(block * BLOCK, (block + 1) * BLOCK)
+                    probs[head, rows, :] = (scores[head, rows, :] * share).astype(bf)
+                lse_ref[pl.ds(2 * pair + head, 1), item * length : (item + 1) * length] = top + jnp.log(whole)
+                mixed.append(lax.dot_general(probs[head], values, TN, preferred_element_type=f32))
+            mixed_ref[item, :, at(0)] = jnp.where(first, mixed[0], mixed[1]).astype(bf)
         return carry
 
     lax.fori_loop(0, pairs, one_pair, 0)
+
 
 def attend(qkv, lines, lengths):
     items, length, width = qkv.shape
@@ -91,20 +104,31 @@
     pairs = width // LANES
     vm = pl.BlockSpec(memory_space=pltpu.VMEM)
     return pl.pallas_call(
-        functools.partial(attend_kernel, pairs, HEAD ** -0.5),
+        functools.partial(attend_kernel, pairs, HEAD**-0.5),
         in_specs=[pl.BlockSpec(memory_space=pltpu.SMEM), vm, vm],
         out_specs=[vm, vm],
-        out_shape=[jax.ShapeDtypeStruct((items, length, width), bf), jax.ShapeDtypeStruct((items, length, width), f32)],
+        out_shape=[
+            jax.ShapeDtypeStruct((items, length, width), bf),
+            jax.ShapeDtypeStruct((2 * pairs, items * length), f32),
+        ],
+        scratch_shapes=[pltpu.VMEM((2, length, length), f32), pltpu.VMEM((2, length, length), bf)],
         compiler_params=pltpu.CompilerParams(vmem_limit_bytes=40 * 2**20),
-        cost_estimate=pl.CostEstimate(flops=8 * items * length * length * width, bytes_accessed=items * length * width * 12, transcendentals=items * length * length * width // HEAD),
+        cost_estimate=pl.CostEstimate(
+            flops=8 * items * length * length * width,
+            bytes_accessed=items * length * width * 12,
+            transcendentals=items * length * length * width // HEAD,
+        ),
         name="attend",
     )(lengths, lines, qkv)
 
-def attend_back_kernel(pairs, scale, lens_ref, line_ref, qkv_ref, lse_ref, dmix_ref, dqkv_ref, dline_ref, dkey, dval, diag):
+
+def attend_back_kernel(
+    pairs, scale, lens_ref, line_ref, qkv_ref, lse_ref, dmix_ref, dqkv_ref, dline_ref, probs, dprobs, low, diag
+):
     items, length, _ = dmix_ref.shape
     blocks = length // BLOCK
     first = lax.broadcasted_iota(jnp.int32, (1, LANES), 1) < HEAD
-    column = lax.broadcasted_iota(jnp.int32, (1, length), 1)
+    key = lax.broadcasted_iota(jnp.int32, (BLOCK, 1), 0)
 
     def one_pair(pair, carry):
         at = lambda part: pl.ds(pl.multiple_of((part * pairs + pair) * LANES, LANES), LANES)
@@ -113,56 +137,64 @@
         for item in range(items):
             keys = qkv_ref[item, :, at(1)]
             values = qkv_ref[item, :, at(2)]
-            valid = column < lens_ref[item]
-            for block in range(blocks):
-                rows = pl.ds(block * BLOCK, BLOCK)
-                queries = qkv_ref[item, rows, at(0)] * scale
-                given = dmix_ref[item, rows, at(0)]
-                stats = lse_ref[item, rows, at(0)]
-                low = length - block * BLOCK
-                dquery, dkeys, dvals = [], [], []
-                for head in range(2):
-                    mine = first if head == 0 else jnp.logical_not(first)
-                    scores = lax.dot_general(jnp.where(mine, queries, 0), keys, NT, preferred_element_type=f32)
-                    scores = jnp.where(valid, scores + biases[head][:, low : low + length], MASK_FILL)
-                    probs = jnp.exp(scores - stats[:, head : head + 1])
-                    dprobs = lax.dot_general(jnp.where(mine, given, 0), values, NT, preferred_element_type=f32)
-                    inner = jnp.sum(probs * dprobs, axis=1, keepdims=True)
-                    dscores = probs * (dprobs - inner)
-                    diag[head, :, low : low + length] += dscores
-                    low_scores = dscores.astype(bf)
-                    dquery.append(jnp.dot(low_scores, keys, preferred_element_type=f32))
-                    dkeys.append(lax.dot_general(low_scores, queries, TN, preferred_element_type=f32))
-                    dvals.append(lax.dot_general(probs.astype(bf), given, TN, preferred_element_type=f32))
-                dqkv_ref[item, rows, at(0)] = (jnp.where(first, dquery[0], dquery[1]) * scale).astype(bf)
-                dk = jnp.where(first, dkeys[0], dkeys[1])
-                dv = jnp.where(first, dvals[0], dvals[1])
-                if block == 0:
-                    dkey[...] = dk
-                    dval[...] = dv
-                else:
-                    dkey[...] += dk
-                    dval[...] += dv
-            dqkv_ref[item, :, at(1)] = dkey[...].astype(bf)
-            dqkv_ref[item, :, at(2)] = dval[...].astype(bf)
+            queries = qkv_ref[item, :, at(0)] * scale
+            given = dmix_ref[item, :, at(0)]
+            dquery, dkeys, dvals = [], [], []
+            for head, (mine, pulled) in enumerate(zip(head_halves(queries), head_halves(given))):
+                stats = lse_ref[pl.ds(2 * pair + head, 1), item * length : (item + 1) * length]
+                inner = jnp.zeros((1, length), f32)
+                for block in range(blocks):
+                    rows = slice(block * BLOCK, (block + 1) * BLOCK)
+                    start = length - block * BLOCK
+                    part = lax.dot_general(keys[rows], mine, NT, preferred_element_type=f32)
+                    part = jnp.exp(part + biases[head][:, start : start + length] - stats)
+                    part = jnp.where(key < lens_ref[item] - block * BLOCK, part, 0.0)
+                    back = lax.dot_general(values[rows], pulled, NT, preferred_element_type=f32)
+                    probs[head, rows, :] = part
+                    dprobs[head, rows, :] = back
+                    low[head, rows, :] = part.astype(bf)
+                    inner += jnp.sum(part * back, axis=0, keepdims=True)
+                dvals.append(jnp.dot(low[head], given, preferred_element_type=f32))
+                for block in range(blocks):
+                    rows = slice(block * BLOCK, (block + 1) * BLOCK)
+                    start = length - block * BLOCK
+                    part = probs[head, rows, :] * (dprobs[head, rows, :] - inner)
+                    diag[head, :, start : start + length] += part
+                    low[head, rows, :] = part.astype(bf)
+                dkeys.append(jnp.dot(low[head], queries, preferred_element_type=f32))
+                dquery.append(lax.dot_general(low[head], keys, TN, preferred_element_type=f32))
+            dqkv_ref[item, :, at(0)] = (jnp.where(first, dquery[0], dquery[1]) * scale).astype(bf)
+            dqkv_ref[item, :, at(1)] = jnp.where(first, dkeys[0], dkeys[1]).astype(bf)
+            dqkv_ref[item, :, at(2)] = jnp.where(first, dvals[0], dvals[1]).astype(bf)
         for head in range(2):
             dline_ref[pl.ds(2 * pair + head, 1), :] = diagonal_sums(diag[head])
         return carry
 
     lax.fori_loop(0, pairs, one_pair, 0)
+
 
 def attend_back(qkv, lines, lengths, lse, dmixed):
     items, length, width = dmixed.shape
     pairs = width // LANES
     vm = pl.BlockSpec(memory_space=pltpu.VMEM)
+    square = (2, length, length)
     return pl.pallas_call(
-        functools.partial(attend_back_kernel, pairs, HEAD ** -0.5),
+        functools.partial(attend_back_kernel, pairs, HEAD**-0.5),
         in_specs=[pl.BlockSpec(memory_space=pltpu.SMEM), vm, vm, vm, vm],
         out_specs=[vm, vm],
         out_shape=[jax.ShapeDtypeStruct(qkv.shape, bf), jax.ShapeDtypeStruct(lines.shape, f32)],
-        scratch_shapes=[pltpu.VMEM((length, LANES), f32), pltpu.VMEM((length, LANES), f32), pltpu.VMEM((2, BLOCK, 2 * length), f32)],
+        scratch_shapes=[
+            pltpu.VMEM(square, f32),
+            pltpu.VMEM(square, f32),
+            pltpu.VMEM(square, bf),
+            pltpu.VMEM((2, BLOCK, 2 * length), f32),
+        ],
         compiler_params=pltpu.CompilerParams(vmem_limit_bytes=40 * 2**20),
-        cost_estimate=pl.CostEstimate(flops=20 * items * length * length * width, bytes_accessed=items * length * width * 20, transcendentals=items * length * length * width // HEAD),
+        cost_estimate=pl.CostEstimate(
+            flops=20 * items * length * length * width,
+            bytes_accessed=items * length * width * 20,
+            transcendentals=items * length * length * width // HEAD,
+        ),
         name="attend_back",
     )(lengths, lines, qkv, lse, dmixed)
 
@@ -261,43 +293,95 @@
     )(table, ids)
 
 
-def merge_rows(features, batch, ids_row_ref, rows_ref, summed):
-    count = rows_ref.shape[0]
+def stage_ids_kernel(batch, order, place_ref, ids_ref, out_ref, flags_ref, flat):
+    lane = lax.broadcasted_iota(jnp.int32, (1, LANES), 1)
+    count, _, chunk = ids_ref.shape[2:]
+    flat[...] = jnp.zeros_like(flat)
+    for at, (slot, other) in enumerate(order):
+        core = lax.rem(place_ref[0] + other, ids_ref.shape[0])
+        for step in range(count):
+            index = at * count + step
+            ids = ids_ref[core, place_ref[1 + slot], step]
+            out_ref[index] = ids
+            flat[2 * index : 2 * index + 2, :] = ids
+    flags = jnp.zeros((flat.shape[0], LANES), jnp.int32)
+    for block in range(chunk // LANES):
+        part = flat[:, block * LANES : (block + 1) * LANES]
+        found = jnp.zeros(part.shape, jnp.int32)
+        for shift in range(1, batch):
+            again = (part == pltpu.roll(part, shift, 1)) & (lane % batch >= shift)
+            found = jnp.where(again, 1, found)
+        flags = jnp.where(lane == block, jnp.max(found, axis=1, keepdims=True), flags)
+    for index in range(out_ref.shape[0]):
+        flags_ref[index] = flags[2 * index : 2 * index + 2]
+
+
+def stage_ids(place, ids, order, batch=8):
+    *_, count, _, chunk = ids.shape
+    vm = pl.BlockSpec(memory_space=pltpu.VMEM)
+    total = len(order) * count
+    return pl.pallas_call(
+        functools.partial(stage_ids_kernel, batch, order),
+        in_specs=[pl.BlockSpec(memory_space=pltpu.SMEM), vm],
+        out_specs=[vm, vm],
+        out_shape=[
+            jax.ShapeDtypeStruct((total, 2, chunk), jnp.int32),
+            jax.ShapeDtypeStruct((total, 2, LANES), jnp.int32),
+        ],
+        scratch_shapes=[pltpu.VMEM((2 * total + -2 * total % 8, chunk), jnp.int32)],
+        name="stage_ids",
+    )(place, ids)
+
+
+def spread_rows(features, rows_ref, summed):
     whole, rest = split_features(features)
-    place = lax.broadcasted_iota(jnp.int32, (LANES, LANES), 0) // batch
-    same_batch = place == lax.broadcasted_iota(jnp.int32, (LANES, LANES), 1) // batch
     lane = lax.broadcasted_iota(jnp.int32, (1, LANES), 1)
-    for low in range(0, count, LANES):
-        block = slice(low, low + LANES)
-        for half in range(2):
-            across = jnp.broadcast_to(ids_row_ref[0, half : half + 1, block], (LANES, LANES))
-            match = jnp.where((across == across.T) & same_batch, 1.0, 0.0).astype(bf)
-            for tile, start in enumerate(packed_starts(features, half)):
-                if start == whole:
-                    part = jnp.dot(match, rows_ref[block, start : start + 2 * rest], preferred_element_type=f32)
-                    if 2 * rest < LANES:
-                        part = jnp.concatenate([part, jnp.zeros((LANES, LANES - 2 * rest), f32)], axis=1)
-                    mine = lane < rest if half == 0 else (lane >= rest) & (lane < 2 * rest)
-                    part = jnp.where(mine, part, 0.0)
-                else:
-                    part = jnp.dot(match, rows_ref[block, start : start + LANES], preferred_element_type=f32)
-                summed[half][tile][block, :] = part
+    for half in range(2):
+        for tile, start in enumerate(packed_starts(features, half)):
+            if start == whole:
+                part = rows_ref[:, start : start + 2 * rest].astype(f32)
+                if 2 * rest < LANES:
+                    part = jnp.concatenate([part, jnp.zeros((part.shape[0], LANES - 2 * rest), f32)], axis=1)
+                mine = lane < rest if half == 0 else (lane >= rest) & (lane < 2 * rest)
+                part = jnp.where(mine, part, 0.0)
+            else:
+                part = rows_ref[:, start : start + LANES].astype(f32)
+            summed[half][tile][...] = part
+
+
+def merge_rows(batch, ids_row_ref, flags_ref, summed):
+    count = summed[0][0].shape[0]
+    for half in range(2):
+        for at in range(count // LANES):
+            block = slice(at * LANES, (at + 1) * LANES)
+
+            @pl.when(flags_ref[0, half, at] > 0)
+            def _():
+                place = lax.broadcasted_iota(jnp.int32, (LANES, LANES), 0) // batch
+                same_batch = place == lax.broadcasted_iota(jnp.int32, (LANES, LANES), 1) // batch
+                across = jnp.broadcast_to(ids_row_ref[0, half : half + 1, block], (LANES, LANES))
+                match = jnp.where((across == across.T) & same_batch, 1.0, 0.0).astype(bf)
+                for rows in summed[half]:
+                    rows[block, :] = jnp.dot(match, rows[block, :].astype(bf), preferred_element_type=f32)
 
 
 def add_rows(batch, ids_ref, totals, summed):
     count = summed[0][0].shape[0]
-    for half in range(2):
-        def add(index, carry):
-            start = pl.multiple_of(index * batch, batch)
+
+    def add(index, carry):
+        start = pl.multiple_of(index * batch, batch)
+        for half in range(2):
             tokens = [ids_ref[0, half, start + inner] for inner in range(batch)]
-            for total, rows in zip(totals, summed[half]):
-                fresh = [
-                    total[pl.ds(tokens[inner], 1), :] + rows[pl.ds(start + inner, 1), :] for inner in range(batch)
-                ]
+            fresh = [
+                [total[pl.ds(tokens[inner], 1), :] + rows[pl.ds(start + inner, 1), :] for inner in range(batch)]
+                for total, rows in zip(totals, summed[half])
+            ]
+            for total, new in zip(totals, fresh):
                 for inner in range(batch):
-                    total[pl.ds(tokens[inner], 1), :] = fresh[inner]
-            return carry
-        lax.fori_loop(0, count // batch, add, 0)
+                    total[pl.ds(tokens[inner], 1), :] = new[inner]
+        return carry
+
+    lax.fori_loop(0, count // batch, add, 0)
 
 
 def table_columns(features, totals, base, width):
@@ -308,56 +392,93 @@
     return pieces
 
 
-def scatter_kernel(features, scatter_steps, batch, ids_ref, ids_row_ref, rows_ref, out_ref, *scratch):
+class Stage:
+    def __init__(self, segments, choices, ids, flags, first, features):
+        self.arrays = [array for candidates in segments for array in candidates]
+        self.segments = [len(candidates) for candidates in segments]
+        self.chunk = ids.shape[2]
+        self.each = segments[0][0].shape[0] // self.chunk
+        self.steps = self.each * len(segments)
+        self.operands = [choices, ids, ids, flags, *self.arrays]
+        at = lambda s: first + jnp.minimum(s, self.steps - 1)
+        self.in_specs = [
+            pl.BlockSpec(memory_space=pltpu.SMEM),
+            pl.BlockSpec((1, 2, self.chunk), lambda s: (at(s), 0, 0), memory_space=pltpu.SMEM),
+            pl.BlockSpec((1, 2, self.chunk), lambda s: (at(s), 0, 0)),
+            pl.BlockSpec((1, 2, LANES), lambda s: (at(s), 0, 0), memory_space=pltpu.SMEM),
+        ]
+        for segment, candidates in enumerate(segments):
+            for _ in candidates:
+                low = segment * self.each
+                self.in_specs.append(
+                    pl.BlockSpec(
+                        (self.chunk, 2 * features), lambda s, low=low: (jnp.clip(s - low, 0, self.each - 1), 0)
+                    )
+                )
+        self.features = features
+
+    def scratch(self, vocab):
+        tiles = tile_count(self.features)
+        return [pltpu.VMEM((vocab, LANES), f32)] * tiles + [pltpu.VMEM((self.chunk, LANES), f32)] * (2 * tiles)
+
+    def add(self, batch, refs, scratch):
+        choice_ref, ids_ref, ids_row_ref, flags_ref, *rows_refs = refs
+        step = pl.program_id(0)
+        tiles = tile_count(self.features)
+        totals = scratch[:tiles]
+        summed = [scratch[tiles : 2 * tiles], scratch[2 * tiles :]]
+
+        @pl.when(step == 0)
+        def _():
+            for total in totals:
+                total[...] = jnp.zeros_like(total)
+
+        for segment, candidates in enumerate(self.segments):
+            now = (step >= segment * self.each) & (step < (segment + 1) * self.each)
+            for candidate in range(candidates):
+                rows_ref, rows_refs = rows_refs[0], rows_refs[1:]
+
+                @pl.when(now & (choice_ref[segment] == candidate))
+                def _():
+                    spread_rows(self.features, rows_ref, summed)
+
+        @pl.when(step < self.steps)
+        def _():
+            merge_rows(batch, ids_row_ref, flags_ref, summed)
+            add_rows(batch, ids_ref, totals, summed)
+
+        return totals
+
+
+def scatter_kernel(stage, batch, *refs):
+    count = len(stage.operands)
+    out_ref = refs[count]
+    totals = stage.add(batch, refs[:count], refs[count + 1 :])
     step = pl.program_id(0)
     width = out_ref.shape[1]
-    tiles = tile_count(features)
-    totals = scratch[:tiles]
-    summed = [scratch[tiles : 2 * tiles], scratch[2 * tiles :]]
-
-    @pl.when(step == 0)
+
+    @pl.when(step >= stage.steps)
     def _():
-        for total in totals:
-            total[...] = jnp.zeros_like(total)
-
-    @pl.when(step < scatter_steps)
-    def _():
-        merge_rows(features, batch, ids_row_ref, rows_ref, summed)
-        add_rows(batch, ids_ref, totals, summed)
-
-    @pl.when(step >= scatter_steps)
-    def _():
-        base = pl.multiple_of((step - scatter_steps) * width, width)
+        base = pl.multiple_of((step - stage.steps) * width, width)
         low = 0
-        for piece in table_columns(features, totals, base, width):
+        for piece in table_columns(stage.features, totals, base, width):
             out_ref[low : low + piece.shape[0], :] = piece.astype(bf)
             low += piece.shape[0]
 
 
-def scatter_scratch(features, vocab, chunk):
-    tiles = tile_count(features)
-    return [pltpu.VMEM((vocab, LANES), f32)] * tiles + [pltpu.VMEM((chunk, LANES), f32)] * (2 * tiles)
-
-
-def scatter_rows(rows, ids, vocab, features, width=2048, batch=16):
-    steps, _, chunk = ids.shape
+def scatter_rows(stage, vocab, width=2048, batch=8):
     flush = pl.cdiv(vocab, width)
-    at = lambda s: jnp.minimum(s, steps - 1)
     return pl.pallas_call(
-        functools.partial(scatter_kernel, features, steps, batch),
-        grid=(steps + flush,),
-        in_specs=[
-            pl.BlockSpec((1, 2, chunk), lambda s: (at(s), 0, 0), memory_space=pltpu.SMEM),
-            pl.BlockSpec((1, 2, chunk), lambda s: (at(s), 0, 0)),
-            pl.BlockSpec((chunk, 2 * features), lambda s: (at(s), 0)),
-        ],
-        out_specs=pl.BlockSpec((features, width), lambda s: (0, jnp.maximum(s - steps, 0))),
-        out_shape=jax.ShapeDtypeStruct((features, vocab), bf),
-        scratch_shapes=scatter_scratch(features, flush * width, chunk),
-        compiler_params=pltpu.CompilerParams(vmem_limit_bytes=60 * 2**20),
+        functools.partial(scatter_kernel, stage, batch),
+        grid=(stage.steps + flush,),
+        in_specs=stage.in_specs,
+        out_specs=pl.BlockSpec((stage.features, width), lambda s: (0, jnp.maximum(s - stage.steps, 0))),
+        out_shape=jax.ShapeDtypeStruct((stage.features, vocab), bf),
+        scratch_shapes=stage.scratch(flush * width),
+        compiler_params=pltpu.CompilerParams(vmem_limit_bytes=127 * 2**19),
         cost_estimate=pl.CostEstimate(flops=0, bytes_accessed=100 * 2**20, transcendentals=0),
         name="scatter_rows",
-    )(ids, ids, rows)
+    )(*stage.operands)
 
 
 def assemble_kernel(features, spread_ref, gain_ref, embedded_ref, normed_ref):
@@ -433,33 +554,24 @@
     return packed, grad_gain[0]
 
 
-def finish_kernel(features, vocab, scatter_steps, batch, ids_ref, ids_row_ref, rows_ref, weight_ref, first_ref, second_ref, *rest):
-    dense_refs, rest = rest[:3], rest[3:]
-    momentum_ref, variance_ref, direction_ref, squares_ref = rest[:4]
-    scratch = rest[4:]
+def finish_kernel(stage, vocab, batch, *refs):
+    count = len(stage.operands)
+    weight_ref, first_ref, second_ref, *dense_refs = refs[count : count + 6]
+    momentum_ref, variance_ref, direction_ref, squares_ref = refs[count + 6 : count + 10]
+    totals = stage.add(batch, refs[:count], refs[count + 10 :])
     step = pl.program_id(0)
-    tiles = tile_count(features)
-    totals = scratch[:tiles]
-    summed = [scratch[tiles : 2 * tiles], scratch[2 * tiles :]]
 
     @pl.when(step == 0)
     def _():
-        for total in totals:
-            total[...] = jnp.zeros_like(total)
         squares_ref[...] = jnp.zeros_like(squares_ref)
 
-    @pl.when(step < scatter_steps)
-    def _():
-        merge_rows(features, batch, ids_row_ref, rows_ref, summed)
-        add_rows(batch, ids_ref, totals, summed)
-
-    @pl.when(step >= scatter_steps)
+    @pl.when(step >= stage.steps)
     def _():
         width = weight_ref.shape[1]
-        base = pl.multiple_of((step - scatter_steps) * width, width)
+        base = pl.multiple_of((step - stage.steps) * width, width)
         inside = base + lax.broadcasted_iota(jnp.int32, (1, width), 1) < vocab
         low = 0
-        for piece in table_columns(features, totals, base, width):
+        for piece in table_columns(stage.features, totals, base, width):
             cut = slice(low, low + piece.shape[0])
             low += piece.shape[0]
             weight = weight_ref[cut, :]
@@ -475,74 +587,86 @@
                 squares_ref[line : line + 1, :] += jnp.sum(value * value, axis=0, keepdims=True)
 
 
-def finish(rows, ids, weight, first, second, dense, width=1024, batch=16):
+def finish(stage, weight, first, second, dense, width=1024, batch=8):
     features, vocab = weight.shape
-    steps, _, chunk = ids.shape
     columns = pl.cdiv(vocab, width)
-    at = lambda s: jnp.minimum(s, steps - 1)
-    block = pl.BlockSpec((features, width), lambda s: (0, jnp.maximum(s - steps, 0)))
+    block = pl.BlockSpec((features, width), lambda s: (0, jnp.maximum(s - stage.steps, 0)))
     full = jax.ShapeDtypeStruct(weight.shape, f32)
     return pl.pallas_call(
-        functools.partial(finish_kernel, features, vocab, steps, batch),
-        grid=(steps + columns,),
-        in_specs=[
-            pl.BlockSpec((1, 2, chunk), lambda s: (at(s), 0, 0), memory_space=pltpu.SMEM),
-            pl.BlockSpec((1, 2, chunk), lambda s: (at(s), 0, 0)),
-            pl.BlockSpec((chunk, 2 * features), lambda s: (at(s), 0)),
-        ]
-        + [block] * 6,
+        functools.partial(finish_kernel, stage, vocab, batch),
+        grid=(stage.steps + columns,),
+        in_specs=stage.in_specs + [block] * 6,
         out_specs=[block, block, block, pl.BlockSpec((8, width), lambda s: (0, 0))],
         out_shape=[full, full, jax.ShapeDtypeStruct(weight.shape, bf), jax.ShapeDtypeStruct((8, width), f32)],
-        scratch_shapes=scatter_scratch(features, columns * width, chunk),
-        compiler_params=pltpu.CompilerParams(vmem_limit_bytes=62 * 2**20),
+        scratch_shapes=stage.scratch(columns * width),
+        compiler_params=pltpu.CompilerParams(vmem_limit_bytes=127 * 2**19),
         cost_estimate=pl.CostEstimate(flops=0, bytes_accessed=300 * 2**20, transcendentals=0),
         name="finish",
-    )(ids, ids, rows, weight, first, second, *dense)
+    )(*stage.operands, weight, first, second, *dense)
 
 
 MESH = pl.DeviceIdType.MESH
 
 
-def share_kernel(axes, facts_ref, out_ref, send, received):
+def exchange(value_ref, out_ref, mine, peers, send, received, slot):
+    copies = []
+    for peer in peers:
+        copy = pltpu.make_async_remote_copy(
+            src_ref=value_ref,
+            dst_ref=out_ref.at[mine],
+            send_sem=send.at[slot],
+            recv_sem=received.at[slot],
+            device_id=peer,
+            device_id_type=MESH,
+        )
+        copy.start()
+        copies.append(copy)
+        slot += 1
+    return copies
+
+
+def line_peers(axis):
+    place, size = lax.axis_index(axis), lax.axis_size(axis)
+    return place, [{axis: lax.rem(place + step, size)} for step in range(1, size)]
+
+
+def plane_peers(axes):
     places = [lax.axis_index(axis) for axis in axes]
     sizes = [lax.axis_size(axis) for axis in axes]
+    count = sizes[0] * sizes[1]
+    mine = places[0] * sizes[1] + places[1]
+    peers = []
+    for step in range(1, count):
+        peer = lax.rem(mine + step, count)
+        peers.append({axes[0]: peer // sizes[1], axes[1]: lax.rem(peer, sizes[1])})
+    return mine, peers
+
+
+def greet(peers):
     barrier = pltpu.get_barrier_semaphore()
-    for axis, place, size in zip(axes, places, sizes):
-        for step in range(1, size):
-            pl.semaphore_signal(barrier, inc=1, device_id={axis: lax.rem(place + step, size)}, device_id_type=MESH)
-    pl.semaphore_wait(barrier, sum(sizes) - len(sizes))
-    out_ref[places[0], places[1]] = facts_ref[...]
-    slot = 0
-    for axis, place, size in reversed(list(zip(axes, places, sizes))):
-        block = out_ref.at[places[0]] if axis == axes[0] else out_ref.at[places[0], places[1]]
-        copies = []
-        for step in range(1, size):
-            copy = pltpu.make_async_remote_copy(
-                src_ref=block,
-                dst_ref=block,
-                send_sem=send.at[slot],
-                recv_sem=received.at[slot],
-                device_id={axis: lax.rem(place + step, size)},
-                device_id_type=MESH,
-            )
-            copy.start()
-            copies.append(copy)
-            slot += 1
-        for copy in copies:
-            copy.wait()
-
-
-def share_facts(facts, axes, sizes):
-    slots = sum(sizes) - 2
+    for peer in peers:
+        pl.semaphore_signal(barrier, inc=1, device_id=peer, device_id_type=MESH)
+    pl.semaphore_wait(barrier, len(peers))
+
+
+def share_kernel(axis, value_ref, out_ref, send, received):
+    mine, peers = line_peers(axis)
+    greet(peers)
+    out_ref[mine] = value_ref[...]
+    for copy in exchange(value_ref, out_ref, mine, peers, send, received, 0):
+        copy.wait()
+
+
+def share(value, axis, size):
     return pl.pallas_call(
-        functools.partial(share_kernel, axes),
+        functools.partial(share_kernel, axis),
         in_specs=[pl.BlockSpec(memory_space=pltpu.VMEM)],
         out_specs=pl.BlockSpec(memory_space=pltpu.VMEM),
-        out_shape=jax.ShapeDtypeStruct((*sizes, *facts.shape), facts.dtype),
-        scratch_shapes=[pltpu.SemaphoreType.DMA((slots,)), pltpu.SemaphoreType.DMA((slots,))],
+        out_shape=jax.ShapeDtypeStruct((size, *value.shape), value.dtype),
+        scratch_shapes=[pltpu.SemaphoreType.DMA((size - 1,)), pltpu.SemaphoreType.DMA((size - 1,))],
         compiler_params=pltpu.CompilerParams(collective_id=0, has_side_effects=True),
-        name="share_facts",
-    )(facts)
+        name="share",
+    )(value)
 
 
 def sum_squares_kernel(axes, rows_ref, table_ref, out_ref, slots, send, received):
@@ -658,6 +782,36 @@
     )(value)
 
 
+def share_both_kernel(plane, line, vectors_ref, ids_ref, all_vectors_ref, all_ids_ref, send, received):
+    mine, near = plane_peers(plane)
+    place, far = line_peers(line)
+    greet(near + far)
+    all_vectors_ref[mine] = vectors_ref[...]
+    all_ids_ref[place] = ids_ref[...]
+    copies = exchange(vectors_ref, all_vectors_ref, mine, near, send, received, 0)
+    copies += exchange(ids_ref, all_ids_ref, place, far, send, received, len(near))
+    for copy in copies:
+        copy.wait()
+
+
+def share_both(vectors, ids, plane, line, sizes):
+    count = sizes[0] * sizes[1]
+    slots = count - 1 + sizes[2] - 1
+    vm = pl.BlockSpec(memory_space=pltpu.VMEM)
+    return pl.pallas_call(
+        functools.partial(share_both_kernel, plane, line),
+        in_specs=[vm, vm],
+        out_specs=[vm, vm],
+        out_shape=[
+            jax.ShapeDtypeStruct((count, *vectors.shape), vectors.dtype),
+            jax.ShapeDtypeStruct((sizes[2], *ids.shape), ids.dtype),
+        ],
+        scratch_shapes=[pltpu.SemaphoreType.DMA((slots,)), pltpu.SemaphoreType.DMA((slots,))],
+        compiler_params=pltpu.CompilerParams(collective_id=3, has_side_effects=True),
+        name="share_both",
+    )(vectors, ids)
+
+
 def lamb_direction(weight, gradient, moment_one, moment_two):
     momentum = BETA_ONE * moment_one + (1.0 - BETA_ONE) * gradient
     variance = BETA_TWO * moment_two + (1.0 - BETA_TWO) * gradient * gradient
@@ -668,24 +822,118 @@
     return (momentum, variance, direction)
 
 
-def table_update_kernel(squares_ref, weight_ref, direction_ref, updated_ref):
-    norms = jnp.sqrt(squares_ref[0:1, :])
-    rate = LEARN_RATE * norms[:, 0:1] / norms[:, 1:2]
-    updated_ref[...] = weight_ref[...] - rate * direction_ref[...].astype(f32)
-
-
-def table_update(squares, weight, direction, rows=16):
-    features, vocab = weight.shape
-    block = pl.BlockSpec((rows, vocab), lambda s: (s, 0))
+def total_of(value):
+    while value.ndim > 2:
+        value = jnp.sum(value, axis=1)
+    return jnp.sum(jnp.sum(value, axis=1, keepdims=True), axis=0, keepdims=True)
+
+
+def small_moments_kernel(mask_ref, ffn_ref, rest_ref, *refs):
+    grad_refs, inputs, outputs, squares_ref = refs[:2], refs[2:20], refs[20:-1], refs[-1]
+    parts, _, width = inputs[0].shape
+    half = ffn_ref.shape[1] // 2
+    gradient_of = (
+        lambda: jnp.stack([rest_ref[:, part * width : (part + 1) * width] for part in range(parts)]),
+        lambda: rest_ref[:, parts * width :],
+        lambda: ffn_ref[:, half:],
+        lambda: ffn_ref[:, :half],
+        lambda: grad_refs[0][...],
+        lambda: grad_refs[1][...],
+    )
+    lane = lax.broadcasted_iota(jnp.int32, (1, LANES), 1)
+
+    @pl.when(pl.program_id(0) == 0)
+    def _():
+        squares_ref[...] = jnp.zeros_like(squares_ref)
+        squares_ref[0:1, :] = mask_ref[0:1, :]
+
+    def update(place):
+        weight_ref, first_ref, second_ref = inputs[3 * place : 3 * place + 3]
+        weight = weight_ref[...]
+        results = lamb_direction(weight, gradient_of[place]().astype(f32), first_ref[...], second_ref[...])
+        for ref, value in zip(outputs[3 * place : 3 * place + 3], results):
+            ref[...] = value
+        return weight * weight, results[2] * results[2]
+
+    def add(line, weight_square, direction_square):
+        both = jnp.where(lane == 0, weight_square, jnp.where(lane == 1, direction_square, 0.0))
+        squares_ref[line : line + 1, :] += both * mask_ref[line : line + 1, :]
+
+    for place in range(4):
+        weight_square, direction_square = update(place)
+        add(place + 1, total_of(weight_square), total_of(direction_square))
+
+    @pl.when(pl.program_id(0) == 0)
+    def _():
+        weight_square, direction_square = update(4)
+        add(5, total_of(weight_square), total_of(direction_square))
+        weight_square, direction_square = update(5)
+        for row in range(weight_square.shape[0]):
+            add(6 + row, total_of(weight_square[row : row + 1]), total_of(direction_square[row : row + 1]))
+
+
+def row_block(value, steps):
+    if value.ndim == 3:
+        return pl.BlockSpec((value.shape[0], value.shape[1] // steps, value.shape[2]), lambda s: (0, s, 0))
+    return pl.BlockSpec((value.shape[0] // steps, value.shape[1]), lambda s: (s, 0))
+
+
+def whole_block(value):
+    return pl.BlockSpec(value.shape, lambda s: (0,) * value.ndim)
+
+
+def small_moments(mask, weights, gradients, moments, steps):
+    operands = [mask, *gradients]
+    in_specs = [whole_block(mask)] + [row_block(value, steps) for value in operands[1:3]]
+    in_specs += [whole_block(value) for value in operands[3:]]
+    out_specs, out_shape = [], []
+    for place, (weight, states) in enumerate(zip(weights, moments)):
+        spec = row_block(weight, steps) if place < 4 else whole_block(weight)
+        operands += [weight, *states]
+        in_specs += [spec] * 3
+        out_specs += [spec] * 3
+        out_shape += [jax.ShapeDtypeStruct(weight.shape, f32)] * 3
     return pl.pallas_call(
-        table_update_kernel,
-        grid=(features // rows,),
-        in_specs=[pl.BlockSpec(squares.shape, lambda s: (0, 0)), block, block],
-        out_specs=block,
-        out_shape=jax.ShapeDtypeStruct(weight.shape, f32),
-        compiler_params=pltpu.CompilerParams(vmem_limit_bytes=40 * 2**20),
-        name="table_update",
-    )(squares, weight, direction)
+        small_moments_kernel,
+        grid=(steps,),
+        in_specs=in_specs,
+        out_specs=out_specs + [whole_block(mask)],
+        out_shape=out_shape + [jax.ShapeDtypeStruct(mask.shape, f32)],
+        compiler_params=pltpu.CompilerParams(vmem_limit_bytes=127 * 2**19),
+        name="small_moments",
+    )(*operands)
+
+
+def update_all_kernel(squares_ref, *refs):
+    norms = jnp.sqrt(squares_ref[...])
+    rates = LEARN_RATE * norms[:, 0:1] / norms[:, 1:2]
+    count = len(refs) // 3
+    for place in range(count):
+        weight_ref, direction_ref, updated_ref = refs[2 * place], refs[2 * place + 1], refs[2 * count + place]
+        rate = rates[6:9] if place == 6 else rates[place : place + 1]
+        weight = weight_ref[...]
+        if weight.ndim == 3:
+            rate = rate[:, :, None]
+        updated_ref[...] = weight - rate * direction_ref[...].astype(f32)
+
+
+def update_all(squares, weights, directions, steps):
+    operands, in_specs, out_specs, out_shape = [squares], [whole_block(squares)], [], []
+    for place, (weight, direction) in enumerate(zip(weights, directions)):
+        spec = row_block(weight, steps) if place < 5 else whole_block(weight)
+        operands += [weight, direction]
+        in_specs += [spec] * 2
+        out_specs += [spec]
+        out_shape += [jax.ShapeDtypeStruct(weight.shape, f32)]
+    return pl.pallas_call(
+        update_all_kernel,
+        grid=(steps,),
+        in_specs=in_specs,
+        out_specs=out_specs,
+        out_shape=out_shape,
+        compiler_params=pltpu.CompilerParams(vmem_limit_bytes=127 * 2**19),
+        name="update_all",
+    )(*operands)
 
 
 def norm_scale(stream, gain_row):
@@ -703,7 +951,7 @@
 
 
 def bucket_onehot(length):
-    relative = jnp.arange(2 * length, dtype=jnp.int32) - length
+    relative = length - jnp.arange(2 * length, dtype=jnp.int32)
     distance = jnp.abs(relative)
     far_bucket = 8 + sum(((distance >= threshold).astype(jnp.int32) for threshold in BUCKET_EDGES))
     bucket = jnp.where(distance < 8, distance, far_bucket) + jnp.where(relative > 0, 16, 0)
@@ -774,49 +1022,52 @@
     tn = ((0,), (0,))
     nt = ((1,), (1,))
 
-    facts = jnp.concatenate([token_ids, partner[:, None]], axis=1)
-    facts = jnp.pad(facts, ((0, 0), (0, -facts.shape[1] % LANES)))
-    shared = share_facts(facts, ("grp", "dat"), (grp_size, dat_size))
-    all_ids = shared[..., :length].reshape(grp_size, dat_size, mdl_size, 2, chunks, chunk).transpose(2, 0, 1, 4, 3, 5)
-    all_ids = all_ids.reshape(mdl_size, grp_size, dat_size * chunks, 2, chunk)
-    core_ids = lax.dynamic_index_in_dim(all_ids, mdl_index, 0, keepdims=False)
-    other_ids = lax.dynamic_index_in_dim(all_ids, (mdl_index + 1) % mdl_size, 0, keepdims=False)
-    group_partner = lax.dynamic_index_in_dim(shared[..., length], group_index, 0, keepdims=False).reshape(-1)
-    my_lengths = lax.dynamic_slice_in_dim(item_lengths, mdl_index * mine, mine)
-    my_prefixes = lax.dynamic_slice_in_dim(prefix_lengths, mdl_index * mine, mine)
+    group_ids = share(token_ids, "dat", dat_size)
+
+    def of_core(table, core):
+        return lax.dynamic_index_in_dim(table, core % mdl_size, 0, keepdims=False)
+
+    def by_core(ids):
+        lead = ids.shape[:-3]
+        ids = ids.reshape(-1, dat_size, mdl_size, 2, chunks, chunk).transpose(2, 0, 1, 4, 3, 5)
+        return ids.reshape(mdl_size, *lead, dat_size * chunks, 2, chunk)
 
     def gathered(*shards):
         return lax.all_gather(
             jnp.concatenate([shard.astype(bf) for shard in shards], axis=1), "dat", axis=0, tiled=True
         )
 
-    def halves(own):
-        return (own, swap_cores(own))
-
-    first_own = gathered(qkv_weight.reshape(features, -1), out_weight.T)
-    split = qkv_weight.shape[1] * qkv_weight.shape[2]
-    first_halves = halves(first_own)
-    qkv_halves = [part[:, :split] for part in first_halves]
-    out_halves = [part[:, split:] for part in first_halves]
-    up_own = gathered(after(up_weight, first_own))
+    def halves(own, *widths):
+        both = (own, swap_cores(own))
+        edges = [0]
+        for part in widths:
+            edges.append(edges[-1] + part)
+        return [[part[:, low:high] for part in both] for low, high in zip(edges, edges[1:])]
+
+    flat_qkv = qkv_weight.reshape(features, -1)
+    first_own = gathered(flat_qkv, out_weight.T)
     onehot = bucket_onehot(length)
     line_halves = [
         jnp.einsum("rb,bh->hr", onehot, table, precision=MAX_PRECISION)
         for table in (bias_table, swap_cores(bias_table))
     ]
 
-    looked_up = gather_rows(embedding, lax.dynamic_index_in_dim(core_ids, group_index, 0, keepdims=False))
+    looked_up = gather_rows(embedding, of_core(by_core(group_ids), mdl_index))
     spread = lax.all_to_all(
         looked_up.reshape(dat_size, pair_rows, 2 * features), "dat", split_axis=0, concat_axis=0, tiled=True
     )
+    second_own = gathered(after(up_weight, looked_up), after(down_weight, looked_up))
+    item_lengths, prefix_lengths, partner = after((item_lengths, prefix_lengths, partner), looked_up)
+    my_lengths, my_prefixes, my_partner = [
+        lax.dynamic_slice_in_dim(value, mdl_index * mine, mine) for value in (item_lengths, prefix_lengths, partner)
+    ]
     embedded_low, normed_one = assemble(spread, norm_gains[0])
-    down_own = gathered(after(down_weight, embedded_low))
     embedded = embedded_low.astype(f32)
+    qkv_halves, out_halves = halves(after(first_own, spread), flat_qkv.shape[1], out_weight.shape[0])
     qkv_rows = [dot(normed_one, weight).astype(bf).reshape(mine, length, -1) for weight in qkv_halves]
     mixed, log_totals = zip(*[attend(item_qkv, lines, my_lengths) for item_qkv, lines in zip(qkv_rows, line_halves)])
     mixed_rows = [heads.reshape(rows, -1) for heads in mixed]
-    up_halves = halves(after(up_own, mixed[0]))
-    down_halves = halves(after(down_own, mixed[1]))
+    up_halves, down_halves = halves(after(second_own, *mixed), up_weight.shape[1], down_weight.shape[1])
     after_attn = embedded + (dot(mixed_rows[0], out_halves[0], nt) + dot(mixed_rows[1], out_halves[1], nt))
     normed_two_f, norm_two_back = jax.vjp(norm_scale, after_attn, norm_gains[1])
     normed_two = normed_two_f.astype(bf)
@@ -837,7 +1088,14 @@
 
     vectors, tail_back = jax.vjp(pool_tail, after_ffn, norm_gains[2])
 
-    group_vectors = lax.all_gather(vectors, ("dat", "mdl"), axis=0, tiled=True)
+    partner_row = jnp.pad(my_partner.astype(f32), (0, width - mine))[None]
+    plane_facts = jnp.concatenate([vectors, partner_row, jnp.zeros((-(mine + 1) % 8, width), f32)], axis=0)
+    plane_facts, all_ids = share_both(
+        plane_facts, group_ids.reshape(-1, length), ("dat", "mdl"), "grp", (dat_size, mdl_size, grp_size)
+    )
+    group_vectors = plane_facts[:, :mine].reshape(group_items, width)
+    group_partner = plane_facts[:, mine, :mine].reshape(group_items).astype(jnp.int32)
+    all_ids = by_core(all_ids.reshape(grp_size, dat_size, item_count, length))
     live_count = jnp.sum(jnp.where(jnp.arange(grp_size) == group_index, group_live, 0))
     live_total = jnp.sum(group_live).astype(f32)
     slots = jnp.arange(group_items)
@@ -915,11 +1173,24 @@
     )
     loss_total = small[used - 1]
 
+    by_group = arrivals(grp_size)
+    sources = jnp.array([[group] + [found[0] for found in by_group[group]] for group in range(grp_size)], jnp.int32)
+    sources = lax.dynamic_index_in_dim(sources, group_index, 0, keepdims=False)
+    place = jnp.concatenate([mdl_index[None].astype(jnp.int32), sources])
+    order = [(slot, 0) for slot in range(grp_size)]
+    order[-1:] = [(grp_size - 2, 1), (grp_size - 1, 0), (grp_size - 1, 1)]
+    staged_ids, staged_flags = stage_ids(place, after(all_ids, outgoing), order)
+
     outgoing = after(outgoing, part_ffn)
     own_rows = lax.all_to_all(outgoing, "dat", split_axis=0, concat_axis=0, tiled=True)
     own_rows = own_rows.reshape(dat_size * pair_rows, 2 * features)
-    by_group = arrivals(grp_size)
     moving = [[own_rows], [own_rows]]
+    swapped = [[None], [None]]
+
+    def swap(hop, *waits):
+        for way in range(2):
+            both = way == 1 and moving[0][hop] is moving[1][hop]
+            swapped[way].append(swapped[0][hop] if both else swap_cores(after(moving[way][hop], *waits)))
 
     def move(hop, *waits):
         senders = range(hop - 1, grp_size - 1)
@@ -934,104 +1205,78 @@
             moving[0].append(moved)
             moving[1].append(moved)
 
-    def arrived(place):
-        chosen = None
-        for way, hop in sorted({found[place][1:] for found in by_group}):
-            hit = jnp.any(jnp.array([found[place][1:] == (way, hop) for found in by_group])[group_index])
-            chosen = moving[way][hop] if chosen is None else jnp.where(hit, moving[way][hop], chosen)
-        return chosen, jnp.array([found[place][0] for found in by_group], jnp.int32)[group_index]
-
-    def ids_of(table, group):
-        return lax.dynamic_index_in_dim(table, group, 0, keepdims=False)
-
-    def both_rows(part, group):
-        return (
-            jnp.concatenate([part, swap_cores(part)], axis=0),
-            jnp.concatenate([ids_of(core_ids, group), ids_of(other_ids, group)], axis=0),
-        )
-
-    early = [(own_rows, group_index)]
-    move(1)
+    def candidates(slot):
+        found = [by_group[group][slot - 1][1:] for group in range(grp_size)]
+        kinds = sorted(set(found))
+        return kinds, [kinds.index(kind) for kind in found]
+
+    def stage(slots, first, both):
+        segments, picks = [], []
+        for slot in slots:
+            if slot == 0:
+                segments.append([own_rows])
+                picks.append([0] * grp_size)
+                continue
+            kinds, pick = candidates(slot)
+            for buffers in (moving, swapped)[: 1 + both]:
+                segments.append([buffers[way][hop] for way, hop in kinds])
+                picks.append(pick)
+        choices = lax.dynamic_index_in_dim(jnp.array(picks, jnp.int32).T, group_index, 0, keepdims=False)
+        return Stage(segments, choices, staged_ids, staged_flags, first * dat_size * chunks, features)
+
+    move(1, staged_flags)
     for hop in range(2, grp_size - 1):
-        early.append(arrived(hop - 2))
-        move(hop, small, early[-1][0])
-    own_table = scatter_rows(
-        after(jnp.concatenate([part for part, _ in early], axis=0), part_rest, small),
-        jnp.concatenate([ids_of(core_ids, group) for _, group in early], axis=0),
-        vocab,
-        features,
-    )
-    other_table = swap_cores(after(own_table, *[ways[-1] for ways in moving]))
-    late_part, late_group = arrived(grp_size - 3)
-    move(grp_size - 1, own_table, late_part)
-    late_rows, late_ids = both_rows(late_part, late_group)
-    late_table = scatter_rows(late_rows, late_ids, vocab, features)
-    last_part, last_group = arrived(grp_size - 2)
-    last_rows, last_ids = both_rows(after(last_part, late_table), last_group)
-    full_ffn, full_rest = lax.psum((after(part_ffn, moving[0][-1], moving[1][-1]), part_rest), "grp")
+        move(hop, small)
+    early = stage(range(grp_size - 2), 0, False)
+    early.operands[0] = after(early.operands[0], part_rest, small)
+    own_table = scatter_rows(early, vocab)
+    for hop in range(1, grp_size - 1):
+        swap(hop, *((own_table,) if hop == grp_size - 2 else ()))
+    move(grp_size - 1, own_table)
+    late_table = scatter_rows(stage([grp_size - 2], grp_size - 2, True), vocab)
+    other_table = swap_cores(after(own_table, *[ways[-1] for ways in swapped]))
+    swap(grp_size - 1, late_table)
+    last = stage([grp_size - 1], grp_size, True)
+    full_ffn, full_rest = lax.psum((after(part_ffn, late_table), part_rest), "grp")
 
     table_momentum, table_variance, table_direction, table_squares = finish(
-        last_rows,
-        last_ids,
+        last,
         embedding,
         embedding_first,
         embedding_second,
         (own_table, other_table, late_table),
     )
     full_ffn, full_rest = after(full_ffn, table_squares), after(full_rest, table_squares)
-    half = total_down.shape[1]
-    grad_down, grad_up = full_ffn[:, :half].astype(f32), full_ffn[:, half:].astype(f32)
-    half = total_qkv.shape[1]
-    grad_qkv = full_rest[:, :half].astype(f32).reshape(qkv_weight.shape)
-    grad_out = full_rest[:, half:].astype(f32).T
-
-    weights = (qkv_weight, out_weight, up_weight, down_weight, bias_table, norm_gains)
-    gradients = (grad_qkv, grad_out, grad_up, grad_down, grad_bias, grad_gains)
+    by_part = lambda value: value.transpose(1, 0, 2)
+    weights = (by_part(qkv_weight), out_weight.T, up_weight, down_weight, bias_table.T, norm_gains)
+    gradients = (full_ffn, full_rest, grad_bias.T, grad_gains)
     moments = (
-        (qkv_first, qkv_second),
-        (out_first, out_second),
+        (by_part(qkv_first), by_part(qkv_second)),
+        (out_first.T, out_second.T),
         (up_first, up_second),
         (down_first, down_second),
-        (bias_first, bias_second),
+        (bias_first.T, bias_second.T),
         (gains_first, gains_second),
     )
-    results = [
-        lamb_direction(weight, gradient, states[0], states[1])
-        for weight, gradient, states in zip(weights, gradients, moments)
-    ]
     first_mdl = (mdl_index == 0).astype(f32)
     first_dat = (dat_index == 0).astype(f32)
-    holder_mask = [1.0, 1.0, 1.0, 1.0, first_dat]
-    square_rows = [jnp.stack([first_mdl, first_mdl])] + [
-        jnp.stack(
-            [
-                jnp.sum(weights[position] * weights[position]),
-                jnp.sum(results[position][2] * results[position][2]),
-            ]
-        )
-        * holder_mask[position]
-        for position in range(5)
-    ]
-    gain_rows = jnp.stack(
-        [jnp.sum(norm_gains * norm_gains, axis=1), jnp.sum(results[5][2] * results[5][2], axis=1)],
-        axis=1,
-    ) * (first_mdl * first_dat)
-    square_table = jnp.concatenate([jnp.stack(square_rows), gain_rows], axis=0)
-    square_table = jnp.pad(square_table, ((0, 16 - square_table.shape[0]), (0, LANES - 2)))
+    mask = jnp.stack([first_mdl, *[jnp.ones((), f32)] * 4, first_dat, *[first_mdl * first_dat] * 3])
+    mask = jnp.broadcast_to(jnp.pad(mask, (0, 16 - mask.shape[0]))[:, None], (16, LANES))
+    *results, square_table = small_moments(mask, weights, gradients, moments, max(1, features // 48))
     squares = sum_over(table_squares, square_table, ("dat", "mdl"), (dat_size, mdl_size))
-    matrix_norms = jnp.sqrt(squares[:9, :2])
-    rates = LEARN_RATE * matrix_norms[:, 0] / matrix_norms[:, 1]
-    updated = [weights[position] - rates[position + 1] * results[position][2] for position in range(5)]
-    updated.append(norm_gains - rates[6:, None] * results[5][2])
+    updated = update_all(squares, (embedding, *weights), (table_direction, *results[2::3]), features // 16)
     outputs = [
         jnp.stack([loss_total, live_total]),
-        matrix_norms,
+        jnp.sqrt(squares[:9, :2]),
         table_momentum,
         table_variance,
-        table_update(squares, embedding, table_direction),
+        updated[0],
     ]
-    for position in range(6):
-        outputs.extend([results[position][0], results[position][1], updated[position]])
+    outputs.extend(by_part(value) for value in (results[0], results[1], updated[1]))
+    outputs.extend(value.T for value in (results[3], results[4], updated[2]))
+    for position in range(2, 6):
+        three = (results[3 * position], results[3 * position + 1], updated[position + 1])
+        outputs.extend(value.T if position == 4 else value for value in three)
     return tuple(outputs)
 
 

time: 713 us -> 614 us (0.86)
  other arithmetic: 79.7 us -> 23.7 us
  Pallas kernels: 384 us -> 350 us
  waiting for transfers between devices: 69.7 us -> 51.1 us
  blocking collectives: 8.91 us -> 20.9 us
    all_to_all x0 -> x1, blocking collectives: none -> 20.9 us  [shards(): lax.all_to_all(looked_up.reshape(dat_size, pair_rows, 2 * features), 'dat...]
    pallas_call x2, Pallas kernels: 47.1 us -> 27.2 us  [attend_back(): pl.pallas_call(functools.partial(attend_back_kernel, pairs, HEAD ** (-0.5...]
    pallas_call x2, Pallas kernels: 39.1 us -> 19.7 us  [attend(): pl.pallas_call(functools.partial(attend_kernel, pairs, HEAD ** (-0.5)), i...]
    all_to_all x1 -> x0, waiting for transfers between devices: 18.6 us -> none  [shards(): lax.all_to_all(looked_up.reshape(dat_size, pair_rows, 2 * features), 'dat...]
    reduce_sum x5 -> x0, other arithmetic: 13.3 us -> none  [the longest x4 12.6 us: shards(): jnp.sum(weights[position] * weights[position])]
    all_gather x3 -> x2, waiting for transfers between devices: 16.1 us -> 2.88 us  [gathered(): lax.all_gather(jnp.concatenate([shard.astype(bf) for shard in shards], ax...]
    ppermute x11 -> x12, waiting for transfers between devices: 12.6 us -> 23.5 us  [swap_cores(): lax.ppermute(value, 'mdl', [(core, (core + 1) % size) for core in range(s...]
    sub x5 -> x0, other arithmetic: 9.65 us -> none  [the longest x4 8.97 us: shards(): weights[position] - rates[position + 1] * results[position][2]]
  transfers between devices with their start and end apart: 24 -> 23, of which waited for: 4 -> 6; matrix products, arithmetic and copies ran while one was open for 16% -> 15% of each run, Pallas kernels for 49% -> 50%
where the time goes in v3:
time: 614 us; the launch traced here: 604 us
  Pallas kernels  350 us (57%)
  matrix products  89.3 us (15%)
  waiting for transfers between devices  51.1 us (8%)
  starting transfers between devices  33.3 us (5%)
  other arithmetic  23.7 us (4%)
  blocking collectives  20.9 us (3%)
  local copies, waits for them, and re-layouts  19.5 us (3%)
  between operations  16.5 us (3%)
    pallas_call x1, Pallas kernels, finish(): pl.pallas_call(functools.partial(finish_kernel, stage, vocab, batch), gri...  96.1 us
    dot_general x24, matrix products, dot(): lax.dot_general(left, right, (dims, ((), ())), preferred_element_type=f32)  87.1 us
    pallas_call x2, Pallas kernels, scatter_rows(): pl.pallas_call(functools.partial(scatter_kernel, stage, batch), grid=(sta...  86.8 us
    pallas_call x1, Pallas kernels, sum_all(): pl.pallas_call(functools.partial(sum_all_kernel, near, far), in_specs=[pl...  33.9 us
    pallas_call x2, Pallas kernels, attend_back(): pl.pallas_call(functools.partial(attend_back_kernel, pairs, HEAD ** (-0.5...  27.2 us
    pallas_call x1, Pallas kernels, update_all(): pl.pallas_call(update_all_kernel, grid=(steps,), in_specs=in_specs, out_s...  26.3 us
    all_to_all x1, waiting for transfers between devices, shards(): lax.all_to_all(outgoing, 'dat', split_axis=0, concat_axis=0, tiled=True)  24.7 us
    pallas_call x1, Pallas kernels, gather_rows(): pl.pallas_call(functools.partial(gather_kernel, features, load_steps, bat...  24.2 us
  transfers between devices with their start and end apart: 23, of which 6 were waited for; matrix products, arithmetic and copies ran while one was open for 15% of the time, Pallas kernels for 50%

profile of v3, /device:TPU:17, one launch (start us, length us, event | category | flops | bytes accessed | tf_op | source)
XLA Modules:
  0.0 604.4 jit_solution(12316962910129083089)
XLA Ops:
  10.5 4.9 share.1
  16.8 24.2 %gather_rows.1 = bf16[2048,384]{1,0:T(8,128)(2,1)} custom-call(f32[192,32128]{1,0:T(8,128)} %refs_0_.1, s32[4,2,512]{2,1,0:T(2,128)} %dynamic-slice_bitcast_fusion.ids_ref), custom_call_target="tpu_custom_call" | custom-call | bytes 83886080 | tf_op jit(solution)/shard_map/gather_rows/pallas_call | solution.py:280
  43.0 20.9 %all_to_all.10.spread_ref = bf16[4,512,384]{2,1,0:T(8,128)(2,1)S(1)} all-to-all(bf16[4,512,384]{2,1,0:T(8,128)(2,1)S(1)} %bitcast.161), channel_id=1, replica_groups=mesh['grp'=4,'dat'=4,'mdl'=2] {'dat'}, dimensions={0} | all-to-all | bytes 3145728 | tf_op jit(solution)/shard_map/all_to_all | solution.py:1056
  63.9 8.4 %collective-permute-start.1 = (bf16[768,1536]{1,0:T(8,128)(2,1)}, bf16[768,1536]{1,0:T(8,128)(2,1)}, u32[]{:S(2)}, u32[]{:S(2)}) collective-permute-start(bf16[768,1536]{1,0:T(8,128)(2,1)} %all-gather.3.cloned.1.call-done), channel_id=1, source_target_pairs={{0,1},{1,0},{2,3},{3,2},{4,5},{5,4},{6,7},{7,6},{8,9},{9,8},{10,11... | collective-permute-start | bytes 7077896 | tf_op jit(solution)/shard_map/ppermute | solution.py:978
  73.0 3.3 collective-permute-done
  78.7 4.8 convolution_convert_fusion.1
  83.5 9.8 %attend.2 = (bf16[2,512,384]{2,1,0:T(8,128)(2,1)S(1)}, f32[6,1024]{1,0:T(8,128)S(1)}) custom-call(s32[2]{0:T(128)S(1)} %dynamic_slice.25.lens_ref, f32[6,1024]{1,0:T(8,128)S(1)} %convolution_bitcast_fusion.3.line_ref, bf16[2,512,1152]{2,1,0:T(8,128)(2,1)S(1)} %bitcast.148), custom_call_target="tpu_custom_call" | custom-call | flops 1610612736 | bytes 4718592 | tf_op jit(solution)/shard_map/attend/pallas_call | solution.py:106
  93.3 3.9 convolution_convert_fusion
  97.3 9.9 %attend.3 = (bf16[2,512,384]{2,1,0:T(8,128)(2,1)S(1)}, f32[6,1024]{1,0:T(8,128)S(1)}) custom-call(s32[2]{0:T(128)S(1)} %dynamic_slice.25.lens_ref, f32[6,1024]{1,0:T(8,128)S(1)} %convolution_bitcast_fusion.2.line_ref, bf16[2,512,1152]{2,1,0:T(8,128)(2,1)S(1)} %bitcast.150), custom_call_target="tpu_custom_call" | custom-call | flops 1610612736 | bytes 4718592 | tf_op jit(solution)/shard_map/attend/pallas_call | solution.py:106
  123.1 3.8 fusion.34
  126.9 4.3 fusion.30
  131.2 7.5 %multiply_reduce_fusion.3 = (f32[1024]{0:T(1024)S(1)}, f32[1024,768]{1,0:T(8,128)S(1)}) fusion(f32[1024,768]{1,0:T(8,128)S(1)} %get-tuple-element.229, f32[1024,768]{1,0:T(8,128)S(1)} %fusion.34, bf16[768,3072]{1,0:T(8,128)(2,1)} %collective-permute-done.2, f32[1024,1536]{1,0:T(8,128)S(1)} %fusion.30), kind=kOutput, calls=%fused_computation.45 | convolution fusion | flops 2433219584 | bytes 18092032 | tf_op jit(solution)/shard_map/dot_general | solution.py:950
  140.6 7.5 %share_both.1 = (f32[8,8,768]{2,1,0:T(8,128)}, s32[4,16,512]{2,1,0:T(8,128)}) custom-call(f32[8,768]{1,0:T(8,128)} %maximum_maximum_fusion.vectors_ref, s32[16,512]{1,0:T(8,128)} %reshape.318.ids_ref), custom_call_target="tpu_custom_call" | custom-call | tf_op jit(solution)/shard_map/share_both/pallas_call | solution.py:801
  159.3 7.1 %fusion.13 = bf16[1024,1536]{1,0:T(8,128)(2,1)S(1)} fusion(f32[1024,1536]{1,0:T(8,128)S(1)} %copy-done.41, bf16[1024,768]{1,0:T(8,128)(2,1)S(1)} %fusion.42, bf16[768,3072]{1,0:T(8,128)(2,1)} %collective-permute-done.2), kind=kOutput, calls=%fused_computation.17 | convolution fusion | flops 2447376384 | bytes 13369344 | tf_op jit(solution)/shard_map/dot_general | solution.py:950
  171.1 6.3 %fusion.6 = bf16[1024,1536]{1,0:T(8,128)(2,1)S(1)} fusion(f32[1024,1536]{1,0:T(8,128)S(1)} %bitcast.195, bf16[1024,768]{1,0:T(8,128)(2,1)S(1)} %fusion.42, bf16[768,3072]{1,0:T(8,128)(2,1)S(1)} %bitcast.184), kind=kOutput, calls=%fused_computation.10 | convolution fusion | flops 2447376384 | bytes 13369344 | tf_op jit(solution)/shard_map/dot_general | solution.py:950
  186.9 5.4 fusion.38
  192.3 5.0 multiply_reduce_fusion
  201.2 13.4 %attend_back.3 = (bf16[2,512,1152]{2,1,0:T(8,128)(2,1)S(1)}, f32[6,1024]{1,0:T(8,128)S(1)}) custom-call(s32[2]{0:T(128)S(1)} %dynamic_slice.25.lens_ref, f32[6,1024]{1,0:T(8,128)S(1)} %convolution_bitcast_fusion.2.line_ref, bf16[2,512,1152]{2,1,0:T(8,128)(2,1)S(1)} %bitcast.151, f32[6,1024]{1,0:T(8,128)S(1)} %get-tuple-element.105.lse_ref, ...), custom_call_target="tpu_custom_call" | custom-call | flops 4026531840 | bytes 7864320 | tf_op jit(solution)/shard_map/attend_back/pallas_call | solution.py:181
  220.3 13.8 %attend_back.2 = (bf16[2,512,1152]{2,1,0:T(8,128)(2,1)S(1)}, f32[6,1024]{1,0:T(8,128)S(1)}) custom-call(s32[2]{0:T(128)S(1)} %dynamic_slice.25.lens_ref, f32[6,1024]{1,0:T(8,128)S(1)} %convolution_bitcast_fusion.3.line_ref, bf16[2,512,1152]{2,1,0:T(8,128)(2,1)S(1)} %bitcast.149, f32[6,1024]{1,0:T(8,128)S(1)} %get-tuple-element.94.lse_ref, ...), custom_call_target="tpu_custom_call" | custom-call | flops 4026531840 | bytes 7864320 | tf_op jit(solution)/shard_map/attend_back/pallas_call | solution.py:181
  234.1 3.9 fusion.48
  243.0 5.6 convolution_add_fusion
  252.5 3.7 all-to-all-start.1
  260.5 24.7 %all-to-all-done.1 = bf16[4,512,384]{2,1,0:T(8,128)(2,1)S(1)} async-done(((bf16[4,512,384]{2,1,0:T(8,128)(2,1)}), bf16[4,512,384]{2,1,0:T(8,128)(2,1)S(1)}, u32[]{:S(2)}, u32[]{:S(2)}) %all-to-all-start.1) | async-done | bytes 1572896 | tf_op jit(solution)/shard_map/all_to_all | solution.py:1185
  293.0 33.9 %sum_all.1 = f32[24,128]{1,0:T(8,128)} custom-call(f32[24,128]{1,0:T(8,128)} %fusion.64.value_ref), custom_call_target="tpu_custom_call" | custom-call | tf_op jit(solution)/shard_map/sum_all/pallas_call | solution.py:769
  328.8 5.6 collective-permute-start.10
  335.7 42.7 %scatter_rows.2.refs_15_ = bf16[192,32128]{1,0:T(8,128)(2,1)} custom-call(s32[2]{0:T(128)} %fusion.106.refs_0_, s32[24,2,512]{2,1,0:T(2,128)} %get-tuple-element.114.refs_1_.refs_2_, s32[24,2,512]{2,1,0:T(2,128)} %get-tuple-element.114.refs_1_.refs_2_, s32[24,2,128]{2,1,0:T(2,128)} %get-tuple-element.115.refs_3_, bf16[2048,384]{1,0:T(8,128)(2,1)} %bitcast.160, ...), custom_call_target="tpu_custom_call" | custom-call | bytes 104857600 | tf_op jit(solution)/shard_map/scatter_rows/pallas_call | solution.py:471
  392.9 14.6 %collective-permute-done.13.refs_8_ = bf16[2048,384]{1,0:T(8,128)(2,1)} collective-permute-done((bf16[2048,384]{1,0:T(8,128)(2,1)}, bf16[2048,384]{1,0:T(8,128)(2,1)}, u32[]{:S(2)}, u32[]{:S(2)}) %collective-permute-start.13) | collective-permute-done | bytes 1572896 | tf_op jit(solution)/shard_map/ppermute | solution.py:978
  407.4 44.1 %scatter_rows.3.refs_17_ = bf16[192,32128]{1,0:T(8,128)(2,1)} custom-call(s32[2]{0:T(128)} %fusion.107.refs_0_, s32[24,2,512]{2,1,0:T(2,128)} %get-tuple-element.114.refs_1_.refs_2_, s32[24,2,512]{2,1,0:T(2,128)} %get-tuple-element.114.refs_1_.refs_2_, s32[24,2,128]{2,1,0:T(2,128)} %get-tuple-element.115.refs_3_, ...), custom_call_target="tpu_custom_call" | custom-call | bytes 104857600 | tf_op jit(solution)/shard_map/scatter_rows/pallas_call | solution.py:471
  456.5 96.1 %finish.1 = (f32[192,32128]{1,0:T(8,128)}, f32[192,32128]{1,0:T(8,128)}, bf16[192,32128]{1,0:T(8,128)(2,1)}, f32[8,1024]{1,0:T(8,128)}) custom-call(s32[2]{0:T(128)} %fusion.104.refs_0_, s32[24,2,512]{2,1,0:T(2,128)} %get-tuple-element.114.refs_1_.refs_2_, s32[24,2,512]{2,1,0:T(2,128)} %get-tuple-element.114.refs_1_.refs_2_, ...), custom_call_target="tpu_custom_call" | custom-call | bytes 314572800 | tf_op jit(solution)/shard_map/finish/pallas_call | solution.py:595
  553.3 10.7 %small_moments.1 = (f32[3,192,384]{2,1,0:T(8,128)}, f32[3,192,384]{2,1,0:T(8,128)}, f32[3,192,384]{2,1,0:T(8,128)}, f32[192,384]{1,0:T(8,128)}, f32[192,384]{1,0...) custom-call(f32[16,128]{1,0:T(8,128)} %broadcast_in_dim.86.mask_ref,, ...), custom_call_target="tpu_custom_call" | custom-call | tf_op jit(solution)/shard_map/small_moments/pallas_call | solution.py:896
  564.0 6.0 sum_over.1.squares_ref
  571.4 26.3 %update_all.1 = (f32[192,32128]{1,0:T(8,128)}, f32[3,192,384]{2,1,0:T(8,128)}, f32[192,384]{1,0:T(8,128)}, f32[192,1536]{1,0:T(8,128)}, f32[192,1536]{1,0:T(8,128)}, /*index=5*/f32[6,32]{1,0:T(8,128)}, f32[3,768]{1,0:T(4,128)}) custom-call(f32[16,128]{1,0:T(8,128)} %sum_over.1.squares_ref, f32[192,32128]{1,0:T(8,128)} %refs_0_.1, ...), custom_call_target="tpu_custom_call" | custom-call | tf_op jit(solution)/shard_map/update_all/pallas_call | solution.py:928
  (249 shorter events, 105.8 us)
Async XLA Ops:
  7.2 56.7 %all-gather.3.cloned.1.call-start = ((), (), s32[]{:S(2)}) async-start(), calls=%async_computation.4 | async-start | bytes 2949120 | tf_op jit(solution)/shard_map/all_gather | solution.py:1036
  10.4 101.2 %all-gather.5.cloned.1.call-start = ((), (), s32[]{:S(2)}) async-start(), calls=%async_computation.5 | async-start | bytes 5898240 | tf_op jit(solution)/shard_map/all_gather | solution.py:1036
  16.8 24.2 %copy-start.19 = (f32[192,1536]{1,0:T(8,128)S(1)}, f32[192,1536]{1,0:T(8,128)}, u32[]{:S(2)}) copy-start(f32[192,1536]{1,0:T(8,128)} %refs_8_.3) | copy-start | bytes 3538948
  16.8 24.2 %copy-start.20 = (f32[192,1536]{1,0:T(8,128)S(1)}, f32[192,1536]{1,0:T(8,128)}, u32[]{:S(2)}) copy-start(f32[192,1536]{1,0:T(8,128)} %refs_6_.1) | copy-start | bytes 3538948
  41.1 31.2 %copy-start.30 = (f32[32,6]{0,1:T(8,128)S(1)}, f32[32,6]{0,1:T(8,128)}, u32[]{:S(2)}) copy-start(f32[32,6]{0,1:T(8,128)} %param.40) | copy-start | bytes 2308
  41.2 31.7 %copy-start.28 = (f32[3,768]{1,0:T(4,128)S(1)}, f32[3,768]{1,0:T(4,128)}, u32[]{:S(2)}) copy-start(f32[3,768]{1,0:T(4,128)} %refs_12_.5) | copy-start | bytes 27652
  41.2 31.7 %copy-start.34 = (s32[4]{0:T(128)S(1)}, s32[4]{0:T(128)}, u32[]{:S(2)}) copy-start(s32[4]{0:T(128)} %param.31) | copy-start | bytes 52
  42.3 210.1 %reduce-scatter.3.cloned.1.call-start = ((), (), s32[]{:S(2)}) async-start(), calls=%async_computation.6 | async-start | bytes 5898240 | tf_op jit(solution)/shard_map/reduce_scatter | solution.py:1122
  63.9 29.4 %collective-permute-start.1 = (bf16[768,1536]{1,0:T(8,128)(2,1)}, bf16[768,1536]{1,0:T(8,128)(2,1)}, u32[]{:S(2)}, u32[]{:S(2)}) collective-permute-start(bf16[768,1536]{1,0:T(8,128)(2,1)} %all-gather.3.cloned.1.call-done), channel_id=1, source_target_pairs={{0,1},{1,0},{2,3},{3,2},{4,5},{5,4},{6,7},{7,6},{8,9},{9,8},{10,11... | collective-permute-start | bytes 7077896 | tf_op jit(solution)/shard_map/ppermute | solution.py:978
  72.3 4.0 collective-permute-start
  78.7 38.9 %copy-start = (bf16[2,512,768]{2,1,0:T(8,128)(2,1)}, bf16[2,512,768]{2,1,0:T(8,128)(2,1)S(1)}, u32[]{:S(2)}) copy-start(bf16[2,512,768]{2,1,0:T(8,128)(2,1)S(1)} %get-tuple-element.95.embedded_ref) | copy-start | bytes 4718596
  93.3 22.2 %copy-start.5 = (bf16[2,512,384]{2,1,0:T(8,128)(2,1)}, bf16[2,512,384]{2,1,0:T(8,128)(2,1)S(1)}, u32[]{:S(2)}) copy-start(bf16[2,512,384]{2,1,0:T(8,128)(2,1)S(1)} %get-tuple-element.96) | copy-start | bytes 2359300
  111.6 15.3 %collective-permute-start.2 = (bf16[768,3072]{1,0:T(8,128)(2,1)}, bf16[768,3072]{1,0:T(8,128)(2,1)}, u32[]{:S(2)}, u32[]{:S(2)}) collective-permute-start(bf16[768,3072]{1,0:T(8,128)(2,1)} %all-gather.5.cloned.1.call-done), channel_id=1, source_target_pairs={{0,1},{1,0},{2,3},{3,2},{4,5},{5,4},{6,7},{7,6},{8,9},{9,8},{10,11... | collective-permute-start | bytes 14155784 | tf_op jit(solution)/shard_map/ppermute | solution.py:978
  158.3 19.2 %collective-permute-start.5 = (bf16[768,1536]{1,0:T(8,128)(2,1)S(1)}, bf16[768,1536]{1,0:T(8,128)(2,1)S(1)}, u32[]{:S(2)}, u32[]{:S(2)}) collective-permute-start(bf16[768,1536]{1,0:T(8,128)(2,1)S(1)} %convolution_convert_fusion.3), channel_id=1, source_target_pairs={{0,1},{1,0},{2,3},{3,2},{4,5},{5,4},{6,7},{7,6},{8,9},{9,8},{10,11... | collective-permute-start | bytes 7077896 | tf_op jit(solution)/shard_map/ppermute | solution.py:978
  171.0 9.8 %collective-permute-start.6 = (bf16[768,1536]{1,0:T(8,128)(2,1)S(1)}, bf16[768,1536]{1,0:T(8,128)(2,1)S(1)}, u32[]{:S(2)}, u32[]{:S(2)}) collective-permute-start(bf16[768,1536]{1,0:T(8,128)(2,1)S(1)} %convolution_convert_fusion.2), channel_id=1, source_target_pairs={{0,1},{1,0},{2,3},{3,2},{4,5},{5,4},{6,7},{7,6},{8,9},{9,8},{10,11... | collective-permute-start | bytes 7077896 | tf_op jit(solution)/shard_map/ppermute | solution.py:978
  186.8 148.9 %reduce-scatter.5.cloned.1.call-start = ((), (), s32[]{:S(2)}) async-start(), calls=%async_computation.7 | async-start | bytes 2949120 | tf_op jit(solution)/shard_map/reduce_scatter | solution.py:1122
  216.9 22.1 %collective-permute-start.3 = (bf16[768,1152]{1,0:T(8,128)(2,1)S(1)}, bf16[768,1152]{1,0:T(8,128)(2,1)S(1)}, u32[]{:S(2)}, u32[]{:S(2)}) collective-permute-start(bf16[768,1152]{1,0:T(8,128)(2,1)S(1)} %fusion.14), channel_id=1, source_target_pairs={{0,1},{1,0},{2,3},{3,2},{4,5},{5,4},{6,7},{7,6},{8,9},{9,8},{10,11... | collective-permute-start | bytes 5308424 | tf_op jit(solution)/shard_map/ppermute | solution.py:978
  218.6 19.4 %collective-permute-start.4 = (bf16[768,384]{1,0:T(8,128)(2,1)S(1)}, bf16[768,384]{1,0:T(8,128)(2,1)S(1)}, u32[]{:S(2)}, u32[]{:S(2)}) collective-permute-start(bf16[768,384]{1,0:T(8,128)(2,1)S(1)} %convolution_convert_fusion.6), channel_id=1, source_target_pairs={{0,1},{1,0},{2,3},{3,2},{4,5},{5,4},{6,7},{7,6},{8,9},{9,8},{10,11... | collective-permute-start | bytes 1769480 | tf_op jit(solution)/shard_map/ppermute | solution.py:978
  252.5 38.2 %copy-start.32 = (s32[1024]{0:T(1024)S(1)}, s32[1024]{0:T(1024)}, u32[]{:S(2)}) copy-start(s32[1024]{0:T(1024)} %copy-done.31) | copy-start | bytes 12292
  252.5 32.7 %all-to-all-start.1 = ((bf16[4,512,384]{2,1,0:T(8,128)(2,1)}), bf16[4,512,384]{2,1,0:T(8,128)(2,1)S(1)}, u32[]{:S(2)}, u32[]{:S(2)}) async-start(bf16[4,512,384]{2,1,0:T(8,128)(2,1)} %copy-done.2), calls=%async_computation.2 | async-start | bytes 3145728 | tf_op jit(solution)/shard_map/all_to_all | solution.py:1185
  256.2 296.5 %all-reduce.6.cloned.1.call-start = ((), (), s32[]{:S(2)}) async-start(), calls=%async_computation.8 | async-start | bytes 3538944 | tf_op jit(solution)/shard_map/psum | solution.py:1240
  285.2 41.7 %collective-permute-start.7 = (bf16[2048,384]{1,0:T(8,128)(2,1)S(1)}, bf16[2048,384]{1,0:T(8,128)(2,1)}, u32[]{:S(2)}, u32[]{:S(2)}) collective-permute-start(bf16[2048,384]{1,0:T(8,128)(2,1)S(1)} %bitcast.158), channel_id=1, source_target_pairs={{0,8},{8,16},{16,24},{1,9},{9,17},{17,25},{2,10},{10,18},{18,26},{... | collective-permute-start | bytes 4718600 | tf_op jit(solution)/shard_map/ppermute | solution.py:1201
  288.2 40.6 %collective-permute-start.9 = (bf16[2048,384]{1,0:T(8,128)(2,1)S(1)}, bf16[2048,384]{1,0:T(8,128)(2,1)}, u32[]{:S(2)}, u32[]{:S(2)}) collective-permute-start(bf16[2048,384]{1,0:T(8,128)(2,1)S(1)} %bitcast.159), channel_id=1, source_target_pairs={{24,16},{16,8},{8,0},{25,17},{17,9},{9,1},{26,18},{18,10},{10,2},{... | collective-permute-start | bytes 4718600 | tf_op jit(solution)/shard_map/ppermute | solution.py:1201
  326.9 51.4 %collective-permute-start.8 = (bf16[2048,384]{1,0:T(8,128)(2,1)}, bf16[2048,384]{1,0:T(8,128)(2,1)}, u32[]{:S(2)}, u32[]{:S(2)}) collective-permute-start(bf16[2048,384]{1,0:T(8,128)(2,1)} %collective-permute-done.7.refs_5_), channel_id=1, source_target_pairs={{8,16},{16,24},{9,17},{17,25},{10,18},{18,26},{11,19},{19,27},{12,... | collective-permute-start | bytes 4718600 | tf_op jit(solution)/shard_map/ppermute | solution.py:1201
  328.8 51.6 %collective-permute-start.10 = (bf16[2048,384]{1,0:T(8,128)(2,1)}, bf16[2048,384]{1,0:T(8,128)(2,1)}, u32[]{:S(2)}, u32[]{:S(2)}) collective-permute-start(bf16[2048,384]{1,0:T(8,128)(2,1)} %collective-permute-done.9.refs_6_.refs_5_), channel_id=1, source_target_pairs={{16,8},{8,0},{17,9},{9,1},{18,10},{10,2},{19,11},{11,3},{20,12},{1... | collective-permute-start | bytes 4718600 | tf_op jit(solution)/shard_map/ppermute | solution.py:1201
  378.3 5.4 collective-permute-start.12
  380.4 5.6 collective-permute-start.14
  386.0 70.5 %collective-permute-start.16 = (bf16[192,32128]{1,0:T(8,128)(2,1)}, bf16[192,32128]{1,0:T(8,128)(2,1)}, u32[]{:S(2)}, u32[]{:S(2)}) collective-permute-start(bf16[192,32128]{1,0:T(8,128)(2,1)} %scatter_rows.2.refs_15_), channel_id=1, source_target_pairs={{0,1},{1,0},{2,3},{3,2},{4,5},{5,4},{6,7},{7,6},{8,9},{9,8},{10,11... | collective-permute-start | bytes 37011464 | tf_op jit(solution)/shard_map/ppermute | solution.py:978
  386.4 21.0 %collective-permute-start.13 = (bf16[2048,384]{1,0:T(8,128)(2,1)}, bf16[2048,384]{1,0:T(8,128)(2,1)}, u32[]{:S(2)}, u32[]{:S(2)}) collective-permute-start(bf16[2048,384]{1,0:T(8,128)(2,1)} %collective-permute-done.9.refs_6_.refs_5_), channel_id=1, source_target_pairs={{0,1},{1,0},{2,3},{3,2},{4,5},{5,4},{6,7},{7,6},{8,9},{9,8},{10,11... | collective-permute-start | bytes 4718600 | tf_op jit(solution)/shard_map/ppermute | solution.py:978
  389.3 62.3 %collective-permute-start.11 = (bf16[2048,384]{1,0:T(8,128)(2,1)}, bf16[2048,384]{1,0:T(8,128)(2,1)}, u32[]{:S(2)}, u32[]{:S(2)}) collective-permute-start(bf16[2048,384]{1,0:T(8,128)(2,1)} %broadcast_select_fusion), channel_id=1, source_target_pairs={{16,24},{8,0},{17,25},{9,1},{18,26},{10,2},{19,27},{11,3},{20,28},... | collective-permute-start | bytes 4718600 | tf_op jit(solution)/shard_map/ppermute | solution.py:1204
  392.9 60.4 %copy-start.29 = (f32[24,128]{1,0:T(8,128)S(1)}, f32[24,128]{1,0:T(8,128)}, u32[]{:S(2)}) copy-start(f32[24,128]{1,0:T(8,128)} %sum_all.1) | copy-start | bytes 36868
  451.6 4.9 collective-permute-start.15
  (40 other events, 310.9 us)
Sparse Core Ops, SparseCore 0:
  10.5 38.5 all-gather.2
  51.5 60.0 all-gather.4
  186.9 57.0 reduce-scatter.2
  246.9 53.7 reduce-scatter.4
  451.7 73.6 all-reduce.5

commit v4 on v3

--- a/solution.py
+++ b/solution.py
@@ -261,7 +261,7 @@
                     for inner in range(batch):
                         rows[half][tile][pl.ds(start + inner, 1), :] = stash[tile][pl.ds(tokens[inner], 1), :]
                 return carry
-            lax.fori_loop(0, count // batch, take, 0)
+            lax.fori_loop(0, count // batch, take, 0, unroll=2)
         for half in range(2):
             for tile in range(whole // LANES):
                 low = packed_starts(features, half)[tile]
@@ -316,7 +316,7 @@
         flags_ref[index] = flags[2 * index : 2 * index + 2]
 
 
-def stage_ids(place, ids, order, batch=8):
+def stage_ids(place, ids, order, batch=4):
     *_, count, _, chunk = ids.shape
     vm = pl.BlockSpec(memory_space=pltpu.VMEM)
     total = len(order) * count
@@ -381,7 +381,7 @@
                     total[pl.ds(tokens[inner], 1), :] = new[inner]
         return carry
 
-    lax.fori_loop(0, count // batch, add, 0)
+    lax.fori_loop(0, count // batch, add, 0, unroll=4)
 
 
 def table_columns(features, totals, base, width):
@@ -450,10 +450,11 @@
         return totals
 
 
-def scatter_kernel(stage, batch, *refs):
+def scatter_kernel(stage, batch, dense, *refs):
     count = len(stage.operands)
-    out_ref = refs[count]
-    totals = stage.add(batch, refs[:count], refs[count + 1 :])
+    dense_refs = refs[count : count + dense]
+    out_ref = refs[count + dense]
+    totals = stage.add(batch, refs[:count], refs[count + dense + 1 :])
     step = pl.program_id(0)
     width = out_ref.shape[1]
 
@@ -462,23 +463,27 @@
         base = pl.multiple_of((step - stage.steps) * width, width)
         low = 0
         for piece in table_columns(stage.features, totals, base, width):
-            out_ref[low : low + piece.shape[0], :] = piece.astype(bf)
+            cut = slice(low, low + piece.shape[0])
             low += piece.shape[0]
-
-
-def scatter_rows(stage, vocab, width=2048, batch=8):
+            for dense_ref in dense_refs:
+                piece = piece + dense_ref[cut, :].astype(f32)
+            out_ref[cut, :] = piece.astype(bf)
+
+
+def scatter_rows(stage, vocab, dense=(), width=2048, batch=4):
     flush = pl.cdiv(vocab, width)
+    block = pl.BlockSpec((stage.features, width), lambda s: (0, jnp.maximum(s - stage.steps, 0)))
     return pl.pallas_call(
-        functools.partial(scatter_kernel, stage, batch),
+        functools.partial(scatter_kernel, stage, batch, len(dense)),
         grid=(stage.steps + flush,),
-        in_specs=stage.in_specs,
-        out_specs=pl.BlockSpec((stage.features, width), lambda s: (0, jnp.maximum(s - stage.steps, 0))),
+        in_specs=stage.in_specs + [block] * len(dense),
+        out_specs=block,
         out_shape=jax.ShapeDtypeStruct((stage.features, vocab), bf),
         scratch_shapes=stage.scratch(flush * width),
         compiler_params=pltpu.CompilerParams(vmem_limit_bytes=127 * 2**19),
         cost_estimate=pl.CostEstimate(flops=0, bytes_accessed=100 * 2**20, transcendentals=0),
         name="scatter_rows",
-    )(*stage.operands)
+    )(*stage.operands, *dense)
 
 
 def assemble_kernel(features, spread_ref, gain_ref, embedded_ref, normed_ref):
@@ -554,11 +559,12 @@
     return packed, grad_gain[0]
 
 
-def finish_kernel(stage, vocab, batch, *refs):
+def finish_kernel(stage, vocab, batch, dense, *refs):
     count = len(stage.operands)
-    weight_ref, first_ref, second_ref, *dense_refs = refs[count : count + 6]
-    momentum_ref, variance_ref, direction_ref, squares_ref = refs[count + 6 : count + 10]
-    totals = stage.add(batch, refs[:count], refs[count + 10 :])
+    weight_ref, first_ref, second_ref, *dense_refs = refs[count : count + 3 + dense]
+    refs, scratch = refs[: count + 7 + dense], refs[count + 7 + dense :]
+    momentum_ref, variance_ref, direction_ref, squares_ref = refs[-4:]
+    totals = stage.add(batch, refs[:count], scratch)
     step = pl.program_id(0)
 
     @pl.when(step == 0)
@@ -587,15 +593,15 @@
                 squares_ref[line : line + 1, :] += jnp.sum(value * value, axis=0, keepdims=True)
 
 
-def finish(stage, weight, first, second, dense, width=1024, batch=8):
+def finish(stage, weight, first, second, dense, width=1024, batch=4):
     features, vocab = weight.shape
     columns = pl.cdiv(vocab, width)
     block = pl.BlockSpec((features, width), lambda s: (0, jnp.maximum(s - stage.steps, 0)))
     full = jax.ShapeDtypeStruct(weight.shape, f32)
     return pl.pallas_call(
-        functools.partial(finish_kernel, stage, vocab, batch),
+        functools.partial(finish_kernel, stage, vocab, batch, len(dense)),
         grid=(stage.steps + columns,),
-        in_specs=stage.in_specs + [block] * 6,
+        in_specs=stage.in_specs + [block] * (3 + len(dense)),
         out_specs=[block, block, block, pl.BlockSpec((8, width), lambda s: (0, 0))],
         out_shape=[full, full, jax.ShapeDtypeStruct(weight.shape, bf), jax.ShapeDtypeStruct((8, width), f32)],
         scratch_shapes=stage.scratch(columns * width),
@@ -828,24 +834,41 @@
     return jnp.sum(jnp.sum(value, axis=1, keepdims=True), axis=0, keepdims=True)
 
 
-def small_moments_kernel(mask_ref, ffn_ref, rest_ref, *refs):
-    grad_refs, inputs, outputs, squares_ref = refs[:2], refs[2:20], refs[20:-1], refs[-1]
+def small_moments_kernel(ffn_ref, rest_ref, small_ref, *refs):
+    inputs, outputs, squares_ref = refs[:18], refs[18:-1], refs[-1]
     parts, _, width = inputs[0].shape
     half = ffn_ref.shape[1] // 2
+    heads, buckets = inputs[12].shape
+    gains, model = inputs[15].shape
+    lines = model // LANES
+    first_mdl, first_dat = lax.axis_index("mdl") == 0, lax.axis_index("dat") == 0
+
+    def bias_gradient():
+        start = gains * lines
+        own = [small_ref[start + core * heads : start + (core + 1) * heads, :buckets] for core in range(HEADS // heads)]
+        return functools.reduce(
+            lambda kept, at: jnp.where(lax.axis_index("mdl") == at, own[at], kept), range(1, len(own)), own[0]
+        )
+
+    def gain_gradient():
+        rows = [[small_ref[gain * lines + at : gain * lines + at + 1, :] for at in range(lines)] for gain in range(gains)]
+        return jnp.concatenate([jnp.concatenate(row, axis=1) for row in rows], axis=0)
+
     gradient_of = (
         lambda: jnp.stack([rest_ref[:, part * width : (part + 1) * width] for part in range(parts)]),
         lambda: rest_ref[:, parts * width :],
         lambda: ffn_ref[:, half:],
         lambda: ffn_ref[:, :half],
-        lambda: grad_refs[0][...],
-        lambda: grad_refs[1][...],
+        bias_gradient,
+        gain_gradient,
     )
     lane = lax.broadcasted_iota(jnp.int32, (1, LANES), 1)
+    counted = [first_mdl, True, True, True, True, first_dat] + [first_mdl & first_dat] * 3
 
     @pl.when(pl.program_id(0) == 0)
     def _():
         squares_ref[...] = jnp.zeros_like(squares_ref)
-        squares_ref[0:1, :] = mask_ref[0:1, :]
+        squares_ref[0:1, :] = jnp.where(counted[0], jnp.ones((1, LANES), f32), 0.0)
 
     def update(place):
         weight_ref, first_ref, second_ref = inputs[3 * place : 3 * place + 3]
@@ -857,7 +880,7 @@
 
     def add(line, weight_square, direction_square):
         both = jnp.where(lane == 0, weight_square, jnp.where(lane == 1, direction_square, 0.0))
-        squares_ref[line : line + 1, :] += both * mask_ref[line : line + 1, :]
+        squares_ref[line : line + 1, :] += jnp.where(counted[line], both, 0.0)
 
     for place in range(4):
         weight_square, direction_square = update(place)
@@ -882,10 +905,9 @@
     return pl.BlockSpec(value.shape, lambda s: (0,) * value.ndim)
 
 
-def small_moments(mask, weights, gradients, moments, steps):
-    operands = [mask, *gradients]
-    in_specs = [whole_block(mask)] + [row_block(value, steps) for value in operands[1:3]]
-    in_specs += [whole_block(value) for value in operands[3:]]
+def small_moments(weights, gradients, moments, steps):
+    operands = [*gradients]
+    in_specs = [row_block(value, steps) for value in operands[:2]] + [whole_block(operands[2])]
     out_specs, out_shape = [], []
     for place, (weight, states) in enumerate(zip(weights, moments)):
         spec = row_block(weight, steps) if place < 4 else whole_block(weight)
@@ -897,8 +919,8 @@
         small_moments_kernel,
         grid=(steps,),
         in_specs=in_specs,
-        out_specs=out_specs + [whole_block(mask)],
-        out_shape=out_shape + [jax.ShapeDtypeStruct(mask.shape, f32)],
+        out_specs=out_specs + [pl.BlockSpec((16, LANES), lambda s: (0, 0))],
+        out_shape=out_shape + [jax.ShapeDtypeStruct((16, LANES), f32)],
         compiler_params=pltpu.CompilerParams(vmem_limit_bytes=127 * 2**19),
         name="small_moments",
     )(*operands)
@@ -1149,29 +1171,20 @@
     part_rest = scattered(total_rest)
 
     grad_bias_own, grad_bias_other = [
-        jnp.einsum("rb,hr->bh", onehot, grad, precision=MAX_PRECISION) for grad in grad_lines
+        jnp.einsum("rb,hr->hb", onehot, grad, precision=MAX_PRECISION) for grad in grad_lines
     ]
     grad_bias_all = jnp.where(
         mdl_index == 0,
-        jnp.concatenate([grad_bias_own, grad_bias_other], axis=1),
-        jnp.concatenate([grad_bias_other, grad_bias_own], axis=1),
+        jnp.concatenate([grad_bias_own, grad_bias_other], axis=0),
+        jnp.concatenate([grad_bias_other, grad_bias_own], axis=0),
     )
     leader = ((dat_index == 0) & (mdl_index == 0)).astype(f32)
+    gain_lines = jnp.stack([grad_gain_one, grad_gain_two, grad_gain_three]).reshape(-1, LANES)
+    loss_line = jnp.full((1, LANES), loss_part * leader)
     small = jnp.concatenate(
-        [
-            jnp.stack([grad_gain_one, grad_gain_two, grad_gain_three]).reshape(-1),
-            grad_bias_all.reshape(-1),
-            (loss_part * leader).reshape(1),
-        ]
+        [gain_lines, jnp.pad(grad_bias_all, ((0, 0), (0, LANES - BUCKETS))), loss_line], axis=0
     )
-    used = small.shape[0]
-    small = after(jnp.pad(small, (0, -used % (8 * LANES))).reshape(-1, LANES), total_rest)
-    small = sum_all(small, ("dat", "mdl"), "grp", (dat_size, mdl_size, grp_size)).reshape(-1)
-    grad_gains = small[: 3 * width].reshape(3, width)
-    grad_bias = lax.dynamic_slice_in_dim(
-        small[3 * width : used - 1].reshape(BUCKETS, -1), mdl_index * bias_table.shape[1], bias_table.shape[1], axis=1
-    )
-    loss_total = small[used - 1]
+    small = jnp.pad(small, ((0, -small.shape[0] % 8), (0, 0)))
 
     by_group = arrivals(grp_size)
     sources = jnp.array([[group] + [found[0] for found in by_group[group]] for group in range(grp_size)], jnp.int32)
@@ -1225,20 +1238,21 @@
         return Stage(segments, choices, staged_ids, staged_flags, first * dat_size * chunks, features)
 
     move(1, staged_flags)
+    first_table = scatter_rows(stage([0], 0, False), vocab)
+    small = sum_all(after(small, first_table), ("dat", "mdl"), "grp", (dat_size, mdl_size, grp_size))
     for hop in range(2, grp_size - 1):
         move(hop, small)
-    early = stage(range(grp_size - 2), 0, False)
-    early.operands[0] = after(early.operands[0], part_rest, small)
-    own_table = scatter_rows(early, vocab)
-    for hop in range(1, grp_size - 1):
-        swap(hop, *((own_table,) if hop == grp_size - 2 else ()))
+        swap(hop - 1)
+    early = stage(range(1, grp_size - 2), 1, False)
+    early.operands[0] = after(early.operands[0], part_rest)
+    own_table = scatter_rows(early, vocab, (first_table,))
+    swap(grp_size - 2, own_table)
     move(grp_size - 1, own_table)
+    other_table = swap_cores(after(own_table, *[kept for way in swapped for kept in way[1:]]))
     late_table = scatter_rows(stage([grp_size - 2], grp_size - 2, True), vocab)
-    other_table = swap_cores(after(own_table, *[ways[-1] for ways in swapped]))
     swap(grp_size - 1, late_table)
     last = stage([grp_size - 1], grp_size, True)
     full_ffn, full_rest = lax.psum((after(part_ffn, late_table), part_rest), "grp")
-
     table_momentum, table_variance, table_direction, table_squares = finish(
         last,
         embedding,
@@ -1247,9 +1261,10 @@
         (own_table, other_table, late_table),
     )
     full_ffn, full_rest = after(full_ffn, table_squares), after(full_rest, table_squares)
+    loss_total = small[gain_lines.shape[0] + HEADS, 0]
     by_part = lambda value: value.transpose(1, 0, 2)
     weights = (by_part(qkv_weight), out_weight.T, up_weight, down_weight, bias_table.T, norm_gains)
-    gradients = (full_ffn, full_rest, grad_bias.T, grad_gains)
+    gradients = (full_ffn, full_rest, small)
     moments = (
         (by_part(qkv_first), by_part(qkv_second)),
         (out_first.T, out_second.T),
@@ -1258,11 +1273,7 @@
         (bias_first.T, bias_second.T),
         (gains_first, gains_second),
     )
-    first_mdl = (mdl_index == 0).astype(f32)
-    first_dat = (dat_index == 0).astype(f32)
-    mask = jnp.stack([first_mdl, *[jnp.ones((), f32)] * 4, first_dat, *[first_mdl * first_dat] * 3])
-    mask = jnp.broadcast_to(jnp.pad(mask, (0, 16 - mask.shape[0]))[:, None], (16, LANES))
-    *results, square_table = small_moments(mask, weights, gradients, moments, max(1, features // 48))
+    *results, square_table = small_moments(weights, gradients, moments, max(1, features // 48))
     squares = sum_over(table_squares, square_table, ("dat", "mdl"), (dat_size, mdl_size))
     updated = update_all(squares, (embedding, *weights), (table_direction, *results[2::3]), features // 16)
     outputs = [

time: 614 us -> 578 us (0.941)
  Pallas kernels: 350 us -> 326 us
  waiting for transfers between devices: 51.1 us -> 38.6 us
    pallas_call x1, Pallas kernels: 33.9 us -> 9.8 us  [sum_all(): pl.pallas_call(functools.partial(sum_all_kernel, near, far), in_specs=[pl...]
    ppermute x12, waiting for transfers between devices: 23.5 us -> 8.99 us  [swap_cores(): lax.ppermute(value, 'mdl', [(core, (core + 1) % size) for core in range(s...]
    pallas_call x3 -> x4, Pallas kernels: 183 us -> 184 us  [the longest x3 93.8 us: scatter_rows(): pl.pallas_call(functools.partial(scatter_kernel, stage, batch, len(dense)...]
  transfers between devices with their start and end apart: 23 -> 23, of which waited for: 6 -> 6; matrix products, arithmetic and copies ran while one was open for 15% -> 16% of each run, Pallas kernels for 50% -> 48%
where the time goes in v4:
time: 578 us; the launch traced here: 568 us
  Pallas kernels  326 us (56%)
  matrix products  89.3 us (15%)
  waiting for transfers between devices  38.6 us (7%)
  starting transfers between devices  34.2 us (6%)
  other arithmetic  23.3 us (4%)
  blocking collectives  22.3 us (4%)
  local copies, waits for them, and re-layouts  17.8 us (3%)
  between operations  16.5 us (3%)
    pallas_call x3, Pallas kernels, scatter_rows(): pl.pallas_call(functools.partial(scatter_kernel, stage, batch, len(dense)...  93.8 us
    pallas_call x1, Pallas kernels, finish(): pl.pallas_call(functools.partial(finish_kernel, stage, vocab, batch, len(...  90 us
    dot_general x24, matrix products, dot(): lax.dot_general(left, right, (dims, ((), ())), preferred_element_type=f32)  87.1 us
    pallas_call x2, Pallas kernels, attend_back(): pl.pallas_call(functools.partial(attend_back_kernel, pairs, HEAD ** (-0.5...  27 us
    pallas_call x1, Pallas kernels, update_all(): pl.pallas_call(update_all_kernel, grid=(steps,), in_specs=in_specs, out_s...  26.3 us
    all_to_all x1, waiting for transfers between devices, shards(): lax.all_to_all(outgoing, 'dat', split_axis=0, concat_axis=0, tiled=True)  24.4 us
    pallas_call x1, Pallas kernels, gather_rows(): pl.pallas_call(functools.partial(gather_kernel, features, load_steps, bat...  23.5 us
    all_to_all x1, blocking collectives, shards(): lax.all_to_all(looked_up.reshape(dat_size, pair_rows, 2 * features), 'dat...  22.3 us
  transfers between devices with their start and end apart: 23, of which 6 were waited for; matrix products, arithmetic and copies ran while one was open for 16% of the time, Pallas kernels for 48%

profile of v4, /device:TPU:17, one launch (start us, length us, event | category | flops | bytes accessed | tf_op | source)
XLA Modules:
  0.0 567.8 jit_solution(15334897548431297705)
XLA Ops:
  10.4 4.9 share.1
  16.8 23.5 %gather_rows.1 = bf16[2048,384]{1,0:T(8,128)(2,1)} custom-call(f32[192,32128]{1,0:T(8,128)} %refs_0_.1, s32[4,2,512]{2,1,0:T(2,128)} %dynamic-slice_bitcast_fusion.ids_ref), custom_call_target="tpu_custom_call" | custom-call | bytes 83886080 | tf_op jit(solution)/shard_map/gather_rows/pallas_call | solution.py:280
  42.3 22.3 %all_to_all.10.spread_ref = bf16[4,512,384]{2,1,0:T(8,128)(2,1)S(1)} all-to-all(bf16[4,512,384]{2,1,0:T(8,128)(2,1)S(1)} %bitcast.150), channel_id=1, replica_groups=mesh['grp'=4,'dat'=4,'mdl'=2] {'dat'}, dimensions={0} | all-to-all | bytes 3145728 | tf_op jit(solution)/shard_map/all_to_all | solution.py:1078
  64.6 6.5 %collective-permute-start.1 = (bf16[768,1536]{1,0:T(8,128)(2,1)}, bf16[768,1536]{1,0:T(8,128)(2,1)}, u32[]{:S(2)}, u32[]{:S(2)}) collective-permute-start(bf16[768,1536]{1,0:T(8,128)(2,1)} %all-gather.3.cloned.1.call-done), channel_id=1, source_target_pairs={{0,1},{1,0},{2,3},{3,2},{4,5},{5,4},{6,7},{7,6},{8,9},{9,8},{10,11... | collective-permute-start | bytes 7077896 | tf_op jit(solution)/shard_map/ppermute | solution.py:1000
  77.5 4.8 convolution_convert_fusion.1
  82.3 9.8 %attend.2 = (bf16[2,512,384]{2,1,0:T(8,128)(2,1)S(1)}, f32[6,1024]{1,0:T(8,128)S(1)}) custom-call(s32[2]{0:T(128)S(1)} %dynamic_slice.28.lens_ref, f32[6,1024]{1,0:T(8,128)S(1)} %convolution_bitcast_fusion.3.line_ref, bf16[2,512,1152]{2,1,0:T(8,128)(2,1)S(1)} %bitcast.140), custom_call_target="tpu_custom_call" | custom-call | flops 1610612736 | bytes 4718592 | tf_op jit(solution)/shard_map/attend/pallas_call | solution.py:106
  92.1 3.9 convolution_convert_fusion
  96.1 10.0 %attend.3 = (bf16[2,512,384]{2,1,0:T(8,128)(2,1)S(1)}, f32[6,1024]{1,0:T(8,128)S(1)}) custom-call(s32[2]{0:T(128)S(1)} %dynamic_slice.28.lens_ref, f32[6,1024]{1,0:T(8,128)S(1)} %convolution_bitcast_fusion.2.line_ref, bf16[2,512,1152]{2,1,0:T(8,128)(2,1)S(1)} %bitcast.142), custom_call_target="tpu_custom_call" | custom-call | flops 1610612736 | bytes 4718592 | tf_op jit(solution)/shard_map/attend/pallas_call | solution.py:106
  107.6 4.0 all-gather.5.cloned.1.call-done
  126.8 4.3 fusion.30
  131.1 7.5 %multiply_reduce_fusion.3 = (f32[1024]{0:T(1024)S(1)}, f32[1024,768]{1,0:T(8,128)S(1)}) fusion(f32[1024,768]{1,0:T(8,128)S(1)} %get-tuple-element.229, f32[1024,768]{1,0:T(8,128)S(1)} %fusion.34, bf16[768,3072]{1,0:T(8,128)(2,1)} %collective-permute-done.2, f32[1024,1536]{1,0:T(8,128)S(1)} %fusion.30), kind=kOutput, calls=%fused_computation.45 | convolution fusion | flops 2433219584 | bytes 18092032 | tf_op jit(solution)/shard_map/dot_general | solution.py:972
  140.5 7.5 %share_both.1 = (f32[8,8,768]{2,1,0:T(8,128)}, s32[4,16,512]{2,1,0:T(8,128)}) custom-call(f32[8,768]{1,0:T(8,128)} %maximum_maximum_fusion.vectors_ref, s32[16,512]{1,0:T(8,128)} %reshape.295.ids_ref), custom_call_target="tpu_custom_call" | custom-call | tf_op jit(solution)/shard_map/share_both/pallas_call | solution.py:807
  159.3 7.1 %fusion.13 = bf16[1024,1536]{1,0:T(8,128)(2,1)S(1)} fusion(f32[1024,1536]{1,0:T(8,128)S(1)} %copy-done.40, bf16[1024,768]{1,0:T(8,128)(2,1)S(1)} %fusion.42, bf16[768,3072]{1,0:T(8,128)(2,1)} %collective-permute-done.2), kind=kOutput, calls=%fused_computation.17 | convolution fusion | flops 2447376384 | bytes 13369344 | tf_op jit(solution)/shard_map/dot_general | solution.py:972
  171.1 6.3 %fusion.6 = bf16[1024,1536]{1,0:T(8,128)(2,1)S(1)} fusion(f32[1024,1536]{1,0:T(8,128)S(1)} %bitcast.181, bf16[1024,768]{1,0:T(8,128)(2,1)S(1)} %fusion.42, bf16[768,3072]{1,0:T(8,128)(2,1)S(1)} %bitcast.170), kind=kOutput, calls=%fused_computation.10 | convolution fusion | flops 2447376384 | bytes 13369344 | tf_op jit(solution)/shard_map/dot_general | solution.py:972
  186.9 5.4 fusion.38
  192.3 5.0 multiply_reduce_fusion
  201.2 13.4 %attend_back.3 = (bf16[2,512,1152]{2,1,0:T(8,128)(2,1)S(1)}, f32[6,1024]{1,0:T(8,128)S(1)}) custom-call(s32[2]{0:T(128)S(1)} %dynamic_slice.28.lens_ref, f32[6,1024]{1,0:T(8,128)S(1)} %convolution_bitcast_fusion.2.line_ref, bf16[2,512,1152]{2,1,0:T(8,128)(2,1)S(1)} %bitcast.143, f32[6,1024]{1,0:T(8,128)S(1)} %get-tuple-element.105.lse_ref, ...), custom_call_target="tpu_custom_call" | custom-call | flops 4026531840 | bytes 7864320 | tf_op jit(solution)/shard_map/attend_back/pallas_call | solution.py:181
  220.3 13.6 %attend_back.2 = (bf16[2,512,1152]{2,1,0:T(8,128)(2,1)S(1)}, f32[6,1024]{1,0:T(8,128)S(1)}) custom-call(s32[2]{0:T(128)S(1)} %dynamic_slice.28.lens_ref, f32[6,1024]{1,0:T(8,128)S(1)} %convolution_bitcast_fusion.3.line_ref, bf16[2,512,1152]{2,1,0:T(8,128)(2,1)S(1)} %bitcast.141, f32[6,1024]{1,0:T(8,128)S(1)} %get-tuple-element.94.lse_ref, ...), custom_call_target="tpu_custom_call" | custom-call | flops 4026531840 | bytes 7864320 | tf_op jit(solution)/shard_map/attend_back/pallas_call | solution.py:181
  233.9 3.9 fusion.48
  242.7 5.6 convolution_add_fusion
  252.3 4.5 all-to-all-start.1
  260.8 24.4 %all-to-all-done.1 = bf16[4,512,384]{2,1,0:T(8,128)(2,1)} async-done(((bf16[4,512,384]{2,1,0:T(8,128)(2,1)}), bf16[4,512,384]{2,1,0:T(8,128)(2,1)}, u32[]{:S(2)}, u32[]{:S(2)}) %all-to-all-start.1) | async-done | bytes 1572896 | tf_op jit(solution)/shard_map/all_to_all | solution.py:1198
  287.3 4.7 collective-permute-start.5
  294.3 25.0 %scatter_rows.3.refs_6_ = bf16[192,32128]{1,0:T(8,128)(2,1)} custom-call(s32[1]{0:T(128)} %constant.134.refs_0_, s32[24,2,512]{2,1,0:T(2,128)} %get-tuple-element.113.refs_1_.refs_2_, s32[24,2,512]{2,1,0:T(2,128)} %get-tuple-element.113.refs_1_.refs_2_, s32[24,2,128]{2,1,0:T(2,128)} %get-tuple-element.114.refs_3_, bf16[2048,384]{1,0:T(8,128)(2,1)} %bitcast.25.refs_4_), custom_call_target="tpu_custom_call" | custom-call | bytes 104857600 | tf_op jit(solution)/shard_map/scatter_rows/pallas_call | solution.py:476
  319.2 9.8 %sum_all.1.small_ref = f32[32,128]{1,0:T(8,128)} custom-call(f32[32,128]{1,0:T(8,128)} %pad.14.value_ref), custom_call_target="tpu_custom_call" | custom-call | tf_op jit(solution)/shard_map/sum_all/pallas_call | solution.py:775
  329.1 4.4 collective-permute-start.8
  337.1 32.2 %scatter_rows.4.refs_15_ = bf16[192,32128]{1,0:T(8,128)(2,1)} custom-call(s32[1]{0:T(128)} %bitcast.29.refs_0_, s32[24,2,512]{2,1,0:T(2,128)} %get-tuple-element.113.refs_1_.refs_2_, s32[24,2,512]{2,1,0:T(2,128)} %get-tuple-element.113.refs_1_.refs_2_, s32[24,2,128]{2,1,0:T(2,128)} %get-tuple-element.114.refs_3_, ...), custom_call_target="tpu_custom_call" | custom-call | bytes 104857600 | tf_op jit(solution)/shard_map/scatter_rows/pallas_call | solution.py:476
  385.7 36.7 %scatter_rows.5.refs_17_ = bf16[192,32128]{1,0:T(8,128)(2,1)} custom-call(s32[2]{0:T(128)} %fusion.105.refs_0_, s32[24,2,512]{2,1,0:T(2,128)} %get-tuple-element.113.refs_1_.refs_2_, s32[24,2,512]{2,1,0:T(2,128)} %get-tuple-element.113.refs_1_.refs_2_, s32[24,2,128]{2,1,0:T(2,128)} %get-tuple-element.114.refs_3_, ...), custom_call_target="tpu_custom_call" | custom-call | bytes 104857600 | tf_op jit(solution)/shard_map/scatter_rows/pallas_call | solution.py:476
  426.5 90.0 %finish.1 = (f32[192,32128]{1,0:T(8,128)}, f32[192,32128]{1,0:T(8,128)}, bf16[192,32128]{1,0:T(8,128)(2,1)}, f32[8,1024]{1,0:T(8,128)}) custom-call(s32[2]{0:T(128)} %fusion.107.refs_0_, s32[24,2,512]{2,1,0:T(2,128)} %get-tuple-element.113.refs_1_.refs_2_, s32[24,2,512]{2,1,0:T(2,128)} %get-tuple-element.113.refs_1_.refs_2_, ...), custom_call_target="tpu_custom_call" | custom-call | bytes 314572800 | tf_op jit(solution)/shard_map/finish/pallas_call | solution.py:601
  516.6 10.8 %small_moments.1 = (f32[3,192,384]{2,1,0:T(8,128)}, f32[3,192,384]{2,1,0:T(8,128)}, f32[3,192,384]{2,1,0:T(8,128)}, f32[192,384]{1,0:T(8,128)}, f32[192,384]{1,0...) custom-call(bf16[192,3072]{1,0:T(8,128)(2,1)} %get-tuple-element.128, ...), custom_call_target="tpu_custom_call" | custom-call | tf_op jit(solution)/shard_map/small_moments/pallas_call | solution.py:918
  527.5 6.0 %sum_over.1.squares_ref = f32[16,128]{1,0:T(8,128)} custom-call(f32[8,1024]{1,0:T(8,128)} %get-tuple-element.126.rows_ref, f32[16,128]{1,0:T(8,128)} %get-tuple-element.130.table_ref), custom_call_target="tpu_custom_call" | custom-call | tf_op jit(solution)/shard_map/sum_over/pallas_call | solution.py:717
  534.8 26.3 %update_all.1 = (f32[192,32128]{1,0:T(8,128)}, f32[3,192,384]{2,1,0:T(8,128)}, f32[192,384]{1,0:T(8,128)}, f32[192,1536]{1,0:T(8,128)}, f32[192,1536]{1,0:T(8,128)}, /*index=5*/f32[6,32]{1,0:T(8,128)}, f32[3,768]{1,0:T(4,128)}) custom-call(f32[16,128]{1,0:T(8,128)} %sum_over.1.squares_ref, f32[192,32128]{1,0:T(8,128)} %refs_0_.1, ...), custom_call_target="tpu_custom_call" | custom-call | tf_op jit(solution)/shard_map/update_all/pallas_call | solution.py:950
  (239 shorter events, 107.4 us)
Async XLA Ops:
  7.2 57.4 %all-gather.3.cloned.1.call-start = ((), (), s32[]{:S(2)}) async-start(), calls=%async_computation.4 | async-start | bytes 2949120 | tf_op jit(solution)/shard_map/all_gather | solution.py:1058
  10.4 101.2 %all-gather.5.cloned.1.call-start = ((), (), s32[]{:S(2)}) async-start(), calls=%async_computation.5 | async-start | bytes 5898240 | tf_op jit(solution)/shard_map/all_gather | solution.py:1058
  16.8 23.6 %copy-start.20 = (f32[192,1536]{1,0:T(8,128)S(1)}, f32[192,1536]{1,0:T(8,128)}, u32[]{:S(2)}) copy-start(f32[192,1536]{1,0:T(8,128)} %refs_6_.3) | copy-start | bytes 3538948
  16.8 23.6 %copy-start.19 = (f32[192,1536]{1,0:T(8,128)S(1)}, f32[192,1536]{1,0:T(8,128)}, u32[]{:S(2)}) copy-start(f32[192,1536]{1,0:T(8,128)} %refs_8_.3) | copy-start | bytes 3538948
  40.5 30.6 %copy-start.28 = (f32[32,6]{0,1:T(8,128)S(1)}, f32[32,6]{0,1:T(8,128)}, u32[]{:S(2)}) copy-start(f32[32,6]{0,1:T(8,128)} %param.41) | copy-start | bytes 2308
  40.5 31.1 %copy-start.27 = (f32[3,768]{1,0:T(4,128)S(1)}, f32[3,768]{1,0:T(4,128)}, u32[]{:S(2)}) copy-start(f32[3,768]{1,0:T(4,128)} %refs_12_.3) | copy-start | bytes 27652
  40.5 31.2 %copy-start.32 = (s32[4]{0:T(128)S(1)}, s32[4]{0:T(128)}, u32[]{:S(2)}) copy-start(s32[4]{0:T(128)} %param.32) | copy-start | bytes 52
  41.7 210.5 %reduce-scatter.3.cloned.1.call-start = ((), (), s32[]{:S(2)}) async-start(), calls=%async_computation.6 | async-start | bytes 5898240 | tf_op jit(solution)/shard_map/reduce_scatter | solution.py:1144
  64.6 27.5 %collective-permute-start.1 = (bf16[768,1536]{1,0:T(8,128)(2,1)}, bf16[768,1536]{1,0:T(8,128)(2,1)}, u32[]{:S(2)}, u32[]{:S(2)}) collective-permute-start(bf16[768,1536]{1,0:T(8,128)(2,1)} %all-gather.3.cloned.1.call-done), channel_id=1, source_target_pairs={{0,1},{1,0},{2,3},{3,2},{4,5},{5,4},{6,7},{7,6},{8,9},{9,8},{10,11... | collective-permute-start | bytes 7077896 | tf_op jit(solution)/shard_map/ppermute | solution.py:1000
  71.1 4.0 collective-permute-start
  77.5 40.0 %copy-start = (bf16[2,512,768]{2,1,0:T(8,128)(2,1)}, bf16[2,512,768]{2,1,0:T(8,128)(2,1)S(1)}, u32[]{:S(2)}) copy-start(bf16[2,512,768]{2,1,0:T(8,128)(2,1)S(1)} %get-tuple-element.95.embedded_ref) | copy-start | bytes 4718596
  92.1 23.3 %copy-start.5 = (bf16[2,512,384]{2,1,0:T(8,128)(2,1)}, bf16[2,512,384]{2,1,0:T(8,128)(2,1)S(1)}, u32[]{:S(2)}) copy-start(bf16[2,512,384]{2,1,0:T(8,128)(2,1)S(1)} %get-tuple-element.96) | copy-start | bytes 2359300
  111.5 15.3 %collective-permute-start.2 = (bf16[768,3072]{1,0:T(8,128)(2,1)}, bf16[768,3072]{1,0:T(8,128)(2,1)}, u32[]{:S(2)}, u32[]{:S(2)}) collective-permute-start(bf16[768,3072]{1,0:T(8,128)(2,1)} %all-gather.5.cloned.1.call-done), channel_id=1, source_target_pairs={{0,1},{1,0},{2,3},{3,2},{4,5},{5,4},{6,7},{7,6},{8,9},{9,8},{10,11... | collective-permute-start | bytes 14155784 | tf_op jit(solution)/shard_map/ppermute | solution.py:1000
  158.3 19.2 %collective-permute-start.3 = (bf16[768,1536]{1,0:T(8,128)(2,1)S(1)}, bf16[768,1536]{1,0:T(8,128)(2,1)S(1)}, u32[]{:S(2)}, u32[]{:S(2)}) collective-permute-start(bf16[768,1536]{1,0:T(8,128)(2,1)S(1)} %convolution_convert_fusion.3), channel_id=1, source_target_pairs={{0,1},{1,0},{2,3},{3,2},{4,5},{5,4},{6,7},{7,6},{8,9},{9,8},{10,11... | collective-permute-start | bytes 7077896 | tf_op jit(solution)/shard_map/ppermute | solution.py:1000
  171.0 9.8 %collective-permute-start.4 = (bf16[768,1536]{1,0:T(8,128)(2,1)S(1)}, bf16[768,1536]{1,0:T(8,128)(2,1)S(1)}, u32[]{:S(2)}, u32[]{:S(2)}) collective-permute-start(bf16[768,1536]{1,0:T(8,128)(2,1)S(1)} %convolution_convert_fusion.2), channel_id=1, source_target_pairs={{0,1},{1,0},{2,3},{3,2},{4,5},{5,4},{6,7},{7,6},{8,9},{9,8},{10,11... | collective-permute-start | bytes 7077896 | tf_op jit(solution)/shard_map/ppermute | solution.py:1000
  186.8 149.2 %reduce-scatter.5.cloned.1.call-start = ((), (), s32[]{:S(2)}) async-start(), calls=%async_computation.7 | async-start | bytes 2949120 | tf_op jit(solution)/shard_map/reduce_scatter | solution.py:1144
  216.9 21.9 %collective-permute-start.9 = (bf16[768,1152]{1,0:T(8,128)(2,1)S(1)}, bf16[768,1152]{1,0:T(8,128)(2,1)S(1)}, u32[]{:S(2)}, u32[]{:S(2)}) collective-permute-start(bf16[768,1152]{1,0:T(8,128)(2,1)S(1)} %fusion.14), channel_id=1, source_target_pairs={{0,1},{1,0},{2,3},{3,2},{4,5},{5,4},{6,7},{7,6},{8,9},{9,8},{10,11... | collective-permute-start | bytes 5308424 | tf_op jit(solution)/shard_map/ppermute | solution.py:1000
  218.5 19.2 %collective-permute-start.10 = (bf16[768,384]{1,0:T(8,128)(2,1)S(1)}, bf16[768,384]{1,0:T(8,128)(2,1)S(1)}, u32[]{:S(2)}, u32[]{:S(2)}) collective-permute-start(bf16[768,384]{1,0:T(8,128)(2,1)S(1)} %convolution_convert_fusion.6), channel_id=1, source_target_pairs={{0,1},{1,0},{2,3},{3,2},{4,5},{5,4},{6,7},{7,6},{8,9},{9,8},{10,11... | collective-permute-start | bytes 1769480 | tf_op jit(solution)/shard_map/ppermute | solution.py:1000
  252.3 40.5 %copy-start.30 = (s32[1024]{0:T(1024)S(1)}, s32[1024]{0:T(1024)}, u32[]{:S(2)}) copy-start(s32[1024]{0:T(1024)} %copy-done.29) | copy-start | bytes 12292
  252.3 32.9 %all-to-all-start.1 = ((bf16[4,512,384]{2,1,0:T(8,128)(2,1)}), bf16[4,512,384]{2,1,0:T(8,128)(2,1)}, u32[]{:S(2)}, u32[]{:S(2)}) async-start(bf16[4,512,384]{2,1,0:T(8,128)(2,1)} %copy-done.2), calls=%async_computation.2 | async-start | bytes 3145728 | tf_op jit(solution)/shard_map/all_to_all | solution.py:1198
  256.8 259.8 %all-reduce.6.cloned.1.call-start = ((), (), s32[]{:S(2)}) async-start(), calls=%async_computation.8 | async-start | bytes 3538944 | tf_op jit(solution)/shard_map/psum | solution.py:1255
  285.2 43.9 %collective-permute-start.7 = (bf16[2048,384]{1,0:T(8,128)(2,1)}, bf16[2048,384]{1,0:T(8,128)(2,1)}, u32[]{:S(2)}, u32[]{:S(2)}) collective-permute-start(bf16[2048,384]{1,0:T(8,128)(2,1)} %bitcast.25.refs_4_), channel_id=1, source_target_pairs={{24,16},{16,8},{8,0},{25,17},{17,9},{9,1},{26,18},{18,10},{10,2},{... | collective-permute-start | bytes 4718600 | tf_op jit(solution)/shard_map/ppermute | solution.py:1214
  287.3 46.2 %collective-permute-start.5 = (bf16[2048,384]{1,0:T(8,128)(2,1)}, bf16[2048,384]{1,0:T(8,128)(2,1)}, u32[]{:S(2)}, u32[]{:S(2)}) collective-permute-start(bf16[2048,384]{1,0:T(8,128)(2,1)} %bitcast.25.refs_4_), channel_id=1, source_target_pairs={{0,8},{8,16},{16,24},{1,9},{9,17},{17,25},{2,10},{10,18},{18,26},{... | collective-permute-start | bytes 4718600 | tf_op jit(solution)/shard_map/ppermute | solution.py:1214
  294.3 41.1 %copy-start.35 = (s32[1,4]{1,0:T(1,128)S(1)}, s32[1,4]{1,0:T(1,128)}, u32[]{:S(2)}) copy-start(s32[1,4]{1,0:T(1,128)} %constant.121.clone) | copy-start | bytes 52
  329.1 40.2 %collective-permute-start.8 = (bf16[2048,384]{1,0:T(8,128)(2,1)}, bf16[2048,384]{1,0:T(8,128)(2,1)}, u32[]{:S(2)}, u32[]{:S(2)}) collective-permute-start(bf16[2048,384]{1,0:T(8,128)(2,1)} %collective-permute-done.7.refs_5_), channel_id=1, source_target_pairs={{16,8},{8,0},{17,9},{9,1},{18,10},{10,2},{19,11},{11,3},{20,12},{1... | collective-permute-start | bytes 4718600 | tf_op jit(solution)/shard_map/ppermute | solution.py:1214
  333.5 37.0 %collective-permute-start.6 = (bf16[2048,384]{1,0:T(8,128)(2,1)}, bf16[2048,384]{1,0:T(8,128)(2,1)}, u32[]{:S(2)}, u32[]{:S(2)}) collective-permute-start(bf16[2048,384]{1,0:T(8,128)(2,1)} %collective-permute-done.5.refs_4_), channel_id=1, source_target_pairs={{8,16},{16,24},{9,17},{17,25},{10,18},{18,26},{11,19},{19,27},{12,... | collective-permute-start | bytes 4718600 | tf_op jit(solution)/shard_map/ppermute | solution.py:1214
  336.0 36.5 %collective-permute-start.13 = (bf16[2048,384]{1,0:T(8,128)(2,1)}, bf16[2048,384]{1,0:T(8,128)(2,1)}, u32[]{:S(2)}, u32[]{:S(2)}) collective-permute-start(bf16[2048,384]{1,0:T(8,128)(2,1)} %collective-permute-done.7.refs_5_), channel_id=1, source_target_pairs={{0,1},{1,0},{2,3},{3,2},{4,5},{5,4},{6,7},{7,6},{8,9},{9,8},{10,11... | collective-permute-start | bytes 4718600 | tf_op jit(solution)/shard_map/ppermute | solution.py:1000
  370.5 5.4 collective-permute-start.12
  372.5 5.6 collective-permute-start.14
  378.1 48.4 %collective-permute-start.16 = (bf16[192,32128]{1,0:T(8,128)(2,1)}, bf16[192,32128]{1,0:T(8,128)(2,1)}, u32[]{:S(2)}, u32[]{:S(2)}) collective-permute-start(bf16[192,32128]{1,0:T(8,128)(2,1)} %scatter_rows.4.refs_15_), channel_id=1, source_target_pairs={{0,1},{1,0},{2,3},{3,2},{4,5},{5,4},{6,7},{7,6},{8,9},{9,8},{10,11... | collective-permute-start | bytes 37011464 | tf_op jit(solution)/shard_map/ppermute | solution.py:1000
  381.2 41.2 %collective-permute-start.11 = (bf16[2048,384]{1,0:T(8,128)(2,1)}, bf16[2048,384]{1,0:T(8,128)(2,1)}, u32[]{:S(2)}, u32[]{:S(2)}) collective-permute-start(bf16[2048,384]{1,0:T(8,128)(2,1)} %broadcast_select_fusion), channel_id=1, source_target_pairs={{16,24},{8,0},{17,25},{9,1},{18,26},{10,2},{19,27},{11,3},{20,28},... | collective-permute-start | bytes 4718600 | tf_op jit(solution)/shard_map/ppermute | solution.py:1217
  422.4 4.1 collective-permute-start.15
  (39 other events, 310.9 us)
Sparse Core Ops, SparseCore 0:
  10.5 38.7 all-gather.2
  51.7 59.7 all-gather.4
  186.9 57.0 reduce-scatter.2
  246.9 53.2 reduce-scatter.4
  422.5 73.5 all-reduce.5

commit v5 on v4

--- a/solution.py
+++ b/solution.py
@@ -393,7 +393,9 @@
 
 
 class Stage:
-    def __init__(self, segments, choices, ids, flags, first, features):
+    def __init__(self, segments, choices, ids, flags, first, blocks, features):
+        self.first = first
+        first = first * blocks
         self.arrays = [array for candidates in segments for array in candidates]
         self.segments = [len(candidates) for candidates in segments]
         self.chunk = ids.shape[2]
@@ -438,7 +440,7 @@
             for candidate in range(candidates):
                 rows_ref, rows_refs = rows_refs[0], rows_refs[1:]
 
-                @pl.when(now & (choice_ref[segment] == candidate))
+                @pl.when(now & (choice_ref[self.first + segment] == candidate))
                 def _():
                     spread_rows(self.features, rows_ref, summed)
 
@@ -593,15 +595,16 @@
                 squares_ref[line : line + 1, :] += jnp.sum(value * value, axis=0, keepdims=True)
 
 
-def finish(stage, weight, first, second, dense, width=1024, batch=4):
+def finish(stage, weight, first, second, dense, width=1024, batch=4, mode=None):
     features, vocab = weight.shape
     columns = pl.cdiv(vocab, width)
     block = pl.BlockSpec((features, width), lambda s: (0, jnp.maximum(s - stage.steps, 0)))
+    ahead = pl.BlockSpec(block.block_shape, block.index_map, pipeline_mode=mode)
     full = jax.ShapeDtypeStruct(weight.shape, f32)
     return pl.pallas_call(
         functools.partial(finish_kernel, stage, vocab, batch, len(dense)),
         grid=(stage.steps + columns,),
-        in_specs=stage.in_specs + [block] * (3 + len(dense)),
+        in_specs=stage.in_specs + [ahead] * (3 + len(dense)),
         out_specs=[block, block, block, pl.BlockSpec((8, width), lambda s: (0, 0))],
         out_shape=[full, full, jax.ShapeDtypeStruct(weight.shape, bf), jax.ShapeDtypeStruct((8, width), f32)],
         scratch_shapes=stage.scratch(columns * width),
@@ -834,8 +837,8 @@
     return jnp.sum(jnp.sum(value, axis=1, keepdims=True), axis=0, keepdims=True)
 
 
-def small_moments_kernel(ffn_ref, rest_ref, small_ref, *refs):
-    inputs, outputs, squares_ref = refs[:18], refs[18:-1], refs[-1]
+def small_moments_kernel(live_ref, ffn_ref, rest_ref, small_ref, *refs):
+    inputs, outputs, squares_ref, loss_ref = refs[:18], refs[18:-2], refs[-2], refs[-1]
     parts, _, width = inputs[0].shape
     half = ffn_ref.shape[1] // 2
     heads, buckets = inputs[12].shape
@@ -869,6 +872,9 @@
     def _():
         squares_ref[...] = jnp.zeros_like(squares_ref)
         squares_ref[0:1, :] = jnp.where(counted[0], jnp.ones((1, LANES), f32), 0.0)
+        loss_line = gains * lines + HEADS
+        loss_ref[0] = jnp.max(small_ref[loss_line : loss_line + 1, :])
+        loss_ref[1] = live_ref[0]
 
     def update(place):
         weight_ref, first_ref, second_ref = inputs[3 * place : 3 * place + 3]
@@ -905,9 +911,10 @@
     return pl.BlockSpec(value.shape, lambda s: (0,) * value.ndim)
 
 
-def small_moments(weights, gradients, moments, steps):
-    operands = [*gradients]
-    in_specs = [row_block(value, steps) for value in operands[:2]] + [whole_block(operands[2])]
+def small_moments(live_total, weights, gradients, moments, steps):
+    operands = [live_total.reshape(1), *gradients]
+    scalars = pl.BlockSpec(memory_space=pltpu.SMEM)
+    in_specs = [scalars] + [row_block(value, steps) for value in gradients[:2]] + [whole_block(gradients[2])]
     out_specs, out_shape = [], []
     for place, (weight, states) in enumerate(zip(weights, moments)):
         spec = row_block(weight, steps) if place < 4 else whole_block(weight)
@@ -919,8 +926,8 @@
         small_moments_kernel,
         grid=(steps,),
         in_specs=in_specs,
-        out_specs=out_specs + [pl.BlockSpec((16, LANES), lambda s: (0, 0))],
-        out_shape=out_shape + [jax.ShapeDtypeStruct((16, LANES), f32)],
+        out_specs=out_specs + [pl.BlockSpec((16, LANES), lambda s: (0, 0)), scalars],
+        out_shape=out_shape + [jax.ShapeDtypeStruct((16, LANES), f32), jax.ShapeDtypeStruct((2,), f32)],
         compiler_params=pltpu.CompilerParams(vmem_limit_bytes=127 * 2**19),
         name="small_moments",
     )(*operands)
@@ -930,6 +937,8 @@
     norms = jnp.sqrt(squares_ref[...])
     rates = LEARN_RATE * norms[:, 0:1] / norms[:, 1:2]
     count = len(refs) // 3
+    norms_ref = refs[-1]
+    norms_ref[...] = norms[: norms_ref.shape[0], :2]
     for place in range(count):
         weight_ref, direction_ref, updated_ref = refs[2 * place], refs[2 * place + 1], refs[2 * count + place]
         rate = rates[6:9] if place == 6 else rates[place : place + 1]
@@ -951,8 +960,8 @@
         update_all_kernel,
         grid=(steps,),
         in_specs=in_specs,
-        out_specs=out_specs,
-        out_shape=out_shape,
+        out_specs=out_specs + [pl.BlockSpec((9, 2), lambda s: (0, 0))],
+        out_shape=out_shape + [jax.ShapeDtypeStruct((9, 2), f32)],
         compiler_params=pltpu.CompilerParams(vmem_limit_bytes=127 * 2**19),
         name="update_all",
     )(*operands)
@@ -1168,7 +1177,6 @@
     outgoing, grad_gain_one = pack_back(one_back, embedded_low, grad_after_attn, norm_gains[0], features)
     total_qkv = both_cores(*[dot(normed_one, grad, tn) for grad in grad_qkv_rows])
     total_rest = jnp.concatenate([total_qkv, total_out], axis=1)
-    part_rest = scattered(total_rest)
 
     grad_bias_own, grad_bias_other = [
         jnp.einsum("rb,hr->hb", onehot, grad, precision=MAX_PRECISION) for grad in grad_lines
@@ -1197,6 +1205,7 @@
     outgoing = after(outgoing, part_ffn)
     own_rows = lax.all_to_all(outgoing, "dat", split_axis=0, concat_axis=0, tiled=True)
     own_rows = own_rows.reshape(dat_size * pair_rows, 2 * features)
+    part_rest = scattered(after(total_rest, own_rows))
     moving = [[own_rows], [own_rows]]
     swapped = [[None], [None]]
 
@@ -1223,35 +1232,32 @@
         kinds = sorted(set(found))
         return kinds, [kinds.index(kind) for kind in found]
 
-    def stage(slots, first, both):
-        segments, picks = [], []
-        for slot in slots:
-            if slot == 0:
-                segments.append([own_rows])
-                picks.append([0] * grp_size)
-                continue
-            kinds, pick = candidates(slot)
-            for buffers in (moving, swapped)[: 1 + both]:
-                segments.append([buffers[way][hop] for way, hop in kinds])
-                picks.append(pick)
-        choices = lax.dynamic_index_in_dim(jnp.array(picks, jnp.int32).T, group_index, 0, keepdims=False)
-        return Stage(segments, choices, staged_ids, staged_flags, first * dat_size * chunks, features)
-
-    move(1, staged_flags)
-    first_table = scatter_rows(stage([0], 0, False), vocab)
+    picks = [[0] * grp_size if slot == 0 else candidates(slot)[1] for slot, _ in order]
+    choices = lax.dynamic_index_in_dim(jnp.array(picks, jnp.int32).T, group_index, 0, keepdims=False)
+    choices = after(choices, outgoing)
+
+    def stage(first, count):
+        segments = []
+        for slot, other in order[first : first + count]:
+            buffers = swapped if other else moving
+            segments.append([own_rows] if slot == 0 else [buffers[way][hop] for way, hop in candidates(slot)[0]])
+        return Stage(segments, choices, staged_ids, staged_flags, first, dat_size * chunks, features)
+
+    move(1)
+    first_table = scatter_rows(stage(0, 1), vocab)
     small = sum_all(after(small, first_table), ("dat", "mdl"), "grp", (dat_size, mdl_size, grp_size))
     for hop in range(2, grp_size - 1):
         move(hop, small)
         swap(hop - 1)
-    early = stage(range(1, grp_size - 2), 1, False)
+    early = stage(1, grp_size - 3)
     early.operands[0] = after(early.operands[0], part_rest)
     own_table = scatter_rows(early, vocab, (first_table,))
     swap(grp_size - 2, own_table)
     move(grp_size - 1, own_table)
     other_table = swap_cores(after(own_table, *[kept for way in swapped for kept in way[1:]]))
-    late_table = scatter_rows(stage([grp_size - 2], grp_size - 2, True), vocab)
+    late_table = scatter_rows(stage(grp_size - 2, 2), vocab)
     swap(grp_size - 1, late_table)
-    last = stage([grp_size - 1], grp_size, True)
+    last = stage(grp_size, 2)
     full_ffn, full_rest = lax.psum((after(part_ffn, late_table), part_rest), "grp")
     table_momentum, table_variance, table_direction, table_squares = finish(
         last,
@@ -1261,7 +1267,6 @@
         (own_table, other_table, late_table),
     )
     full_ffn, full_rest = after(full_ffn, table_squares), after(full_rest, table_squares)
-    loss_total = small[gain_lines.shape[0] + HEADS, 0]
     by_part = lambda value: value.transpose(1, 0, 2)
     weights = (by_part(qkv_weight), out_weight.T, up_weight, down_weight, bias_table.T, norm_gains)
     gradients = (full_ffn, full_rest, small)
@@ -1273,12 +1278,12 @@
         (bias_first.T, bias_second.T),
         (gains_first, gains_second),
     )
-    *results, square_table = small_moments(weights, gradients, moments, max(1, features // 48))
+    *results, square_table, loss_pair = small_moments(live_total, weights, gradients, moments, max(1, features // 48))
     squares = sum_over(table_squares, square_table, ("dat", "mdl"), (dat_size, mdl_size))
     updated = update_all(squares, (embedding, *weights), (table_direction, *results[2::3]), features // 16)
     outputs = [
-        jnp.stack([loss_total, live_total]),
-        jnp.sqrt(squares[:9, :2]),
+        loss_pair,
+        updated[-1],
         table_momentum,
         table_variance,
         updated[0],

time: 578 us -> 572 us (0.990)
  waiting for transfers between devices: 38.6 us -> 30.6 us
  local copies, waits for them, and re-layouts: 17.8 us -> 11.1 us
    all_to_all x1, waiting for transfers between devices: 24.4 us -> 11.2 us  [shards(): lax.all_to_all(outgoing, 'dat', split_axis=0, concat_axis=0, tiled=True)]
  transfers between devices with their start and end apart: 23 -> 23, of which waited for: 6 -> 7; matrix products, arithmetic and copies ran while one was open for 16% -> 16% of each run, Pallas kernels for 48% -> 49%
where the time goes in v5:
time: 572 us; the launch traced here: 562 us
  Pallas kernels  327 us (57%)
  matrix products  92.1 us (16%)
  starting transfers between devices  33.6 us (6%)
  waiting for transfers between devices  30.6 us (5%)
  other arithmetic  28.4 us (5%)
  blocking collectives  22.7 us (4%)
  between operations  16.7 us (3%)
  local copies, waits for them, and re-layouts  11.1 us (2%)
    pallas_call x3, Pallas kernels, scatter_rows(): pl.pallas_call(functools.partial(scatter_kernel, stage, batch, len(dense)...  93.4 us
    pallas_call x1, Pallas kernels, finish(): pl.pallas_call(functools.partial(finish_kernel, stage, vocab, batch, len(...  90.2 us
    dot_general x24, matrix products, dot(): lax.dot_general(left, right, (dims, ((), ())), preferred_element_type=f32)  89.9 us
    pallas_call x2, Pallas kernels, attend_back(): pl.pallas_call(functools.partial(attend_back_kernel, pairs, HEAD ** (-0.5...  26.9 us
    pallas_call x1, Pallas kernels, update_all(): pl.pallas_call(update_all_kernel, grid=(steps,), in_specs=in_specs, out_s...  26.3 us
    pallas_call x1, Pallas kernels, gather_rows(): pl.pallas_call(functools.partial(gather_kernel, features, load_steps, bat...  23.5 us
    all_to_all x1, blocking collectives, shards(): lax.all_to_all(looked_up.reshape(dat_size, pair_rows, 2 * features), 'dat...  22.7 us
    pallas_call x2, Pallas kernels, attend(): pl.pallas_call(functools.partial(attend_kernel, pairs, HEAD ** (-0.5)), i...  19.7 us
  transfers between devices with their start and end apart: 23, of which 7 were waited for; matrix products, arithmetic and copies ran while one was open for 16% of the time, Pallas kernels for 49%

profile of v5, /device:TPU:17, one launch (start us, length us, event | category | flops | bytes accessed | tf_op | source)
XLA Modules:
  0.0 562.2 jit_solution(9683542402221759047)
XLA Ops:
  10.4 4.9 share.1
  16.8 23.5 %gather_rows.1 = bf16[2048,384]{1,0:T(8,128)(2,1)} custom-call(f32[192,32128]{1,0:T(8,128)} %refs_0_.1, s32[4,2,512]{2,1,0:T(2,128)} %dynamic-slice_bitcast_fusion.ids_ref), custom_call_target="tpu_custom_call" | custom-call | bytes 83886080 | tf_op jit(solution)/shard_map/gather_rows/pallas_call | solution.py:280
  42.1 22.7 %all_to_all.10.spread_ref = bf16[4,512,384]{2,1,0:T(8,128)(2,1)S(1)} all-to-all(bf16[4,512,384]{2,1,0:T(8,128)(2,1)S(1)} %bitcast.146), channel_id=1, replica_groups=mesh['grp'=4,'dat'=4,'mdl'=2] {'dat'}, dimensions={0} | all-to-all | bytes 3145728 | tf_op jit(solution)/shard_map/all_to_all | solution.py:1087
  64.8 5.8 %collective-permute-start.1 = (bf16[768,1536]{1,0:T(8,128)(2,1)}, bf16[768,1536]{1,0:T(8,128)(2,1)}, u32[]{:S(2)}, u32[]{:S(2)}) collective-permute-start(bf16[768,1536]{1,0:T(8,128)(2,1)} %all-gather.3.cloned.1.call-done), channel_id=1, source_target_pairs={{0,1},{1,0},{2,3},{3,2},{4,5},{5,4},{6,7},{7,6},{8,9},{9,8},{10,11... | collective-permute-start | bytes 7077896 | tf_op jit(solution)/shard_map/ppermute | solution.py:1009
  76.9 4.3 convolution_convert_fusion.1
  81.2 9.7 %attend.2 = (bf16[2,512,384]{2,1,0:T(8,128)(2,1)S(1)}, f32[6,1024]{1,0:T(8,128)S(1)}) custom-call(s32[2]{0:T(128)S(1)} %dynamic_slice.20.lens_ref, f32[6,1024]{1,0:T(8,128)S(1)} %convolution_bitcast_fusion.3.line_ref, bf16[2,512,1152]{2,1,0:T(8,128)(2,1)S(1)} %bitcast.136), custom_call_target="tpu_custom_call" | custom-call | flops 1610612736 | bytes 4718592 | tf_op jit(solution)/shard_map/attend/pallas_call | solution.py:106
  94.7 9.9 %attend.3 = (bf16[2,512,384]{2,1,0:T(8,128)(2,1)S(1)}, f32[6,1024]{1,0:T(8,128)S(1)}) custom-call(s32[2]{0:T(128)S(1)} %dynamic_slice.20.lens_ref, f32[6,1024]{1,0:T(8,128)S(1)} %convolution_bitcast_fusion.2.line_ref, bf16[2,512,1152]{2,1,0:T(8,128)(2,1)S(1)} %bitcast.138), custom_call_target="tpu_custom_call" | custom-call | flops 1610612736 | bytes 4718592 | tf_op jit(solution)/shard_map/attend/pallas_call | solution.py:106
  106.1 5.4 all-gather.5.cloned.1.call-done
  123.0 3.8 fusion.34
  126.8 4.3 fusion.30
  131.1 9.0 %multiply_reduce_fusion.3 = (f32[1024]{0:T(1024)S(1)}, f32[1024,768]{1,0:T(8,128)}) fusion(f32[1024,768]{1,0:T(8,128)S(1)} %get-tuple-element.235, f32[1024,768]{1,0:T(8,128)S(1)} %fusion.34, bf16[768,3072]{1,0:T(8,128)(2,1)} %collective-permute-done.2, f32[1024,1536]{1,0:T(8,128)S(1)} %fusion.30), kind=kOutput, calls=%fused_computation.45 | convolution fusion | flops 2433219584 | bytes 18092032 | tf_op jit(solution)/shard_map/dot_general | solution.py:981
  143.7 7.5 %share_both.1 = (f32[8,8,768]{2,1,0:T(8,128)}, s32[4,16,512]{2,1,0:T(8,128)}) custom-call(f32[8,768]{1,0:T(8,128)} %maximum_maximum_fusion.vectors_ref, s32[16,512]{1,0:T(8,128)} %reshape.293.ids_ref), custom_call_target="tpu_custom_call" | custom-call | tf_op jit(solution)/shard_map/share_both/pallas_call | solution.py:810
  165.1 7.1 %fusion.13 = bf16[1024,1536]{1,0:T(8,128)(2,1)S(1)} fusion(f32[1024,1536]{1,0:T(8,128)S(1)} %copy-done.32, bf16[1024,768]{1,0:T(8,128)(2,1)S(1)} %fusion.42, bf16[768,3072]{1,0:T(8,128)(2,1)} %collective-permute-done.2), kind=kOutput, calls=%fused_computation.17 | convolution fusion | flops 2447376384 | bytes 13369344 | tf_op jit(solution)/shard_map/dot_general | solution.py:981
  175.4 6.3 %fusion.6 = bf16[1024,1536]{1,0:T(8,128)(2,1)S(1)} fusion(f32[1024,1536]{1,0:T(8,128)S(1)} %bitcast.177, bf16[1024,768]{1,0:T(8,128)(2,1)S(1)} %fusion.42, bf16[768,3072]{1,0:T(8,128)(2,1)S(1)} %bitcast.166), kind=kOutput, calls=%fused_computation.10 | convolution fusion | flops 2447376384 | bytes 13369344 | tf_op jit(solution)/shard_map/dot_general | solution.py:981
  191.3 5.4 fusion.38
  196.7 4.8 multiply_reduce_fusion
  209.3 13.6 %attend_back.3 = (bf16[2,512,1152]{2,1,0:T(8,128)(2,1)S(1)}, f32[6,1024]{1,0:T(8,128)S(1)}) custom-call(s32[2]{0:T(128)S(1)} %dynamic_slice.20.lens_ref, f32[6,1024]{1,0:T(8,128)S(1)} %convolution_bitcast_fusion.2.line_ref, bf16[2,512,1152]{2,1,0:T(8,128)(2,1)S(1)} %bitcast.139, f32[6,1024]{1,0:T(8,128)S(1)} %get-tuple-element.108.lse_ref, ...), custom_call_target="tpu_custom_call" | custom-call | flops 4026531840 | bytes 7864320 | tf_op jit(solution)/shard_map/attend_back/pallas_call | solution.py:181
  228.1 13.4 %attend_back.2 = (bf16[2,512,1152]{2,1,0:T(8,128)(2,1)S(1)}, f32[6,1024]{1,0:T(8,128)S(1)}) custom-call(s32[2]{0:T(128)S(1)} %dynamic_slice.20.lens_ref, f32[6,1024]{1,0:T(8,128)S(1)} %convolution_bitcast_fusion.3.line_ref, bf16[2,512,1152]{2,1,0:T(8,128)(2,1)S(1)} %bitcast.137, f32[6,1024]{1,0:T(8,128)S(1)} %get-tuple-element.106.lse_ref, ...), custom_call_target="tpu_custom_call" | custom-call | flops 4026531840 | bytes 7864320 | tf_op jit(solution)/shard_map/attend_back/pallas_call | solution.py:181
  243.7 3.7 convolution_add_fusion
  250.9 4.4 all-to-all-start.1
  258.3 3.7 add_convert_fusion.2
  263.7 11.2 %all-to-all-done.1 = bf16[4,512,384]{2,1,0:T(8,128)(2,1)} async-done(((bf16[4,512,384]{2,1,0:T(8,128)(2,1)}), bf16[4,512,384]{2,1,0:T(8,128)(2,1)}, u32[]{:S(2)}, u32[]{:S(2)}) %all-to-all-start.1) | async-done | bytes 1572896 | tf_op jit(solution)/shard_map/all_to_all | solution.py:1206
  277.4 3.9 collective-permute-start.5
  288.9 25.0 %scatter_rows.3.refs_6_ = bf16[192,32128]{1,0:T(8,128)(2,1)} custom-call(s32[6]{0:T(128)} %fusion.104.refs_0_, s32[24,2,512]{2,1,0:T(2,128)} %get-tuple-element.115.refs_1_.refs_2_, s32[24,2,512]{2,1,0:T(2,128)} %get-tuple-element.115.refs_1_.refs_2_, s32[24,2,128]{2,1,0:T(2,128)} %get-tuple-element.116.refs_3_, bf16[2048,384]{1,0:T(8,128)(2,1)} %bitcast.27.refs_4_), custom_call_target="tpu_custom_call" | custom-call | bytes 104857600 | tf_op jit(solution)/shard_map/scatter_rows/pallas_call | solution.py:478
  313.9 10.3 %sum_all.1.small_ref = f32[32,128]{1,0:T(8,128)} custom-call(f32[32,128]{1,0:T(8,128)} %pad.14.value_ref), custom_call_target="tpu_custom_call" | custom-call | tf_op jit(solution)/shard_map/sum_all/pallas_call | solution.py:778
  324.1 4.1 collective-permute-start.8
  331.8 31.5 %scatter_rows.4.refs_15_ = bf16[192,32128]{1,0:T(8,128)(2,1)} custom-call(s32[6]{0:T(128)} %fusion.104.refs_0_, s32[24,2,512]{2,1,0:T(2,128)} %get-tuple-element.115.refs_1_.refs_2_, s32[24,2,512]{2,1,0:T(2,128)} %get-tuple-element.115.refs_1_.refs_2_, s32[24,2,128]{2,1,0:T(2,128)} %get-tuple-element.116.refs_3_, ...), custom_call_target="tpu_custom_call" | custom-call | bytes 104857600 | tf_op jit(solution)/shard_map/scatter_rows/pallas_call | solution.py:478
  379.4 36.9 %scatter_rows.5.refs_17_ = bf16[192,32128]{1,0:T(8,128)(2,1)} custom-call(s32[6]{0:T(128)} %fusion.104.refs_0_, s32[24,2,512]{2,1,0:T(2,128)} %get-tuple-element.115.refs_1_.refs_2_, s32[24,2,512]{2,1,0:T(2,128)} %get-tuple-element.115.refs_1_.refs_2_, s32[24,2,128]{2,1,0:T(2,128)} %get-tuple-element.116.refs_3_, ...), custom_call_target="tpu_custom_call" | custom-call | bytes 104857600 | tf_op jit(solution)/shard_map/scatter_rows/pallas_call | solution.py:478
  420.2 90.2 %finish.1 = (f32[192,32128]{1,0:T(8,128)}, f32[192,32128]{1,0:T(8,128)}, bf16[192,32128]{1,0:T(8,128)(2,1)}, f32[8,1024]{1,0:T(8,128)}) custom-call(s32[6]{0:T(128)} %fusion.104.refs_0_, s32[24,2,512]{2,1,0:T(2,128)} %get-tuple-element.115.refs_1_.refs_2_, s32[24,2,512]{2,1,0:T(2,128)} %get-tuple-element.115.refs_1_.refs_2_, ...), custom_call_target="tpu_custom_call" | custom-call | bytes 314572800 | tf_op jit(solution)/shard_map/finish/pallas_call | solution.py:604
  510.4 11.0 %small_moments.1 = (f32[3,192,384]{2,1,0:T(8,128)}, f32[3,192,384]{2,1,0:T(8,128)}, f32[3,192,384]{2,1,0:T(8,128)}, f32[192,384]{1,0:T(8,128)}, f32[192,384]{1,0...) custom-call(f32[1]{0:T(128)} %bitcast.live_ref, ...), custom_call_target="tpu_custom_call" | custom-call | tf_op jit(solution)/shard_map/small_moments/pallas_call | solution.py:925
  521.3 6.3 %sum_over.1.squares_ref = f32[16,128]{1,0:T(8,128)} custom-call(f32[8,1024]{1,0:T(8,128)} %get-tuple-element.131.rows_ref, f32[16,128]{1,0:T(8,128)} %get-tuple-element.135.table_ref), custom_call_target="tpu_custom_call" | custom-call | tf_op jit(solution)/shard_map/sum_over/pallas_call | solution.py:720
  527.6 26.3 %update_all.1 = (f32[192,32128]{1,0:T(8,128)}, f32[3,192,384]{2,1,0:T(8,128)}, f32[192,384]{1,0:T(8,128)}, f32[192,1536]{1,0:T(8,128)}, f32[192,1536]{1,0:T(8,12...) custom-call(f32[16,128]{1,0:T(8,128)} %sum_over.1.squares_ref, f32[192,32128]{1,0:T(8,128)} %refs_0_.1, ...), custom_call_target="tpu_custom_call" | custom-call | tf_op jit(solution)/shard_map/update_all/pallas_call | solution.py:959
  (218 shorter events, 115.8 us)
Async XLA Ops:
  7.2 57.6 %all-gather.3.cloned.1.call-start = ((), (), s32[]{:S(2)}) async-start(), calls=%async_computation.4 | async-start | bytes 2949120 | tf_op jit(solution)/shard_map/all_gather | solution.py:1067
  10.4 101.2 %all-gather.5.cloned.1.call-start = ((), (), s32[]{:S(2)}) async-start(), calls=%async_computation.5 | async-start | bytes 5898240 | tf_op jit(solution)/shard_map/all_gather | solution.py:1067
  16.8 23.6 %copy-start.12 = (f32[192,1536]{1,0:T(8,128)S(1)}, f32[192,1536]{1,0:T(8,128)}, u32[]{:S(2)}) copy-start(f32[192,1536]{1,0:T(8,128)} %refs_6_.3) | copy-start | bytes 3538948
  16.8 23.6 %copy-start.11 = (f32[192,1536]{1,0:T(8,128)S(1)}, f32[192,1536]{1,0:T(8,128)}, u32[]{:S(2)}) copy-start(f32[192,1536]{1,0:T(8,128)} %refs_8_.3) | copy-start | bytes 3538948
  40.5 30.1 %copy-start.21 = (f32[32,6]{0,1:T(8,128)S(1)}, f32[32,6]{0,1:T(8,128)}, u32[]{:S(2)}) copy-start(f32[32,6]{0,1:T(8,128)} %param.38) | copy-start | bytes 2308
  40.5 30.6 %copy-start.20 = (f32[3,768]{1,0:T(4,128)S(1)}, f32[3,768]{1,0:T(4,128)}, u32[]{:S(2)}) copy-start(f32[3,768]{1,0:T(4,128)} %refs_12_.3) | copy-start | bytes 27652
  40.5 30.6 %copy-start.25 = (s32[4]{0:T(128)S(1)}, s32[4]{0:T(128)}, u32[]{:S(2)}) copy-start(s32[4]{0:T(128)} %param.29) | copy-start | bytes 52
  41.7 209.2 %reduce-scatter.3.cloned.1.call-start = ((), (), s32[]{:S(2)}) async-start(), calls=%async_computation.6 | async-start | bytes 5898240 | tf_op jit(solution)/shard_map/reduce_scatter | solution.py:1153
  64.8 26.2 %collective-permute-start.1 = (bf16[768,1536]{1,0:T(8,128)(2,1)}, bf16[768,1536]{1,0:T(8,128)(2,1)}, u32[]{:S(2)}, u32[]{:S(2)}) collective-permute-start(bf16[768,1536]{1,0:T(8,128)(2,1)} %all-gather.3.cloned.1.call-done), channel_id=1, source_target_pairs={{0,1},{1,0},{2,3},{3,2},{4,5},{5,4},{6,7},{7,6},{8,9},{9,8},{10,11... | collective-permute-start | bytes 7077896 | tf_op jit(solution)/shard_map/ppermute | solution.py:1009
  70.6 4.0 collective-permute-start
  94.7 19.5 %copy-start.27 = (s32[4]{0:T(128)S(1)}, s32[4]{0:T(128)}, u32[]{:S(2)}) copy-start(s32[4]{0:T(128)} %param.32) | copy-start | bytes 52
  111.5 15.2 %collective-permute-start.2 = (bf16[768,3072]{1,0:T(8,128)(2,1)}, bf16[768,3072]{1,0:T(8,128)(2,1)}, u32[]{:S(2)}, u32[]{:S(2)}) collective-permute-start(bf16[768,3072]{1,0:T(8,128)(2,1)} %all-gather.5.cloned.1.call-done), channel_id=1, source_target_pairs={{0,1},{1,0},{2,3},{3,2},{4,5},{5,4},{6,7},{7,6},{8,9},{9,8},{10,11... | collective-permute-start | bytes 14155784 | tf_op jit(solution)/shard_map/ppermute | solution.py:1009
  164.1 17.6 %collective-permute-start.3 = (bf16[768,1536]{1,0:T(8,128)(2,1)S(1)}, bf16[768,1536]{1,0:T(8,128)(2,1)S(1)}, u32[]{:S(2)}, u32[]{:S(2)}) collective-permute-start(bf16[768,1536]{1,0:T(8,128)(2,1)S(1)} %convolution_convert_fusion.3), channel_id=1, source_target_pairs={{0,1},{1,0},{2,3},{3,2},{4,5},{5,4},{6,7},{7,6},{8,9},{9,8},{10,11... | collective-permute-start | bytes 7077896 | tf_op jit(solution)/shard_map/ppermute | solution.py:1009
  175.2 9.8 %collective-permute-start.4 = (bf16[768,1536]{1,0:T(8,128)(2,1)S(1)}, bf16[768,1536]{1,0:T(8,128)(2,1)S(1)}, u32[]{:S(2)}, u32[]{:S(2)}) collective-permute-start(bf16[768,1536]{1,0:T(8,128)(2,1)S(1)} %convolution_convert_fusion.2), channel_id=1, source_target_pairs={{0,1},{1,0},{2,3},{3,2},{4,5},{5,4},{6,7},{7,6},{8,9},{9,8},{10,11... | collective-permute-start | bytes 7077896 | tf_op jit(solution)/shard_map/ppermute | solution.py:1009
  204.5 21.8 %copy-start.16 = (bf16[1024,768]{1,0:T(8,128)(2,1)}, bf16[1024,768]{1,0:T(8,128)(2,1)S(1)}, u32[]{:S(2)}) copy-start(bf16[1024,768]{1,0:T(8,128)(2,1)S(1)} %get-tuple-element.223) | copy-start | bytes 4718596
  206.4 49.2 %collective-permute-start.10 = (bf16[768,384]{1,0:T(8,128)(2,1)}, bf16[768,384]{1,0:T(8,128)(2,1)}, u32[]{:S(2)}, u32[]{:S(2)}) collective-permute-start(bf16[768,384]{1,0:T(8,128)(2,1)} %convolution_convert_fusion.6), channel_id=1, source_target_pairs={{0,1},{1,0},{2,3},{3,2},{4,5},{5,4},{6,7},{7,6},{8,9},{9,8},{10,11... | collective-permute-start | bytes 1769480 | tf_op jit(solution)/shard_map/ppermute | solution.py:1009
  226.4 31.9 %collective-permute-start.9 = (bf16[768,1152]{1,0:T(8,128)(2,1)}, bf16[768,1152]{1,0:T(8,128)(2,1)}, u32[]{:S(2)}, u32[]{:S(2)}) collective-permute-start(bf16[768,1152]{1,0:T(8,128)(2,1)} %fusion.14), channel_id=1, source_target_pairs={{0,1},{1,0},{2,3},{3,2},{4,5},{5,4},{6,7},{7,6},{8,9},{9,8},{10,11... | collective-permute-start | bytes 5308424 | tf_op jit(solution)/shard_map/ppermute | solution.py:1009
  250.9 24.0 %all-to-all-start.1 = ((bf16[4,512,384]{2,1,0:T(8,128)(2,1)}), bf16[4,512,384]{2,1,0:T(8,128)(2,1)}, u32[]{:S(2)}, u32[]{:S(2)}) async-start(bf16[4,512,384]{2,1,0:T(8,128)(2,1)} %get-tuple-element.111), calls=%async_computation.2 | async-start | bytes 3145728 | tf_op jit(solution)/shard_map/all_to_all | solution.py:1206
  255.3 76.5 %reduce-scatter.5.cloned.1.call-start = ((), (), s32[]{:S(2)}) async-start(), calls=%async_computation.7 | async-start | bytes 2949120 | tf_op jit(solution)/shard_map/reduce_scatter | solution.py:1153
  262.1 21.8 %copy-start.19 = (s32[4,16,512]{2,1,0:T(8,128)S(1)}, s32[4,16,512]{2,1,0:T(8,128)}, u32[]{:S(2)}) copy-start(s32[4,16,512]{2,1,0:T(8,128)} %get-tuple-element.113) | copy-start | bytes 393220
  262.1 23.4 %copy-start.23 = (s32[1024]{0:T(1024)S(1)}, s32[1024]{0:T(1024)}, u32[]{:S(2)}) copy-start(s32[1024]{0:T(1024)} %copy-done.22) | copy-start | bytes 12292
  274.9 235.5 %all-reduce.6.cloned.1.call-start = ((), (), s32[]{:S(2)}) async-start(), calls=%async_computation.8 | async-start | bytes 3538944 | tf_op jit(solution)/shard_map/psum | solution.py:1261
  274.9 49.2 %collective-permute-start.7 = (bf16[2048,384]{1,0:T(8,128)(2,1)}, bf16[2048,384]{1,0:T(8,128)(2,1)}, u32[]{:S(2)}, u32[]{:S(2)}) collective-permute-start(bf16[2048,384]{1,0:T(8,128)(2,1)} %bitcast.27.refs_4_), channel_id=1, source_target_pairs={{24,16},{16,8},{8,0},{25,17},{17,9},{9,1},{26,18},{18,10},{10,2},{... | collective-permute-start | bytes 4718600 | tf_op jit(solution)/shard_map/ppermute | solution.py:1223
  277.4 50.8 %collective-permute-start.5 = (bf16[2048,384]{1,0:T(8,128)(2,1)}, bf16[2048,384]{1,0:T(8,128)(2,1)}, u32[]{:S(2)}, u32[]{:S(2)}) collective-permute-start(bf16[2048,384]{1,0:T(8,128)(2,1)} %bitcast.27.refs_4_), channel_id=1, source_target_pairs={{0,8},{8,16},{16,24},{1,9},{9,17},{17,25},{2,10},{10,18},{18,26},{... | collective-permute-start | bytes 4718600 | tf_op jit(solution)/shard_map/ppermute | solution.py:1223
  324.1 39.1 %collective-permute-start.8 = (bf16[2048,384]{1,0:T(8,128)(2,1)}, bf16[2048,384]{1,0:T(8,128)(2,1)}, u32[]{:S(2)}, u32[]{:S(2)}) collective-permute-start(bf16[2048,384]{1,0:T(8,128)(2,1)} %collective-permute-done.7.refs_5_), channel_id=1, source_target_pairs={{16,8},{8,0},{17,9},{9,1},{18,10},{10,2},{19,11},{11,3},{20,12},{1... | collective-permute-start | bytes 4718600 | tf_op jit(solution)/shard_map/ppermute | solution.py:1223
  328.3 36.6 %collective-permute-start.6 = (bf16[2048,384]{1,0:T(8,128)(2,1)}, bf16[2048,384]{1,0:T(8,128)(2,1)}, u32[]{:S(2)}, u32[]{:S(2)}) collective-permute-start(bf16[2048,384]{1,0:T(8,128)(2,1)} %collective-permute-done.5.refs_4_), channel_id=1, source_target_pairs={{8,16},{16,24},{9,17},{17,25},{10,18},{18,26},{11,19},{19,27},{12,... | collective-permute-start | bytes 4718600 | tf_op jit(solution)/shard_map/ppermute | solution.py:1223
  330.2 37.1 %collective-permute-start.12 = (bf16[2048,384]{1,0:T(8,128)(2,1)}, bf16[2048,384]{1,0:T(8,128)(2,1)}, u32[]{:S(2)}, u32[]{:S(2)}) collective-permute-start(bf16[2048,384]{1,0:T(8,128)(2,1)} %collective-permute-done.7.refs_5_), channel_id=1, source_target_pairs={{0,1},{1,0},{2,3},{3,2},{4,5},{5,4},{6,7},{7,6},{8,9},{9,8},{10,11... | collective-permute-start | bytes 4718600 | tf_op jit(solution)/shard_map/ppermute | solution.py:1009
  364.8 5.8 %collective-permute-start.11 = (bf16[2048,384]{1,0:T(8,128)(2,1)}, bf16[2048,384]{1,0:T(8,128)(2,1)}, u32[]{:S(2)}, u32[]{:S(2)}) collective-permute-start(bf16[2048,384]{1,0:T(8,128)(2,1)} %collective-permute-done.6.refs_4_), channel_id=1, source_target_pairs={{0,1},{1,0},{2,3},{3,2},{4,5},{5,4},{6,7},{7,6},{8,9},{9,8},{10,11... | collective-permute-start | bytes 4718600 | tf_op jit(solution)/shard_map/ppermute | solution.py:1009
  367.3 5.6 %collective-permute-start.13 = (bf16[2048,384]{1,0:T(8,128)(2,1)}, bf16[2048,384]{1,0:T(8,128)(2,1)}, u32[]{:S(2)}, u32[]{:S(2)}) collective-permute-start(bf16[2048,384]{1,0:T(8,128)(2,1)} %collective-permute-done.8.refs_6_), channel_id=1, source_target_pairs={{0,1},{1,0},{2,3},{3,2},{4,5},{5,4},{6,7},{7,6},{8,9},{9,8},{10,11... | collective-permute-start | bytes 4718600 | tf_op jit(solution)/shard_map/ppermute | solution.py:1009
  372.9 47.3 %collective-permute-start.16 = (bf16[192,32128]{1,0:T(8,128)(2,1)}, bf16[192,32128]{1,0:T(8,128)(2,1)}, u32[]{:S(2)}, u32[]{:S(2)}) collective-permute-start(bf16[192,32128]{1,0:T(8,128)(2,1)} %scatter_rows.4.refs_15_), channel_id=1, source_target_pairs={{0,1},{1,0},{2,3},{3,2},{4,5},{5,4},{6,7},{7,6},{8,9},{9,8},{10,11... | collective-permute-start | bytes 37011464 | tf_op jit(solution)/shard_map/ppermute | solution.py:1009
  376.0 40.3 %collective-permute-start.14 = (bf16[2048,384]{1,0:T(8,128)(2,1)}, bf16[2048,384]{1,0:T(8,128)(2,1)}, u32[]{:S(2)}, u32[]{:S(2)}) collective-permute-start(bf16[2048,384]{1,0:T(8,128)(2,1)} %broadcast_select_fusion), channel_id=1, source_target_pairs={{16,24},{8,0},{17,25},{9,1},{18,26},{10,2},{19,27},{11,3},{20,28},... | collective-permute-start | bytes 4718600 | tf_op jit(solution)/shard_map/ppermute | solution.py:1226
  416.3 3.9 collective-permute-start.15
  (31 other events, 244.6 us)
Sparse Core Ops, SparseCore 0:
  10.5 38.8 all-gather.2
  51.8 59.6 all-gather.4
  191.4 57.0 reduce-scatter.2
  275.0 37.7 reduce-scatter.4
  416.4 73.7 all-reduce.5

commit v6 on v5

--- a/solution.py
+++ b/solution.py
@@ -293,15 +293,25 @@
     )(table, ids)
 
 
-def stage_ids_kernel(batch, order, place_ref, ids_ref, out_ref, flags_ref, flat):
+def stage_ids_kernel(batch, order, sources, picks, ids_ref, out_ref, flags_ref, choices_ref, flat):
     lane = lax.broadcasted_iota(jnp.int32, (1, LANES), 1)
     count, _, chunk = ids_ref.shape[2:]
+    group = lax.axis_index("grp")
+
+    def of_group(values):
+        found = jnp.int32(values[0])
+        for at, value in enumerate(values[1:], 1):
+            found = jnp.where(group == at, value, found)
+        return found
+
     flat[...] = jnp.zeros_like(flat)
     for at, (slot, other) in enumerate(order):
-        core = lax.rem(place_ref[0] + other, ids_ref.shape[0])
+        choices_ref[at] = of_group(picks[at])
+        core = lax.rem(lax.axis_index("mdl") + other, ids_ref.shape[0])
+        source = of_group(sources[slot])
         for step in range(count):
             index = at * count + step
-            ids = ids_ref[core, place_ref[1 + slot], step]
+            ids = ids_ref[core, source, step]
             out_ref[index] = ids
             flat[2 * index : 2 * index + 2, :] = ids
     flags = jnp.zeros((flat.shape[0], LANES), jnp.int32)
@@ -316,21 +326,22 @@
         flags_ref[index] = flags[2 * index : 2 * index + 2]
 
 
-def stage_ids(place, ids, order, batch=4):
+def stage_ids(ids, order, sources, picks, batch=4):
     *_, count, _, chunk = ids.shape
     vm = pl.BlockSpec(memory_space=pltpu.VMEM)
     total = len(order) * count
     return pl.pallas_call(
-        functools.partial(stage_ids_kernel, batch, order),
-        in_specs=[pl.BlockSpec(memory_space=pltpu.SMEM), vm],
-        out_specs=[vm, vm],
+        functools.partial(stage_ids_kernel, batch, order, sources, picks),
+        in_specs=[vm],
+        out_specs=[vm, vm, pl.BlockSpec(memory_space=pltpu.SMEM)],
         out_shape=[
             jax.ShapeDtypeStruct((total, 2, chunk), jnp.int32),
             jax.ShapeDtypeStruct((total, 2, LANES), jnp.int32),
+            jax.ShapeDtypeStruct((len(order),), jnp.int32),
         ],
         scratch_shapes=[pltpu.VMEM((2 * total + -2 * total % 8, chunk), jnp.int32)],
         name="stage_ids",
-    )(place, ids)
+    )(ids)
 
 
 def spread_rows(features, rows_ref, summed):
@@ -472,7 +483,7 @@
             out_ref[cut, :] = piece.astype(bf)
 
 
-def scatter_rows(stage, vocab, dense=(), width=2048, batch=4):
+def scatter_rows(stage, vocab, dense=(), width=4096, batch=4):
     flush = pl.cdiv(vocab, width)
     block = pl.BlockSpec((stage.features, width), lambda s: (0, jnp.maximum(s - stage.steps, 0)))
     return pl.pallas_call(
@@ -1195,12 +1206,17 @@
     small = jnp.pad(small, ((0, -small.shape[0] % 8), (0, 0)))
 
     by_group = arrivals(grp_size)
-    sources = jnp.array([[group] + [found[0] for found in by_group[group]] for group in range(grp_size)], jnp.int32)
-    sources = lax.dynamic_index_in_dim(sources, group_index, 0, keepdims=False)
-    place = jnp.concatenate([mdl_index[None].astype(jnp.int32), sources])
+    sources = [list(range(grp_size))] + [[found[slot][0] for found in by_group] for slot in range(grp_size - 1)]
     order = [(slot, 0) for slot in range(grp_size)]
     order[-1:] = [(grp_size - 2, 1), (grp_size - 1, 0), (grp_size - 1, 1)]
-    staged_ids, staged_flags = stage_ids(place, after(all_ids, outgoing), order)
+
+    def candidates(slot):
+        found = [by_group[group][slot - 1][1:] for group in range(grp_size)]
+        kinds = sorted(set(found))
+        return kinds, [kinds.index(kind) for kind in found]
+
+    picks = [[0] * grp_size if slot == 0 else candidates(slot)[1] for slot, _ in order]
+    staged_ids, staged_flags, choices = stage_ids(after(all_ids, outgoing), order, sources, picks)
 
     outgoing = after(outgoing, part_ffn)
     own_rows = lax.all_to_all(outgoing, "dat", split_axis=0, concat_axis=0, tiled=True)
@@ -1226,15 +1242,6 @@
             moved = lax.ppermute(after(jnp.where(rising, moving[0][-1], moving[1][-1]), *waits), "grp", upward + downward)
             moving[0].append(moved)
             moving[1].append(moved)
-
-    def candidates(slot):
-        found = [by_group[group][slot - 1][1:] for group in range(grp_size)]
-        kinds = sorted(set(found))
-        return kinds, [kinds.index(kind) for kind in found]
-
-    picks = [[0] * grp_size if slot == 0 else candidates(slot)[1] for slot, _ in order]
-    choices = lax.dynamic_index_in_dim(jnp.array(picks, jnp.int32).T, group_index, 0, keepdims=False)
-    choices = after(choices, outgoing)
 
     def stage(first, count):
         segments = []

time: 572 us -> 565 us (0.988)
  Pallas kernels: 327 us -> 319 us
    pallas_call x3, Pallas kernels: 93.4 us -> 84.3 us  [scatter_rows(): pl.pallas_call(functools.partial(scatter_kernel, stage, batch, len(dense)...]
  transfers between devices with their start and end apart: 23 -> 23, of which waited for: 7 -> 8; matrix products, arithmetic and copies ran while one was open for 16% -> 16% of each run, Pallas kernels for 49% -> 48%
where the time goes in v6:
time: 565 us; the launch traced here: 554 us
  Pallas kernels  319 us (56%)
  matrix products  91.9 us (16%)
  waiting for transfers between devices  34.3 us (6%)
  starting transfers between devices  33 us (6%)
  other arithmetic  28 us (5%)
  blocking collectives  22.7 us (4%)
  between operations  16.4 us (3%)
  local copies, waits for them, and re-layouts  9.21 us (2%)
    pallas_call x1, Pallas kernels, finish(): pl.pallas_call(functools.partial(finish_kernel, stage, vocab, batch, len(...  90.1 us
    dot_general x24, matrix products, dot(): lax.dot_general(left, right, (dims, ((), ())), preferred_element_type=f32)  89.6 us
    pallas_call x3, Pallas kernels, scatter_rows(): pl.pallas_call(functools.partial(scatter_kernel, stage, batch, len(dense)...  84.3 us
    pallas_call x2, Pallas kernels, attend_back(): pl.pallas_call(functools.partial(attend_back_kernel, pairs, HEAD ** (-0.5...  27 us
    pallas_call x1, Pallas kernels, update_all(): pl.pallas_call(update_all_kernel, grid=(steps,), in_specs=in_specs, out_s...  26.3 us
    pallas_call x1, Pallas kernels, gather_rows(): pl.pallas_call(functools.partial(gather_kernel, features, load_steps, bat...  23.5 us
    all_to_all x1, blocking collectives, shards(): lax.all_to_all(looked_up.reshape(dat_size, pair_rows, 2 * features), 'dat...  22.7 us
    pallas_call x2, Pallas kernels, attend(): pl.pallas_call(functools.partial(attend_kernel, pairs, HEAD ** (-0.5)), i...  19.7 us
  transfers between devices with their start and end apart: 23, of which 8 were waited for; matrix products, arithmetic and copies ran while one was open for 16% of the time, Pallas kernels for 48%

profile of v6, /device:TPU:17, one launch (start us, length us, event | category | flops | bytes accessed | tf_op | source)
XLA Modules:
  0.0 554.2 jit_solution(8114419103876414342)
XLA Ops:
  10.4 4.9 share.1
  16.8 23.5 %gather_rows.1 = bf16[2048,384]{1,0:T(8,128)(2,1)} custom-call(f32[192,32128]{1,0:T(8,128)} %refs_0_.1, s32[4,2,512]{2,1,0:T(2,128)} %dynamic-slice_bitcast_fusion.ids_ref), custom_call_target="tpu_custom_call" | custom-call | bytes 83886080 | tf_op jit(solution)/shard_map/gather_rows/pallas_call | solution.py:280
  42.1 22.7 %all_to_all.10.spread_ref = bf16[4,512,384]{2,1,0:T(8,128)(2,1)S(1)} all-to-all(bf16[4,512,384]{2,1,0:T(8,128)(2,1)S(1)} %bitcast.141), channel_id=1, replica_groups=mesh['grp'=4,'dat'=4,'mdl'=2] {'dat'}, dimensions={0} | all-to-all | bytes 3145728 | tf_op jit(solution)/shard_map/all_to_all | solution.py:1098
  64.8 5.8 %collective-permute-start.1 = (bf16[768,1536]{1,0:T(8,128)(2,1)}, bf16[768,1536]{1,0:T(8,128)(2,1)}, u32[]{:S(2)}, u32[]{:S(2)}) collective-permute-start(bf16[768,1536]{1,0:T(8,128)(2,1)} %all-gather.3.cloned.1.call-done), channel_id=1, source_target_pairs={{0,1},{1,0},{2,3},{3,2},{4,5},{5,4},{6,7},{7,6},{8,9},{9,8},{10,11... | collective-permute-start | bytes 7077896 | tf_op jit(solution)/shard_map/ppermute | solution.py:1020
  76.9 4.3 convolution_convert_fusion.1
  81.2 9.7 %attend.2 = (bf16[2,512,384]{2,1,0:T(8,128)(2,1)S(1)}, f32[6,1024]{1,0:T(8,128)S(1)}) custom-call(s32[2]{0:T(128)S(1)} %dynamic_slice.14.lens_ref, f32[6,1024]{1,0:T(8,128)S(1)} %convolution_bitcast_fusion.3.line_ref, bf16[2,512,1152]{2,1,0:T(8,128)(2,1)S(1)} %bitcast.131), custom_call_target="tpu_custom_call" | custom-call | flops 1610612736 | bytes 4718592 | tf_op jit(solution)/shard_map/attend/pallas_call | solution.py:106
  94.7 9.9 %attend.3 = (bf16[2,512,384]{2,1,0:T(8,128)(2,1)S(1)}, f32[6,1024]{1,0:T(8,128)S(1)}) custom-call(s32[2]{0:T(128)S(1)} %dynamic_slice.14.lens_ref, f32[6,1024]{1,0:T(8,128)S(1)} %convolution_bitcast_fusion.2.line_ref, bf16[2,512,1152]{2,1,0:T(8,128)(2,1)S(1)} %bitcast.133), custom_call_target="tpu_custom_call" | custom-call | flops 1610612736 | bytes 4718592 | tf_op jit(solution)/shard_map/attend/pallas_call | solution.py:106
  106.2 5.4 all-gather.5.cloned.1.call-done
  123.0 3.8 fusion.34
  126.8 4.3 fusion.30
  131.1 9.0 %multiply_reduce_fusion.3 = (f32[1024]{0:T(1024)S(1)}, f32[1024,768]{1,0:T(8,128)}) fusion(f32[1024,768]{1,0:T(8,128)S(1)} %get-tuple-element.235, f32[1024,768]{1,0:T(8,128)S(1)} %fusion.34, bf16[768,3072]{1,0:T(8,128)(2,1)} %collective-permute-done.2, f32[1024,1536]{1,0:T(8,128)S(1)} %fusion.30), kind=kOutput, calls=%fused_computation.45 | convolution fusion | flops 2433219584 | bytes 18092032 | tf_op jit(solution)/shard_map/dot_general | solution.py:992
  143.9 7.5 %share_both.1 = (f32[8,8,768]{2,1,0:T(8,128)}, s32[4,16,512]{2,1,0:T(8,128)}) custom-call(f32[8,768]{1,0:T(8,128)} %maximum_maximum_fusion.vectors_ref, s32[16,512]{1,0:T(8,128)} %reshape.291.ids_ref), custom_call_target="tpu_custom_call" | custom-call | tf_op jit(solution)/shard_map/share_both/pallas_call | solution.py:821
  165.3 7.1 %fusion.13 = bf16[1024,1536]{1,0:T(8,128)(2,1)S(1)} fusion(f32[1024,1536]{1,0:T(8,128)S(1)} %copy-done.32, bf16[1024,768]{1,0:T(8,128)(2,1)S(1)} %fusion.42, bf16[768,3072]{1,0:T(8,128)(2,1)} %collective-permute-done.2), kind=kOutput, calls=%fused_computation.17 | convolution fusion | flops 2447376384 | bytes 13369344 | tf_op jit(solution)/shard_map/dot_general | solution.py:992
  175.6 6.3 %fusion.6 = bf16[1024,1536]{1,0:T(8,128)(2,1)S(1)} fusion(f32[1024,1536]{1,0:T(8,128)S(1)} %bitcast.172, bf16[1024,768]{1,0:T(8,128)(2,1)S(1)} %fusion.42, bf16[768,3072]{1,0:T(8,128)(2,1)S(1)} %bitcast.161), kind=kOutput, calls=%fused_computation.10 | convolution fusion | flops 2447376384 | bytes 13369344 | tf_op jit(solution)/shard_map/dot_general | solution.py:992
  191.2 5.4 fusion.38
  196.7 4.8 multiply_reduce_fusion
  209.3 13.6 %attend_back.3 = (bf16[2,512,1152]{2,1,0:T(8,128)(2,1)S(1)}, f32[6,1024]{1,0:T(8,128)S(1)}) custom-call(s32[2]{0:T(128)S(1)} %dynamic_slice.14.lens_ref, f32[6,1024]{1,0:T(8,128)S(1)} %convolution_bitcast_fusion.2.line_ref, bf16[2,512,1152]{2,1,0:T(8,128)(2,1)S(1)} %bitcast.134, f32[6,1024]{1,0:T(8,128)S(1)} %get-tuple-element.109.lse_ref, ...), custom_call_target="tpu_custom_call" | custom-call | flops 4026531840 | bytes 7864320 | tf_op jit(solution)/shard_map/attend_back/pallas_call | solution.py:181
  228.0 13.4 %attend_back.2 = (bf16[2,512,1152]{2,1,0:T(8,128)(2,1)S(1)}, f32[6,1024]{1,0:T(8,128)S(1)}) custom-call(s32[2]{0:T(128)S(1)} %dynamic_slice.14.lens_ref, f32[6,1024]{1,0:T(8,128)S(1)} %convolution_bitcast_fusion.3.line_ref, bf16[2,512,1152]{2,1,0:T(8,128)(2,1)S(1)} %bitcast.132, f32[6,1024]{1,0:T(8,128)S(1)} %get-tuple-element.107.lse_ref, ...), custom_call_target="tpu_custom_call" | custom-call | flops 4026531840 | bytes 7864320 | tf_op jit(solution)/shard_map/attend_back/pallas_call | solution.py:181
  243.7 3.7 convolution_add_fusion
  250.9 4.4 all-to-all-start.1
  258.5 3.7 add_convert_fusion.2
  263.8 11.0 %all-to-all-done.1 = bf16[4,512,384]{2,1,0:T(8,128)(2,1)} async-done(((bf16[4,512,384]{2,1,0:T(8,128)(2,1)}), bf16[4,512,384]{2,1,0:T(8,128)(2,1)}, u32[]{:S(2)}, u32[]{:S(2)}) %all-to-all-start.1) | async-done | bytes 1572896 | tf_op jit(solution)/shard_map/all_to_all | solution.py:1222
  277.5 3.9 collective-permute-start.5
  286.4 22.6 %scatter_rows.3.refs_6_ = bf16[192,32128]{1,0:T(8,128)(2,1)} custom-call(s32[6]{0:T(128)} %get-tuple-element.124.refs_0_, s32[24,2,512]{2,1,0:T(2,128)} %get-tuple-element.114.refs_1_.refs_2_, s32[24,2,512]{2,1,0:T(2,128)} %get-tuple-element.114.refs_1_.refs_2_, s32[24,2,128]{2,1,0:T(2,128)} %get-tuple-element.115.refs_3_, bf16[2048,384]{1,0:T(8,128)(2,1)} %bitcast.24.refs_4_), custom_call_target="tpu_custom_call" | custom-call | bytes 104857600 | tf_op jit(solution)/shard_map/scatter_rows/pallas_call | solution.py:489
  308.9 11.1 %sum_all.1.small_ref = f32[32,128]{1,0:T(8,128)} custom-call(f32[32,128]{1,0:T(8,128)} %pad.14.value_ref), custom_call_target="tpu_custom_call" | custom-call | tf_op jit(solution)/shard_map/sum_all/pallas_call | solution.py:789
  327.1 27.7 %scatter_rows.4.refs_15_ = bf16[192,32128]{1,0:T(8,128)(2,1)} custom-call(s32[6]{0:T(128)} %get-tuple-element.124.refs_0_, s32[24,2,512]{2,1,0:T(2,128)} %get-tuple-element.114.refs_1_.refs_2_, s32[24,2,512]{2,1,0:T(2,128)} %get-tuple-element.114.refs_1_.refs_2_, s32[24,2,128]{2,1,0:T(2,128)} %get-tuple-element.115.refs_3_, ...), custom_call_target="tpu_custom_call" | custom-call | bytes 104857600 | tf_op jit(solution)/shard_map/scatter_rows/pallas_call | solution.py:489
  355.3 5.0 collective-permute-done.6.refs_4_
  374.7 34.0 %scatter_rows.5.refs_17_ = bf16[192,32128]{1,0:T(8,128)(2,1)} custom-call(s32[6]{0:T(128)} %get-tuple-element.124.refs_0_, s32[24,2,512]{2,1,0:T(2,128)} %get-tuple-element.114.refs_1_.refs_2_, s32[24,2,512]{2,1,0:T(2,128)} %get-tuple-element.114.refs_1_.refs_2_, s32[24,2,128]{2,1,0:T(2,128)} %get-tuple-element.115.refs_3_, ...), custom_call_target="tpu_custom_call" | custom-call | bytes 104857600 | tf_op jit(solution)/shard_map/scatter_rows/pallas_call | solution.py:489
  412.6 90.1 %finish.1 = (f32[192,32128]{1,0:T(8,128)}, f32[192,32128]{1,0:T(8,128)}, bf16[192,32128]{1,0:T(8,128)(2,1)}, f32[8,1024]{1,0:T(8,128)}) custom-call(s32[6]{0:T(128)} %get-tuple-element.124.refs_0_, s32[24,2,512]{2,1,0:T(2,128)} %get-tuple-element.114.refs_1_.refs_2_, s32[24,2,512]{2,1,0:T(2,128)} %get-tuple-element.114.refs_1_.refs_2_, ...), custom_call_target="tpu_custom_call" | custom-call | bytes 314572800 | tf_op jit(solution)/shard_map/finish/pallas_call | solution.py:615
  502.8 11.0 %small_moments.1 = (f32[3,192,384]{2,1,0:T(8,128)}, f32[3,192,384]{2,1,0:T(8,128)}, f32[3,192,384]{2,1,0:T(8,128)}, f32[192,384]{1,0:T(8,128)}, f32[192,384]{1,0...) custom-call(f32[1]{0:T(128)} %bitcast.live_ref, ...), custom_call_target="tpu_custom_call" | custom-call | tf_op jit(solution)/shard_map/small_moments/pallas_call | solution.py:936
  513.7 6.1 %sum_over.1.squares_ref = f32[16,128]{1,0:T(8,128)} custom-call(f32[8,1024]{1,0:T(8,128)} %get-tuple-element.131.rows_ref, f32[16,128]{1,0:T(8,128)} %get-tuple-element.135.table_ref), custom_call_target="tpu_custom_call" | custom-call | tf_op jit(solution)/shard_map/sum_over/pallas_call | solution.py:731
  519.9 26.3 %update_all.1 = (f32[192,32128]{1,0:T(8,128)}, f32[3,192,384]{2,1,0:T(8,128)}, f32[192,384]{1,0:T(8,128)}, f32[192,1536]{1,0:T(8,128)}, f32[192,1536]{1,0:T(8,12...) custom-call(f32[16,128]{1,0:T(8,128)} %sum_over.1.squares_ref, f32[192,32128]{1,0:T(8,128)} %refs_0_.1, ...), custom_call_target="tpu_custom_call" | custom-call | tf_op jit(solution)/shard_map/update_all/pallas_call | solution.py:970
  (215 shorter events, 115.9 us)
Async XLA Ops:
  7.2 57.6 %all-gather.3.cloned.1.call-start = ((), (), s32[]{:S(2)}) async-start(), calls=%async_computation.4 | async-start | bytes 2949120 | tf_op jit(solution)/shard_map/all_gather | solution.py:1078
  10.4 101.2 %all-gather.5.cloned.1.call-start = ((), (), s32[]{:S(2)}) async-start(), calls=%async_computation.5 | async-start | bytes 5898240 | tf_op jit(solution)/shard_map/all_gather | solution.py:1078
  16.8 23.6 %copy-start.12 = (f32[192,1536]{1,0:T(8,128)S(1)}, f32[192,1536]{1,0:T(8,128)}, u32[]{:S(2)}) copy-start(f32[192,1536]{1,0:T(8,128)} %refs_6_.3) | copy-start | bytes 3538948
  16.8 23.6 %copy-start.11 = (f32[192,1536]{1,0:T(8,128)S(1)}, f32[192,1536]{1,0:T(8,128)}, u32[]{:S(2)}) copy-start(f32[192,1536]{1,0:T(8,128)} %refs_8_.3) | copy-start | bytes 3538948
  40.5 30.1 %copy-start.21 = (f32[32,6]{0,1:T(8,128)S(1)}, f32[32,6]{0,1:T(8,128)}, u32[]{:S(2)}) copy-start(f32[32,6]{0,1:T(8,128)} %param.36) | copy-start | bytes 2308
  40.5 30.6 %copy-start.20 = (f32[3,768]{1,0:T(4,128)S(1)}, f32[3,768]{1,0:T(4,128)}, u32[]{:S(2)}) copy-start(f32[3,768]{1,0:T(4,128)} %refs_12_.3) | copy-start | bytes 27652
  40.5 30.6 %copy-start.25 = (s32[4]{0:T(128)S(1)}, s32[4]{0:T(128)}, u32[]{:S(2)}) copy-start(s32[4]{0:T(128)} %param.27) | copy-start | bytes 52
  41.7 209.2 %reduce-scatter.3.cloned.1.call-start = ((), (), s32[]{:S(2)}) async-start(), calls=%async_computation.6 | async-start | bytes 5898240 | tf_op jit(solution)/shard_map/reduce_scatter | solution.py:1164
  64.8 26.2 %collective-permute-start.1 = (bf16[768,1536]{1,0:T(8,128)(2,1)}, bf16[768,1536]{1,0:T(8,128)(2,1)}, u32[]{:S(2)}, u32[]{:S(2)}) collective-permute-start(bf16[768,1536]{1,0:T(8,128)(2,1)} %all-gather.3.cloned.1.call-done), channel_id=1, source_target_pairs={{0,1},{1,0},{2,3},{3,2},{4,5},{5,4},{6,7},{7,6},{8,9},{9,8},{10,11... | collective-permute-start | bytes 7077896 | tf_op jit(solution)/shard_map/ppermute | solution.py:1020
  70.6 4.0 collective-permute-start
  94.7 19.4 %copy-start.26 = (s32[4]{0:T(128)S(1)}, s32[4]{0:T(128)}, u32[]{:S(2)}) copy-start(s32[4]{0:T(128)} %param.28) | copy-start | bytes 52
  94.7 19.5 %copy-start.27 = (s32[4]{0:T(128)S(1)}, s32[4]{0:T(128)}, u32[]{:S(2)}) copy-start(s32[4]{0:T(128)} %param.30) | copy-start | bytes 52
  111.5 15.2 %collective-permute-start.2 = (bf16[768,3072]{1,0:T(8,128)(2,1)}, bf16[768,3072]{1,0:T(8,128)(2,1)}, u32[]{:S(2)}, u32[]{:S(2)}) collective-permute-start(bf16[768,3072]{1,0:T(8,128)(2,1)} %all-gather.5.cloned.1.call-done), channel_id=1, source_target_pairs={{0,1},{1,0},{2,3},{3,2},{4,5},{5,4},{6,7},{7,6},{8,9},{9,8},{10,11... | collective-permute-start | bytes 14155784 | tf_op jit(solution)/shard_map/ppermute | solution.py:1020
  164.3 17.6 %collective-permute-start.3 = (bf16[768,1536]{1,0:T(8,128)(2,1)S(1)}, bf16[768,1536]{1,0:T(8,128)(2,1)S(1)}, u32[]{:S(2)}, u32[]{:S(2)}) collective-permute-start(bf16[768,1536]{1,0:T(8,128)(2,1)S(1)} %convolution_convert_fusion.3), channel_id=1, source_target_pairs={{0,1},{1,0},{2,3},{3,2},{4,5},{5,4},{6,7},{7,6},{8,9},{9,8},{10,11... | collective-permute-start | bytes 7077896 | tf_op jit(solution)/shard_map/ppermute | solution.py:1020
  175.4 9.8 %collective-permute-start.4 = (bf16[768,1536]{1,0:T(8,128)(2,1)S(1)}, bf16[768,1536]{1,0:T(8,128)(2,1)S(1)}, u32[]{:S(2)}, u32[]{:S(2)}) collective-permute-start(bf16[768,1536]{1,0:T(8,128)(2,1)S(1)} %convolution_convert_fusion.2), channel_id=1, source_target_pairs={{0,1},{1,0},{2,3},{3,2},{4,5},{5,4},{6,7},{7,6},{8,9},{9,8},{10,11... | collective-permute-start | bytes 7077896 | tf_op jit(solution)/shard_map/ppermute | solution.py:1020
  204.5 21.8 %copy-start.16 = (bf16[1024,768]{1,0:T(8,128)(2,1)}, bf16[1024,768]{1,0:T(8,128)(2,1)S(1)}, u32[]{:S(2)}) copy-start(bf16[1024,768]{1,0:T(8,128)(2,1)S(1)} %get-tuple-element.223) | copy-start | bytes 4718596
  206.3 49.4 %collective-permute-start.10 = (bf16[768,384]{1,0:T(8,128)(2,1)}, bf16[768,384]{1,0:T(8,128)(2,1)}, u32[]{:S(2)}, u32[]{:S(2)}) collective-permute-start(bf16[768,384]{1,0:T(8,128)(2,1)} %convolution_convert_fusion.6), channel_id=1, source_target_pairs={{0,1},{1,0},{2,3},{3,2},{4,5},{5,4},{6,7},{7,6},{8,9},{9,8},{10,11... | collective-permute-start | bytes 1769480 | tf_op jit(solution)/shard_map/ppermute | solution.py:1020
  226.3 32.1 %collective-permute-start.9 = (bf16[768,1152]{1,0:T(8,128)(2,1)}, bf16[768,1152]{1,0:T(8,128)(2,1)}, u32[]{:S(2)}, u32[]{:S(2)}) collective-permute-start(bf16[768,1152]{1,0:T(8,128)(2,1)} %fusion.14), channel_id=1, source_target_pairs={{0,1},{1,0},{2,3},{3,2},{4,5},{5,4},{6,7},{7,6},{8,9},{9,8},{10,11... | collective-permute-start | bytes 5308424 | tf_op jit(solution)/shard_map/ppermute | solution.py:1020
  250.9 23.9 %all-to-all-start.1 = ((bf16[4,512,384]{2,1,0:T(8,128)(2,1)}), bf16[4,512,384]{2,1,0:T(8,128)(2,1)}, u32[]{:S(2)}, u32[]{:S(2)}) async-start(bf16[4,512,384]{2,1,0:T(8,128)(2,1)} %get-tuple-element.116), calls=%async_computation.2 | async-start | bytes 3145728 | tf_op jit(solution)/shard_map/all_to_all | solution.py:1222
  255.3 71.8 %reduce-scatter.5.cloned.1.call-start = ((), (), s32[]{:S(2)}) async-start(), calls=%async_computation.7 | async-start | bytes 2949120 | tf_op jit(solution)/shard_map/reduce_scatter | solution.py:1164
  262.2 22.6 %copy-start.23 = (s32[1024]{0:T(1024)S(1)}, s32[1024]{0:T(1024)}, u32[]{:S(2)}) copy-start(s32[1024]{0:T(1024)} %copy-done.22) | copy-start | bytes 12292
  274.8 227.9 %all-reduce.6.cloned.1.call-start = ((), (), s32[]{:S(2)}) async-start(), calls=%async_computation.8 | async-start | bytes 3538944 | tf_op jit(solution)/shard_map/psum | solution.py:1268
  274.9 45.1 %collective-permute-start.7 = (bf16[2048,384]{1,0:T(8,128)(2,1)}, bf16[2048,384]{1,0:T(8,128)(2,1)}, u32[]{:S(2)}, u32[]{:S(2)}) collective-permute-start(bf16[2048,384]{1,0:T(8,128)(2,1)} %bitcast.24.refs_4_), channel_id=1, source_target_pairs={{24,16},{16,8},{8,0},{25,17},{17,9},{9,1},{26,18},{18,10},{10,2},{... | collective-permute-start | bytes 4718600 | tf_op jit(solution)/shard_map/ppermute | solution.py:1239
  277.5 46.2 %collective-permute-start.5 = (bf16[2048,384]{1,0:T(8,128)(2,1)}, bf16[2048,384]{1,0:T(8,128)(2,1)}, u32[]{:S(2)}, u32[]{:S(2)}) collective-permute-start(bf16[2048,384]{1,0:T(8,128)(2,1)} %bitcast.24.refs_4_), channel_id=1, source_target_pairs={{0,8},{8,16},{16,24},{1,9},{9,17},{17,25},{2,10},{10,18},{18,26},{... | collective-permute-start | bytes 4718600 | tf_op jit(solution)/shard_map/ppermute | solution.py:1239
  320.0 35.3 %collective-permute-start.8 = (bf16[2048,384]{1,0:T(8,128)(2,1)}, bf16[2048,384]{1,0:T(8,128)(2,1)}, u32[]{:S(2)}, u32[]{:S(2)}) collective-permute-start(bf16[2048,384]{1,0:T(8,128)(2,1)} %collective-permute-done.7.refs_5_), channel_id=1, source_target_pairs={{16,8},{8,0},{17,9},{9,1},{18,10},{10,2},{19,11},{11,3},{20,12},{1... | collective-permute-start | bytes 4718600 | tf_op jit(solution)/shard_map/ppermute | solution.py:1239
  323.6 36.6 %collective-permute-start.6 = (bf16[2048,384]{1,0:T(8,128)(2,1)}, bf16[2048,384]{1,0:T(8,128)(2,1)}, u32[]{:S(2)}, u32[]{:S(2)}) collective-permute-start(bf16[2048,384]{1,0:T(8,128)(2,1)} %collective-permute-done.5.refs_4_), channel_id=1, source_target_pairs={{8,16},{16,24},{9,17},{17,25},{10,18},{18,26},{11,19},{19,27},{12,... | collective-permute-start | bytes 4718600 | tf_op jit(solution)/shard_map/ppermute | solution.py:1239
  325.6 37.1 %collective-permute-start.12 = (bf16[2048,384]{1,0:T(8,128)(2,1)}, bf16[2048,384]{1,0:T(8,128)(2,1)}, u32[]{:S(2)}, u32[]{:S(2)}) collective-permute-start(bf16[2048,384]{1,0:T(8,128)(2,1)} %collective-permute-done.7.refs_5_), channel_id=1, source_target_pairs={{0,1},{1,0},{2,3},{3,2},{4,5},{5,4},{6,7},{7,6},{8,9},{9,8},{10,11... | collective-permute-start | bytes 4718600 | tf_op jit(solution)/shard_map/ppermute | solution.py:1020
  360.3 5.7 %collective-permute-start.11 = (bf16[2048,384]{1,0:T(8,128)(2,1)}, bf16[2048,384]{1,0:T(8,128)(2,1)}, u32[]{:S(2)}, u32[]{:S(2)}) collective-permute-start(bf16[2048,384]{1,0:T(8,128)(2,1)} %collective-permute-done.6.refs_4_), channel_id=1, source_target_pairs={{0,1},{1,0},{2,3},{3,2},{4,5},{5,4},{6,7},{7,6},{8,9},{9,8},{10,11... | collective-permute-start | bytes 4718600 | tf_op jit(solution)/shard_map/ppermute | solution.py:1020
  362.6 5.6 %collective-permute-start.13 = (bf16[2048,384]{1,0:T(8,128)(2,1)}, bf16[2048,384]{1,0:T(8,128)(2,1)}, u32[]{:S(2)}, u32[]{:S(2)}) collective-permute-start(bf16[2048,384]{1,0:T(8,128)(2,1)} %collective-permute-done.8.refs_6_), channel_id=1, source_target_pairs={{0,1},{1,0},{2,3},{3,2},{4,5},{5,4},{6,7},{7,6},{8,9},{9,8},{10,11... | collective-permute-start | bytes 4718600 | tf_op jit(solution)/shard_map/ppermute | solution.py:1020
  368.3 44.3 %collective-permute-start.16 = (bf16[192,32128]{1,0:T(8,128)(2,1)}, bf16[192,32128]{1,0:T(8,128)(2,1)}, u32[]{:S(2)}, u32[]{:S(2)}) collective-permute-start(bf16[192,32128]{1,0:T(8,128)(2,1)} %scatter_rows.4.refs_15_), channel_id=1, source_target_pairs={{0,1},{1,0},{2,3},{3,2},{4,5},{5,4},{6,7},{7,6},{8,9},{9,8},{10,11... | collective-permute-start | bytes 37011464 | tf_op jit(solution)/shard_map/ppermute | solution.py:1020
  371.4 37.3 %collective-permute-start.14 = (bf16[2048,384]{1,0:T(8,128)(2,1)}, bf16[2048,384]{1,0:T(8,128)(2,1)}, u32[]{:S(2)}, u32[]{:S(2)}) collective-permute-start(bf16[2048,384]{1,0:T(8,128)(2,1)} %broadcast_select_fusion), channel_id=1, source_target_pairs={{16,24},{8,0},{17,25},{9,1},{18,26},{10,2},{19,27},{11,3},{20,28},... | collective-permute-start | bytes 4718600 | tf_op jit(solution)/shard_map/ppermute | solution.py:1242
  408.7 3.9 collective-permute-start.15
  (31 other events, 244.6 us)
Sparse Core Ops, SparseCore 0:
  10.5 38.8 all-gather.2
  51.8 59.6 all-gather.4
  191.3 57.0 reduce-scatter.2
  274.9 37.7 reduce-scatter.4
  408.8 73.5 all-reduce.5
